TPU v7x, 128 devices: a whole 4x4x4 slice. The times are simulated.
128 devices in a mesh: ctx: 64 (over y_lo, x, z, core), dp: 2 (over y_hi).
Axes of the slice: x: 4, y: 4 (y_hi: 2, y_lo: 2; y = y_hi * 2 + y_lo), z: 4, core: 2. Of those that a mesh axis runs over, the one named last changes fastest.
Arguments:
- query_proj: bfloat16 [2, 8192, 1024], P('dp', 'ctx'), may hold values from -6 to 6
- key_proj: bfloat16 [2, 8192, 1024], P('dp', 'ctx'), may hold values from -6 to 6
- value_proj: bfloat16 [2, 8192, 1024], P('dp', 'ctx'), may hold values from -6 to 6
- grad_out: bfloat16 [2, 8192, 4096], P('dp', 'ctx'), may hold values from -6 to 6
- out_weight: bfloat16 [1024, 4096], P('ctx'), may hold values from -0.1875 to 0.1875
- short_taps: float32 [3, 1024, 7], replicated, may hold values from -2 to 2
- residues: float32 [1024, 16], replicated, may hold values from -1.5 to 1.5
- decay_rate: float32 [1024, 16], replicated, may hold values from 3.0517578e-05 to 0.05
Outputs:
- grad_query: bfloat16 [2, 8192, 1024], P('dp', 'ctx')
- grad_key: bfloat16 [2, 8192, 1024], P('dp', 'ctx')
- grad_value: bfloat16 [2, 8192, 1024], P('dp', 'ctx')
- weight_grad: float32 [1024, 4096], P('ctx')
- taps_grad: float32 [3, 1024, 7], replicated
- residue_grad: float32 [1024, 16], replicated
All inputs are finite; a program needn't handle non-finite values.
Results may differ from a plain program's by a relative error of at most 0.0075.
Values may be sent and summed in bfloat16 or wider, within the bound.
No kernel may reach another device: no remote copies, remote signals or barrier semaphores. Data moves between devices by JAX's collectives and lax.ppermute only.
A program may use at most 192 MiB of HBM per device.

v0:
```python
import math

import jax
import jax.numpy as jnp
from jax import lax
from jax.sharding import PartitionSpec as P

HIGH = lax.Precision.HIGHEST


def passed_along(value, axis, steps):
    count = lax.axis_size(axis)
    first, last = (max(0, -steps), min(count, count - steps))
    return lax.ppermute(value, axis, [(source, source + steps) for source in range(first, last)])


def local_modes(mixed, grad_filtered, rate, coef):
    tokens, width = mixed.shape
    sub = math.gcd(tokens, 64)
    blocks = tokens // sub
    offsets = jnp.arange(sub, dtype=jnp.float32)
    rows_index = jnp.arange(sub)
    lower_mask = rows_index[:, None] >= rows_index[None, :]
    upper_mask = rows_index[:, None] <= rows_index[None, :]
    lag_index = jnp.maximum(rows_index[:, None] - rows_index[None, :], 0)
    decay_lag = jnp.exp(-rate[:, None, :] * offsets[None, :, None])
    kernel = jnp.einsum("mc,mdc->dc", coef, decay_lag, precision=HIGH)
    toeplitz = jnp.where(lower_mask[:, :, None], kernel[lag_index], 0.0)
    mixed_blocks = mixed.reshape(blocks, sub, width)
    grad_blocks = grad_filtered.reshape(blocks, sub, width)
    filt_inner = jnp.einsum("bjc,njc->nbc", toeplitz, mixed_blocks, precision=HIGH)
    adj_inner = jnp.einsum("jbc,njc->nbc", toeplitz, grad_blocks, precision=HIGH)
    to_end = jnp.exp(-rate[:, None, :] * (sub - 1.0 - offsets)[None, :, None])
    ends_block = jnp.einsum("njc,mjc->nmc", mixed_blocks, to_end, precision=HIGH)
    firsts_block = jnp.einsum("njc,mjc->nmc", grad_blocks, decay_lag, precision=HIGH)
    places = jnp.arange(blocks, dtype=jnp.float32)
    diff = places[:, None] - places[None, :]
    carry_mat = jnp.where(
        (diff >= 0)[:, :, None, None],
        jnp.exp(-(rate * sub)[None, None] * jnp.maximum(diff, 0.0)[:, :, None, None]),
        0.0,
    )
    after = jnp.einsum("ikmc,kmc->imc", carry_mat, ends_block, precision=HIGH)
    before = jnp.einsum("kimc,kmc->imc", carry_mat, firsts_block, precision=HIGH)
    correlation = jnp.einsum("nbc,njc->bjc", mixed_blocks, grad_blocks, precision=HIGH)
    correlation = jnp.where(upper_mask[:, :, None], correlation, 0.0)
    growth = jnp.exp(rate[:, None, :] * offsets[None, :, None])
    partial_y = jnp.einsum("bjc,mbc->mjc", correlation, growth, precision=HIGH)
    within = jnp.sum(partial_y * decay_lag, axis=1)
    return (filt_inner, adj_inner, ends_block, after, before, within)


def shards(
    query_proj, key_proj, value_proj, grad_out, out_weight, short_taps, residues, decay_rate
):
    stacked = jnp.stack([query_proj[0], key_proj[0], value_proj[0]])
    tokens = stacked.shape[1]
    width = stacked.shape[2]
    behind = passed_along(stacked[:, tokens - 6 :, :], "ctx", 1)
    widened = jnp.concatenate([behind, stacked], axis=1).astype(jnp.float32)
    shaped = jnp.zeros((3, tokens, width), jnp.float32)
    for lag in range(7):
        shaped = shaped + short_taps[:, None, :, lag] * widened[:, 6 - lag : 6 - lag + tokens, :]
    shaped_q, shaped_k, shaped_v = (shaped[0], shaped[1], shaped[2])
    mixed = shaped_k * shaped_v
    out_rows = grad_out[0]
    upstream = lax.dot_general(
        out_rows,
        lax.all_gather(out_weight, "ctx", axis=0, tiled=True),
        (((1,), (1,)), ((), ())),
        preferred_element_type=jnp.float32,
    )
    grad_filtered = upstream * shaped_q
    rate_t = decay_rate.T
    norm_t = jnp.sqrt(-jnp.expm1(-2.0 * rate_t))
    coef_t = residues.T * norm_t
    filt_inner, adj_inner, ends_block, after, before, within = local_modes(
        mixed, grad_filtered, rate_t, coef_t
    )
    blocks = ends_block.shape[0]
    sub = tokens // blocks
    ends = after[blocks - 1]
    firsts = before[0]
    span = jnp.exp(-rate_t * tokens)

    def advance(step, pair):
        fore, aft = pair
        fore = passed_along(span * fore + ends, "ctx", 1)
        aft = passed_along(span * aft + firsts, "ctx", -1)
        return (fore, aft)

    blank = jnp.zeros_like(ends)
    incoming, outgoing = lax.fori_loop(0, lax.axis_size("ctx") - 1, advance, (blank, blank))
    blank_row = jnp.zeros_like(ends)[None]
    places = jnp.arange(blocks, dtype=jnp.float32)[:, None, None]
    span_sub = (rate_t * sub)[None]
    starts = (
        jnp.concatenate([blank_row, after[: blocks - 1]], axis=0)
        + jnp.exp(-span_sub * places) * incoming[None]
    )
    back_starts = (
        jnp.concatenate([before[1:], blank_row], axis=0)
        + jnp.exp(-span_sub * (blocks - 1.0 - places)) * outgoing[None]
    )
    offsets = jnp.arange(sub, dtype=jnp.float32)[None, :, None]
    apply_fore = coef_t[:, None, :] * jnp.exp(-rate_t[:, None, :] * (offsets + 1.0))
    apply_back = coef_t[:, None, :] * jnp.exp(-rate_t[:, None, :] * (sub - offsets))
    filtered = (
        filt_inner + jnp.einsum("nmc,mbc->nbc", starts, apply_fore, precision=HIGH)
    ).reshape(tokens, width)
    grad_mixed = (
        adj_inner + jnp.einsum("nmc,mbc->nbc", back_starts, apply_back, precision=HIGH)
    ).reshape(tokens, width)
    residue_part = norm_t * (within + jnp.exp(-rate_t) * jnp.sum(back_starts * ends_block, axis=0))
    gated = (shaped_q * filtered).astype(jnp.bfloat16)
    grad_shaped = jnp.stack([upstream * filtered, grad_mixed * shaped_v, grad_mixed * shaped_k])
    ahead = passed_along(grad_shaped[:, :6, :].astype(jnp.bfloat16), "ctx", -1).astype(jnp.float32)
    longer = jnp.concatenate([grad_shaped, ahead], axis=1)
    streams = jnp.zeros((3, tokens, width), jnp.float32)
    for lag in range(7):
        streams = streams + short_taps[:, None, :, lag] * longer[:, lag : lag + tokens, :]
    streams = streams.astype(jnp.bfloat16)
    taps_part = jnp.stack(
        [
            jnp.sum(grad_shaped * widened[:, 6 - lag : 6 - lag + tokens, :], axis=1)
            for lag in range(7)
        ],
        axis=1,
    )
    taps_total, residue_total = lax.psum((taps_part, residue_part), ("ctx", "dp"))
    taps_grad = jnp.swapaxes(taps_total, 1, 2)
    residue_grad = residue_total.T
    summed = lax.psum_scatter(
        lax.dot_general(
            gated, out_rows, (((0,), (0,)), ((), ())), preferred_element_type=jnp.float32
        ),
        "ctx",
        scatter_dimension=0,
        tiled=True,
    )
    weight_grad = lax.psum(summed.astype(jnp.bfloat16), "dp").astype(jnp.float32)
    return (
        streams[0][None],
        streams[1][None],
        streams[2][None],
        weight_grad,
        taps_grad,
        residue_grad,
    )


def solution(mesh):
    placed = (
        P("dp", "ctx", None),
        P("dp", "ctx", None),
        P("dp", "ctx", None),
        P("dp", "ctx", None),
        P("ctx", None),
        P(),
        P(),
        P(),
    )
    return jax.shard_map(
        shards,
        mesh=mesh,
        in_specs=placed,
        out_specs=(
            P("dp", "ctx", None),
            P("dp", "ctx", None),
            P("dp", "ctx", None),
            P("ctx", None),
            P(),
            P(),
        ),
        check_vma=False,
    )
```

profile of v0, /device:TPU:0, one launch (start us, length us, event | category | flops | bytes accessed | tf_op | source)
XLA Modules:
  0.0 1762.4 jit_solution(8179337737185172629)
XLA Ops:
  23.2 16.1 fusion.19
  47.4 76.3 %all-gather.2.cloned.1.call-done = bf16[1024,4096]{1,0:T(8,128)(2,1)} async-done(((bf16[16,4096]{1,0:T(8,128)(2,1)}), bf16[1024,4096]{1,0:T(8,128)(2,1)}) %all-gather.2.cloned.1.call-update) | async-done | bytes 8388624 | tf_op jit(solution)/shard_map/all_gather | solution.py:69
  133.2 16.4 fusion.46
  149.6 56.8 %fusion.81 = f32[1024,64,64]{2,1,0:T(8,128)} fusion(f32[2,64,1024]{1,0,2:T(2,128)S(1)} %copy-done.4, f32[2,64,1024]{1,0,2:T(2,128)S(1)} %copy-done.3), kind=kOutput, calls=%fused_computation.135 | convolution fusion | flops 100663296 | bytes 17825792 | tf_op jit(solution)/shard_map/nbc,njc->bjc/dot_general | solution.py:45
  215.3 706.2 %while.12 = (s32[]{:T(128)}, f32[16,1024]{1,0:T(8,128)S(1)}, f32[16,1024]{1,0:T(8,128)S(1)}, f32[16,1024]{1,0:T(8,128)S(1)}, f32[16,1024]{1,0:T(8,128)S(1)}, /*index=5*/f32[16,1024]{1,0:T(8,128)S(1)}, s32[]{:T(128)}) while((s32[]{:T(128)}, f32[16,1024]{1,0:T(8,128)S(1)}, f32[16,1024]{1,0:T(8,128)S(1)}, f32[16,1024]{1,0:T(8,128)S(1)}, ...), condition=%wide.region_1.2_spmd, body=%wide.region_0.1_spmd.sunk | while | flops 65538 | bytes 983197 | solution.py:93
  526.4 9.2 collective-permute-start
  551.1 9.2 collective-permute-start
  575.8 9.2 collective-permute-start
  600.6 9.2 collective-permute-start
  625.3 9.2 collective-permute-start
  650.0 9.2 collective-permute-start
  674.8 9.2 collective-permute-start
  699.5 9.2 collective-permute-start
  724.3 9.2 collective-permute-start
  749.0 9.2 collective-permute-start
  773.7 9.2 collective-permute-start
  798.5 9.2 collective-permute-start
  823.2 9.2 collective-permute-start
  848.0 9.2 collective-permute-start
  872.7 9.2 collective-permute-start
  897.4 9.2 collective-permute-start
  931.4 57.2 %fusion.11 = f32[16,1024]{0,1:T(8,128)} fusion(f32[16,1024]{0,1:T(8,128)S(1)} %copy.87, f32[1024,64,64]{2,1,0:T(8,128)} %fusion.81, pred[64,64]{0,1:T(8,128)(4,1)S(1)} %iota_compare_fusion, f32[16,1024]{0,1:T(8,128)} %copy.104), kind=kOutput, calls=%fused_computation.16 | convolution fusion | flops 813678592 | bytes 16977920 | tf_op jit(solution)/shard_map/bjc,mbc->mjc/dot_general | solution.py:48
  992.6 16.3 multiply_reduce_fusion
  1010.1 18.5 %gather_fusion = f32[4096,1024]{1,0:T(8,128)} fusion(f32[64,1024]{1,0:T(8,128)S(1)} %bitcast.115, s32[4096]{0:T(1024)S(1)} %copy-done.31), kind=kCustom, calls=%fused_computation | custom fusion | bytes 33570816 | tf_op jit(solution)/shard_map/gather | solution.py:28
  1028.6 30.9 %copy.88 = f32[64,64,1024]{0,1,2:T(8,128)} copy(f32[64,64,1024]{2,1,0:T(8,128)} %bitcast.116) | data formatting | bytes 33554432 | tf_op jit(solution)/shard_map/gather | solution.py:28
  1059.5 31.1 %fusion.3 = f32[1024,2,64]{2,1,0:T(2,128)} fusion(f32[2,64,1024]{1,0,2:T(2,128)} %copy.89, f32[64,64,1024]{0,1,2:T(8,128)} %copy.88, pred[64,64]{0,1:T(8,128)(4,1)S(1)} %iota_compare_fusion.1), kind=kOutput, calls=%fused_computation.7 | convolution fusion | flops 104857600 | bytes 17829888 | tf_op jit(solution)/shard_map/bjc,njc->nbc/dot_general | solution.py:31
  1090.6 56.7 %fusion.53 = f32[2,64,1024]{1,0,2:T(2,128)} fusion(f32[2,64,1024]{1,0,2:T(2,128)S(1)} %copy-done.5, f32[64,64,1024]{0,1,2:T(8,128)} %copy.88, pred[64,64]{0,1:T(8,128)(4,1)S(1)} %iota_compare_fusion.1), kind=kOutput, calls=%fused_computation.70 | convolution fusion | flops 104857600 | bytes 17829888 | tf_op jit(solution)/shard_map/jbc,njc->nbc/dot_general | solution.py:32
  1150.4 13.1 fusion.22
  1165.7 13.6 fusion.50
  1195.2 382.8 %reduce-scatter.2.cloned.1.call-done = f32[16,4096]{1,0:T(8,128)} async-done(((f32[1024,4096]{1,0:T(8,128)}), f32[16,4096]{1,0:T(8,128)}) %reduce-scatter.2.cloned.1.call-update) | async-done | bytes 262160 | tf_op jit(solution)/shard_map/reduce_scatter | solution.py:133
  1587.0 19.5 %all-reduce.6.cloned.1.call-done = bf16[16,4096]{1,0:T(8,128)(2,1)} async-done(((bf16[16,4096]{1,0:T(8,128)(2,1)}), bf16[16,4096]{1,0:T(8,128)(2,1)}) %all-reduce.6.cloned.1.call-update) | async-done | bytes 131088 | tf_op jit(solution)/shard_map/psum | solution.py:141
  1608.1 144.5 %all-reduce.8.cloned.1.call-done = (f32[3,1024,7]{1,2,0:T(8,128)}, f32[1024,16]{0,1:T(8,128)}) async-done(((f32[3,1024,7]{1,2,0:T(8,128)}, f32[1024,16]{0,1:T(8,128)}), (f32[3,1024,7]{1,2,0:T(8,128)}, f32[1024,16]{0,1:T(8,128)})) %all-reduce.8.cloned.1.call-update) | async-done | bytes 151568 | tf_op jit(solution)/shard_map/psum | solution.py:130
  (466 shorter events, 649.6 us)
Async XLA Ops:
  7.2 116.5 %all-gather.2.cloned.1.call-start = ((), (), s32[]{:S(2)}) async-start(), calls=%async_computation.1 | async-start | bytes 8519680 | tf_op jit(solution)/shard_map/all_gather | solution.py:69
  7.9 1570.0 %reduce-scatter.2.cloned.1.call-start = ((), (), s32[]{:S(2)}) async-start(), calls=%async_computation.2 | async-start | bytes 17039360 | tf_op jit(solution)/shard_map/reduce_scatter | solution.py:133
  502.6 9.5 collective-permute-start
  514.6 9.3 collective-permute-start
  526.4 10.5 collective-permute-start
  539.3 9.3 collective-permute-start
  551.1 10.5 collective-permute-start
  564.1 9.3 collective-permute-start
  575.8 10.5 collective-permute-start
  588.8 9.3 collective-permute-start
  600.6 10.5 collective-permute-start
  613.5 9.3 collective-permute-start
  625.3 10.5 collective-permute-start
  638.3 9.3 collective-permute-start
  650.0 10.5 collective-permute-start
  663.0 9.3 collective-permute-start
  674.8 10.5 collective-permute-start
  687.8 9.3 collective-permute-start
  699.5 10.5 collective-permute-start
  724.3 10.5 collective-permute-start
  737.2 9.3 collective-permute-start
  749.0 10.5 collective-permute-start
  773.7 10.5 collective-permute-start
  798.5 10.5 collective-permute-start
  823.2 10.5 collective-permute-start
  836.2 9.3 collective-permute-start
  848.0 10.5 collective-permute-start
  872.7 10.5 collective-permute-start
  897.4 10.5 collective-permute-start
  1191.8 414.6 %all-reduce.6.cloned.1.call-start = ((), (), s32[]{:S(2)}) async-start(), calls=%async_computation.3 | async-start | bytes 262144 | tf_op jit(solution)/shard_map/psum | solution.py:141
  1193.9 389.3 %collective-permute-start.3 = (bf16[3,6,1024]{2,1,0:T(8,128)(2,1)S(1)}, bf16[3,6,1024]{2,1,0:T(8,128)(2,1)S(1)}, u32[]{:S(2)}, u32[]{:S(2)}) collective-permute-start(bf16[3,6,1024]{2,1,0:T(8,128)(2,1)S(1)} %slice.223), channel_id=1, source_target_pairs={{2,0},{4,2},{6,4},{8,6},{10,8},{12,10},{14,12},{16,14},{18,16},{20... | collective-permute-start | bytes 110600 | tf_op jit(solution)/shard_map/ppermute | solution.py:14
  1579.6 173.0 %all-reduce.8.cloned.1.call-start = ((), (), s32[]{:S(2)}) async-start(), calls=%async_computation.4 | async-start | bytes 327680 | tf_op jit(solution)/shard_map/psum | solution.py:130
  (139 other events, 1398.1 us)
Sparse Core Ops, SparseCore 0:
  9.8 113.9 all-gather.1
  1192.0 385.9 reduce-scatter.1
  1581.0 25.4 all-reduce.5
  1611.8 140.7 all-reduce.7
where the time goes:
time: 1770 us; the launch traced here: 1760 us
  waiting for transfers between devices  740 us (42%)
  starting transfers between devices  550 us (31%)
  matrix products  276 us (16%)
  local copies, waits for them, and re-layouts  95.9 us (5%)
  other arithmetic  83.6 us (5%)
    ppermute x128, starting transfers between devices, passed_along(): lax.ppermute(value, axis, [(source, source + steps) for source in range(f...  550 us
    reduce_scatter x1, waiting for transfers between devices, shards(): lax.psum_scatter(lax.dot_general(gated, out_rows, (((0,), (0,)), ((), ())...  383 us
    psum x1, waiting for transfers between devices, shards(): lax.psum((taps_part, residue_part), ('ctx', 'dp'))  145 us
    ppermute x128, waiting for transfers between devices, passed_along(): lax.ppermute(value, axis, [(source, source + steps) for source in range(f...  116 us
    all_gather x1, waiting for transfers between devices, shards(): lax.all_gather(out_weight, 'ctx', axis=0, tiled=True)  76.3 us
    dot_general x1, matrix products, local_modes(): partial_y = jnp.einsum('bjc,mbc->mjc', correlation, growth, precision=HIGH)  57.2 us
    dot_general x1, matrix products, local_modes(): jnp.einsum('nbc,njc->bjc', mixed_blocks, grad_blocks, precision=HIGH)  56.8 us
    dot_general x1, matrix products, local_modes(): jnp.einsum('jbc,njc->nbc', toeplitz, grad_blocks, precision=HIGH)  56.7 us
  transfers between devices with their start and end apart: 132, of which 67 were waited for; matrix products, arithmetic and copies ran while one was open for 3% of the time, Pallas kernels for 0%

commit v1 on v0

v1 whole, which is shorter than its diff:
```python
import functools

import jax
import jax.numpy as jnp
from jax import lax
from jax.experimental import pallas as pl
from jax.experimental.pallas import tpu as pltpu
from jax.sharding import Mesh, PartitionSpec as P

BF = jnp.bfloat16
F32 = jnp.float32
T = 128
C = 1024
D = 4096
M = 16
PAD = 64
ROWS = 8 * T
XR = PAD + ROWS
CTX = ("yl", "x", "z", "core")
GRP = ("yl", "x", "z")
LEVELS = (("core", 2, 1), ("z", 4, 2), ("x", 4, 8), ("yl", 2, 32))

VMEM = pl.BlockSpec(memory_space=pltpu.VMEM)


def call(body, outs, ins, scratch=(), flops=10_000_000):
    return pl.pallas_call(
        body,
        out_shape=outs,
        in_specs=[VMEM] * len(ins),
        out_specs=[VMEM] * len(outs),
        scratch_shapes=list(scratch),
        compiler_params=pltpu.CompilerParams(vmem_limit_bytes=40 * 1024 * 1024),
        cost_estimate=pl.CostEstimate(flops=flops, bytes_accessed=4_000_000, transcendentals=0),
    )(*ins)


def row(ref, at):
    return ref[pl.ds(pl.multiple_of(at, 8), 8), :]


def put(ref, at, value):
    ref[pl.ds(pl.multiple_of(at, 8), 8), :] = value


def shape_kernel(q, k, v, halo, taps, factor, xs, ys, ends):
    for i, src in enumerate((q, k, v)):
        base = i * XR
        xs[base : base + PAD, :] = halo[i * PAD : (i + 1) * PAD, :]
        for g in range(T // 16):
            for s in range(8):
                val = src[16 * g : 16 * g + 16, 128 * s : 128 * s + 128].astype(F32)
                xs[pl.ds(base + PAD + 128 * g + s, 16, stride=8), :] = val
    for i in range(3):
        tap = [taps[(i * 7 + j) * 8 : (i * 7 + j) * 8 + 8, :] for j in range(7)]

        def body(b, _):
            at = i * XR + PAD + b * 64
            win = [row(xs, at + 8 * d) for d in range(-6, 8)]
            for t in range(8):
                acc = tap[0] * win[t + 6]
                for j in range(1, 7):
                    acc = acc + tap[j] * win[t + 6 - j]
                put(ys, i * ROWS + b * 64 + 8 * t, acc)
            return 0

        lax.fori_loop(0, T // 8, body, 0)
    fac = [factor[8 * m : 8 * m + 8, :] for m in range(M)]

    def step(b, state):
        for u in range(8):
            at = b * 64 + u * 8
            mixed = row(ys, ROWS + at) * row(ys, 2 * ROWS + at)
            state = tuple(f * x + mixed for f, x in zip(fac, state))
        return state

    state = lax.fori_loop(0, T // 8, step, (jnp.zeros((8, 128), F32),) * M)
    for m in range(M):
        ends[8 * m : 8 * m + 8, :] = state[m]


def fore_kernel(ys, factor, coef, incoming, filt, gated_t, scr):
    state = tuple(incoming[8 * m : 8 * m + 8, :] for m in range(M))

    def step(b, state):
        for u in range(4):
            at = b * 32 + u * 8
            mixed = row(ys, ROWS + at) * row(ys, 2 * ROWS + at)
            state = tuple(factor[8 * m : 8 * m + 8, :] * state[m] + mixed for m in range(M))
            terms = [coef[8 * m : 8 * m + 8, :] * state[m] for m in range(M)]
            while len(terms) > 1:
                terms = [a + b for a, b in zip(terms[::2], terms[1::2])]
            put(filt, at, terms[0])
            put(scr, at, terms[0] * row(ys, at))
        return state

    lax.fori_loop(0, T // 4, step, state)
    for s in range(8):
        block = scr[pl.ds(s, T, stride=8), :]
        turned = block.T.astype(BF)
        for n in range(8):
            at = 64 * s + 16 * (n // 2)
            gated_t[n % 2, at : at + 16, :] = turned[16 * n : 16 * n + 16, :]


def back_kernel(up, ys, filt, factor, gf, gq, firsts, scr):
    for g in range(T // 16):
        for s in range(8):
            scr[pl.ds(128 * g + s, 16, stride=8), :] = up[16 * g : 16 * g + 16, 128 * s : 128 * s + 128]
    fac = [factor[8 * m : 8 * m + 8, :] for m in range(M)]

    def step(b, state):
        for u in range(8):
            at = ROWS - 8 - b * 64 - u * 8
            upv = row(scr, at)
            grad = upv * row(ys, at)
            put(gf, at, grad)
            put(gq, at, upv * row(filt, at))
            state = tuple(f * x + grad for f, x in zip(fac, state))
        return state

    state = lax.fori_loop(0, T // 8, step, (jnp.zeros((8, 128), F32),) * M)
    for m in range(M):
        firsts[8 * m : 8 * m + 8, :] = state[m]


def tree(terms):
    while len(terms) > 1:
        terms = [a + b for a, b in zip(terms[::2], terms[1::2])]
    return terms[0]


def last_kernel(gf, gq, ys, xs, halo, outgoing, factor, coef, inverse, norm, taps, oq, ok, ov, sums, gs, res):
    adj = [outgoing[8 * m : 8 * m + 8, :] for m in range(M)]
    for n in range(6):
        mix = tree([coef[8 * m : 8 * m + 8, :] * adj[m] for m in range(M)])
        put(gs, ROWS + 8 * n, halo[PAD + 8 * n : PAD + 8 * n + 8, :])
        put(gs, XR + ROWS + 8 * n, mix * halo[3 * PAD + 8 * n : 3 * PAD + 8 * n + 8, :])
        put(gs, 2 * XR + ROWS + 8 * n, mix * halo[2 * PAD + 8 * n : 2 * PAD + 8 * n + 8, :])
        if n < 5:
            first = halo[8 * n : 8 * n + 8, :]
            adj = [(adj[m] - first) * inverse[8 * m : 8 * m + 8, :] for m in range(M)]
    half = M // 2
    for part in range(2):
        ms = range(part * half, (part + 1) * half)
        adj = tuple(outgoing[8 * m : 8 * m + 8, :] for m in ms)
        total = (jnp.zeros((8, 128), F32),) * half

        def step(b, carry):
            adj, total = carry
            for u in range(4):
                at = ROWS - 8 - b * 32 - u * 8
                grad = row(gf, at)
                ks, vs = row(ys, ROWS + at), row(ys, 2 * ROWS + at)
                mixed = ks * vs
                adj = tuple(factor[8 * m : 8 * m + 8, :] * a + grad for m, a in zip(ms, adj))
                total = tuple(t + mixed * a for t, a in zip(total, adj))
                mix = tree([coef[8 * m : 8 * m + 8, :] * a for m, a in zip(ms, adj)])
                if part == 0:
                    put(res, at, mix)
                else:
                    mix = mix + row(res, at)
                    put(gs, at, row(gq, at))
                    put(gs, XR + at, mix * vs)
                    put(gs, 2 * XR + at, mix * ks)
            return adj, total

        adj, total = lax.fori_loop(0, T // 4, step, (adj, total))
        for m, t in zip(ms, total):
            sums[21 * 8 + 8 * m : 21 * 8 + 8 * m + 8, :] = t * norm[8 * m : 8 * m + 8, :]
    for i, out in enumerate((oq, ok, ov)):
        tap = [taps[(i * 7 + j) * 8 : (i * 7 + j) * 8 + 8, :] for j in range(7)]

        def body(b, acc):
            at = i * XR + b * 64
            win = [row(gs, at + 8 * d) for d in range(14)]
            field = [row(xs, at + PAD + 8 * d) for d in range(-6, 8)]
            acc = list(acc)
            for t in range(8):
                value = tap[0] * win[t]
                for j in range(1, 7):
                    value = value + tap[j] * win[t + j]
                put(res, b * 64 + 8 * t, value)
                for j in range(7):
                    acc[j] = acc[j] + win[t] * field[t + 6 - j]
            return tuple(acc)

        acc = lax.fori_loop(0, T // 8, body, (jnp.zeros((8, 128), F32),) * 7)
        for j in range(7):
            sums[(i * 7 + j) * 8 : (i * 7 + j) * 8 + 8, :] = acc[j]
        for g in range(T // 16):
            for s in range(8):
                val = res[pl.ds(128 * g + s, 16, stride=8), :]
                out[16 * g : 16 * g + 16, 128 * s : 128 * s + 128] = val.astype(BF)


def sds(*shape, dtype=F32):
    return jax.ShapeDtypeStruct(shape, dtype)


def shifted(value, steps):
    n = 64
    first, last = max(0, -steps), min(n, n - steps)
    return lax.ppermute(value, CTX, [(i, i + steps) for i in range(first, last)])


def swapped(value, axis):
    return lax.ppermute(value, axis, [(0, 1), (1, 0)])


def carry_weights(rate, forward):
    plan = []
    for axis, n, stride in LEVELS:
        mine = lax.axis_index(axis)
        j = jnp.arange(n)
        if forward:
            inside, lag, all_lag, here = j < mine, mine - 1 - j, n - 1 - j, mine
        else:
            inside, lag, all_lag, here = j > mine, j - 1 - mine, j, n - 1 - mine
        unit = rate * (T * stride)
        lag = jnp.maximum(lag, 0).astype(F32)[:, None, None]
        prefix = jnp.where(inside[:, None, None], jnp.exp(-unit * lag), 0.0)
        whole = jnp.exp(-unit * all_lag.astype(F32)[:, None, None])
        decay = jnp.exp(-unit * here.astype(F32))
        plan.append((axis, prefix, whole, decay))
    return plan


def carried(ends, plan):
    scale, result = None, None
    for level, (axis, prefix, whole, decay) in enumerate(plan):
        parts = lax.all_gather(ends, axis)
        entering = jnp.sum(prefix * parts, axis=0)
        result = entering if level == 0 else result + scale * entering
        scale = decay if level == 0 else scale * decay
        ends = jnp.sum(whole * parts, axis=0)
    return result


def shards(query_proj, key_proj, value_proj, grad_out, out_weight, short_taps, residues, decay_rate):
    q, k, v, go = query_proj[0], key_proj[0], value_proj[0], grad_out[0]
    core = lax.axis_index("core")
    mine_w = lax.all_to_all(jnp.broadcast_to(out_weight, (32, 16, D)), GRP, 0, 0)
    other_w = swapped(mine_w, "core")
    weight = jnp.where(
        core == 0, jnp.stack([mine_w, other_w], axis=1), jnp.stack([other_w, mine_w], axis=1)
    ).reshape(C, D)

    tail = jnp.stack([q[T - 8 :], k[T - 8 :], v[T - 8 :]])
    behind = shifted(tail, 1).astype(F32).reshape(3 * PAD, 128)

    rate = decay_rate.T.reshape(M * 8, 128)
    factor = jnp.exp(-rate)
    norm = jnp.sqrt(-jnp.expm1(-2.0 * rate))
    coef = residues.T.reshape(M * 8, 128) * norm
    taps = jnp.transpose(short_taps, (0, 2, 1)).reshape(21 * 8, 128)

    xs, ys, ends = call(
        shape_kernel, [sds(3 * XR, 128), sds(3 * ROWS, 128), sds(M * 8, 128)], (q, k, v, behind, taps, factor)
    )
    incoming = carried(ends, carry_weights(rate, True))
    filt, gated_t = call(
        fore_kernel,
        [sds(ROWS, 128), sds(2, 512, T, dtype=BF)],
        (ys, factor, coef, incoming),
        [pltpu.VMEM((ROWS, 128), F32)],
    )
    theirs = lax.dynamic_index_in_dim(gated_t, 1 - core, 0, keepdims=False)
    mine = lax.dynamic_index_in_dim(gated_t, core, 0, keepdims=False)
    sent = jnp.dot(theirs, go, preferred_element_type=F32).astype(BF)
    got = swapped(sent, "core")
    kept = (jnp.dot(mine, go, preferred_element_type=F32) + got.astype(F32)).astype(BF)
    pieces = lax.all_to_all(kept.reshape(32, 16, D), GRP, 0, 0)
    summed = jnp.sum(pieces.astype(F32), axis=0).astype(BF)
    weight_grad = summed.astype(F32) + swapped(summed, "yh").astype(F32)

    upstream = lax.dot_general(go, weight, (((1,), (1,)), ((), ())), preferred_element_type=F32)
    gf, gq, firsts = call(
        back_kernel,
        [sds(ROWS, 128), sds(ROWS, 128), sds(M * 8, 128)],
        (upstream, ys, filt, factor),
        [pltpu.VMEM((ROWS, 128), F32)],
    )
    head = jnp.concatenate([gf[:PAD], gq[:PAD], ys[ROWS : ROWS + PAD], ys[2 * ROWS : 2 * ROWS + PAD]], axis=0)
    ahead = shifted(head, -1)
    outgoing = carried(firsts, carry_weights(rate, False))
    oq, ok, ov, sums = call(
        last_kernel,
        [sds(T, C, dtype=BF)] * 3 + [sds((21 + M) * 8, 128)],
        (gf, gq, ys, xs, ahead, outgoing, factor, coef, jnp.exp(rate), norm, taps),
        [pltpu.VMEM((3 * XR, 128), F32), pltpu.VMEM((ROWS, 128), F32)],
    )
    for axis in ("core", "z", "x", ("yl", "yh")):
        sums = jnp.sum(lax.all_gather(sums, axis), axis=0)
    taps_grad = jnp.transpose(sums[: 21 * 8].reshape(3, 7, C), (0, 2, 1))
    residue_grad = sums[21 * 8 :].reshape(M, C).T
    return (oq[None], ok[None], ov[None], weight_grad, taps_grad, residue_grad)


def solution(mesh):
    grid = Mesh(mesh.devices.reshape(2, 4, 4, 2, 2), ("yl", "x", "z", "core", "yh"))
    stream = P("yh", CTX, None)
    return jax.shard_map(
        shards,
        mesh=grid,
        in_specs=(stream, stream, stream, stream, P(CTX, None), P(), P(), P()),
        out_specs=(stream, stream, stream, P(CTX, None), P(), P()),
        check_vma=False,
    )
```

time: 1770 us -> 280 us (0.16)
  waiting for transfers between devices: 740 us -> 7 us
  starting transfers between devices: 550 us -> 23 us
  matrix products: 276 us -> 11.5 us
  blocking collectives: 0 us -> 192 us
  local copies, waits for them, and re-layouts: 95.9 us -> 15 us
  other arithmetic: 83.6 us -> 19.8 us
    ppermute x128 -> x5, starting transfers between devices: 550 us -> 6.16 us  [the longest x3 3.42 us: swapped(): return lax.ppermute(value, axis, [(0, 1), (1, 0)])]
    reduce_scatter x1 -> x0, waiting for transfers between devices: 383 us -> none  [shards(): lax.psum_scatter(lax.dot_general(gated, out_rows, (((0,), (0,)), ((), ())...]
    dot_general x10 -> x3, matrix products: 276 us -> 11.5 us  [the longest x1 5.41 us: shards(): jnp.dot(mine, go, preferred_element_type=F32) + got.astype(F32)]
    all_gather x0 -> x12, blocking collectives: none -> 192 us  [the longest x8 147 us: carried(): parts = lax.all_gather(ends, axis)]
    psum x2 -> x0, waiting for transfers between devices: 164 us -> none  [the longest x1 145 us: shards(): lax.psum((taps_part, residue_part), ('ctx', 'dp'))]
    ppermute x128 -> x5, waiting for transfers between devices: 116 us -> 7 us  [the longest x3 6.99 us: swapped(): return lax.ppermute(value, axis, [(0, 1), (1, 0)])]
    all_gather x1 -> x0, waiting for transfers between devices: 76.3 us -> none  [shards(): lax.all_gather(out_weight, 'ctx', axis=0, tiled=True)]
    gather x2 -> x0, local copies, waits for them, and re-layouts: 49.5 us -> none  [local_modes(): toeplitz = jnp.where(lower_mask[:, :, None], kernel[lag_index], 0.0)]
  transfers between devices with their start and end apart: 132 -> 7, of which waited for: 67 -> 1; matrix products, arithmetic and copies ran while one was open for 3% -> 12% of each run, Pallas kernels for 0% -> 4%
where the time goes in v1:
time: 280 us; the launch traced here: 279 us
  blocking collectives  192 us (69%)
  starting transfers between devices  23 us (8%)
  other arithmetic  19.8 us (7%)
  local copies, waits for them, and re-layouts  15 us (5%)
  matrix products  11.5 us (4%)
  Pallas kernels  9.99 us (4%)
  waiting for transfers between devices  7 us (2%)
    all_gather x8, blocking collectives, carried(): parts = lax.all_gather(ends, axis)  147 us
    all_gather x4, blocking collectives, shards(): sums = jnp.sum(lax.all_gather(sums, axis), axis=0)  45 us
    pallas_call x4, Pallas kernels, call(): pl.pallas_call(body, out_shape=outs, in_specs=[VMEM] * len(ins), out_spec...  9.99 us
    all_to_all x1, starting transfers between devices, shards(): lax.all_to_all(jnp.broadcast_to(out_weight, (32, 16, D)), GRP, 0, 0)  9.53 us
    select_n x1, other arithmetic, shards(): jnp.where(core == 0, jnp.stack([mine_w, other_w], axis=1), jnp.stack([oth...  8.47 us
    unnamed x42, local copies, waits for them, and re-layouts  8.06 us
    all_to_all x1, starting transfers between devices, shards(): pieces = lax.all_to_all(kept.reshape(32, 16, D), GRP, 0, 0)  7.35 us
    ppermute x3, waiting for transfers between devices, swapped(): return lax.ppermute(value, axis, [(0, 1), (1, 0)])  6.99 us
  transfers between devices with their start and end apart: 7, of which 1 were waited for; matrix products, arithmetic and copies ran while one was open for 12% of the time, Pallas kernels for 4%

profile of v1, /device:TPU:0, one launch (start us, length us, event | category | flops | bytes accessed | tf_op | source)
XLA Modules:
  0.0 279.3 jit_solution(682882748336487391)
XLA Ops:
  0.6 3.5 %broadcast_in_dim.108 = bf16[32,16,4096]{2,1,0:T(8,128)(2,1)} broadcast(bf16[16,4096]{1,0:T(8,128)(2,1)} %param.12), dimensions={1,2} | broadcast | bytes 4325376 | tf_op jit(solution)/shard_map/broadcast_in_dim | solution.py:243
  4.2 9.5 %all-to-all-start = ((bf16[32,16,4096]{2,1,0:T(8,128)(2,1)}), bf16[32,16,4096]{2,1,0:T(8,128)(2,1)}, u32[]{:S(2)}, u32[]{:S(2)}) async-start(bf16[32,16,4096]{2,1,0:T(8,128)(2,1)} %broadcast_in_dim.108), calls=%async_computation | async-start | bytes 8388608 | tf_op jit(solution)/shard_map/all_to_all | solution.py:243
  13.7 1.5 collective-permute-start.1
  19.5 1.8 shard_map.127
  21.3 1.2 copy-done.1
  22.5 24.4 %all-gather = f32[256,128]{1,0:T(8,128)S(1)} all-gather(f32[128,128]{1,0:T(8,128)S(1)} %get-tuple-element.19), channel_id=2, replica_groups=mesh['yl'=2,'x'=4,'z'=4,'core'=2,'yh'=2] {'core'}, dimensions={0}, use_global_device_ids=true | all-gather | bytes 196608 | tf_op jit(solution)/shard_map/all_gather | solution.py:232
  47.1 30.5 %all-gather.1 = f32[512,128]{1,0:T(8,128)S(1)} all-gather(f32[128,128]{1,0:T(8,128)S(1)} %get-tuple-element.41), channel_id=3, replica_groups=mesh['yl'=2,'x'=4,'z'=4,'core'=2,'yh'=2] {'z'}, dimensions={0}, use_global_device_ids=true | all-gather | bytes 327680 | tf_op jit(solution)/shard_map/all_gather | solution.py:232
  77.8 21.5 %all-gather.2 = f32[512,128]{1,0:T(8,128)S(1)} all-gather(f32[128,128]{1,0:T(8,128)S(1)} %get-tuple-element.35), channel_id=4, replica_groups=mesh['yl'=2,'x'=4,'z'=4,'core'=2,'yh'=2] {'x'}, dimensions={0}, use_global_device_ids=true | all-gather | bytes 327680 | tf_op jit(solution)/shard_map/all_gather | solution.py:232
  99.3 1.0 multiply_reduce_fusion.5
  100.3 5.6 %all-gather.3 = f32[256,128]{1,0:T(8,128)S(1)} all-gather(f32[128,128]{1,0:T(8,128)S(1)} %get-tuple-element.37), channel_id=5, replica_groups=mesh['yl'=2,'x'=4,'z'=4,'core'=2,'yh'=2] {'yl'}, dimensions={0}, use_global_device_ids=true | all-gather | bytes 196608 | tf_op jit(solution)/shard_map/all_gather | solution.py:232
  107.8 1.5 shard_map.128
  110.1 3.2 %convolution_convert_fusion = bf16[512,4096]{1,0:T(8,128)(2,1)} fusion(bf16[1,128,4096]{2,1,0:T(8,128)(2,1)S(1)} %copy-done, bf16[2,512,128]{2,1,0:T(8,128)(2,1)S(1)} %get-tuple-element.28, s32[]{:T(128)S(6)} %select_n.63), kind=kOutput, calls=%fused_computation.2 | convolution fusion | flops 538968064 | bytes 5373956 | tf_op jit(solution)/shard_map/dot_general | solution.py:270
  113.8 7.0 %collective-permute-done.3 = bf16[512,4096]{1,0:T(8,128)(2,1)} collective-permute-done((bf16[512,4096]{1,0:T(8,128)(2,1)}, bf16[512,4096]{1,0:T(8,128)(2,1)}, u32[]{:S(2)}, u32[]{:S(2)}) %collective-permute-start.3) | collective-permute-done | bytes 4194336 | tf_op jit(solution)/shard_map/ppermute | solution.py:208
  120.8 5.4 %add_convert_fusion = bf16[512,4096]{1,0:T(8,128)(2,1)} fusion(bf16[512,4096]{1,0:T(8,128)(2,1)} %collective-permute-done.3, bf16[1,128,4096]{2,1,0:T(8,128)(2,1)S(1)} %copy-done, bf16[2,512,128]{2,1,0:T(8,128)(2,1)S(1)} %get-tuple-element.28, s32[]{:T(128)S(6)} %select_n.62), kind=kOutput, calls=%fused_computation.1 | convolution fusion | flops 543162368 | bytes 9568260 | tf_op jit(solution)/shard_map/dot_general | solution.py:272
  126.2 7.3 %all-to-all-start.1 = ((bf16[32,16,4096]{2,1,0:T(8,128)(2,1)}), bf16[32,16,4096]{2,1,0:T(8,128)(2,1)}, u32[]{:S(2)}, u32[]{:S(2)}) async-start(bf16[32,16,4096]{2,1,0:T(8,128)(2,1)} %bitcast.61), calls=%async_computation.1 | async-start | bytes 8388608 | tf_op jit(solution)/shard_map/all_to_all | solution.py:273
  134.4 8.5 %maximum_select_fusion = bf16[32,2,16,4096]{3,2,1,0:T(8,128)(2,1)S(1)} fusion(bf16[32,1,16,4096]{3,2,1,0:T(8,128)(2,1)} %bitcast.1, bf16[32,1,16,4096]{3,2,1,0:T(8,128)(2,1)} %bitcast, pred[]{:T(512)S(6)} %eq.3), kind=kLoop, calls=%fused_computation | loop fusion | flops 12582912 | bytes 16777216 | tf_op jit(solution)/shard_map/jit(_where)/select_n | solution.py:245
  142.9 2.9 %convolution_bitcast_fusion.up = f32[128,1024]{1,0:T(8,128)S(1)} fusion(bf16[1024,4096]{1,0:T(8,128)(2,1)S(1)} %bitcast.62, bf16[1,128,4096]{2,1,0:T(8,128)(2,1)S(1)} %copy-done), kind=kOutput, calls=%fused_computation.3 | convolution fusion | flops 1073741824 | bytes 9961472 | tf_op jit(solution)/shard_map/dot_general | solution.py:277
  148.0 1.3 collective-permute-start.2
  149.3 2.7 all-gather.4
  152.1 39.1 %all-gather.5 = f32[512,128]{1,0:T(8,128)S(1)} all-gather(f32[128,128]{1,0:T(8,128)S(1)} %get-tuple-element.39), channel_id=7, replica_groups=mesh['yl'=2,'x'=4,'z'=4,'core'=2,'yh'=2] {'z'}, dimensions={0}, use_global_device_ids=true | all-gather | bytes 327680 | tf_op jit(solution)/shard_map/all_gather | solution.py:232
  191.4 18.1 %all-gather.6 = f32[512,128]{1,0:T(8,128)S(1)} all-gather(f32[128,128]{1,0:T(8,128)S(1)} %get-tuple-element.31), channel_id=8, replica_groups=mesh['yl'=2,'x'=4,'z'=4,'core'=2,'yh'=2] {'x'}, dimensions={0}, use_global_device_ids=true | all-gather | bytes 327680 | tf_op jit(solution)/shard_map/all_gather | solution.py:232
  209.7 4.9 %all-gather.7 = f32[256,128]{1,0:T(8,128)S(1)} all-gather(f32[128,128]{1,0:T(8,128)S(1)} %get-tuple-element.33), channel_id=9, replica_groups=mesh['yl'=2,'x'=4,'z'=4,'core'=2,'yh'=2] {'yl'}, dimensions={0}, use_global_device_ids=true | all-gather | bytes 196608 | tf_op jit(solution)/shard_map/all_gather | solution.py:232
  215.6 3.5 %reduce_sum.188 = bf16[16,4096]{1,0:T(8,128)(2,1)} reduce(bf16[32,16,4096]{2,1,0:T(8,128)(2,1)} %all-to-all-done.1, bf16[]{:T(256)} %constant.56.clone.1), dimensions={0}, to_apply=%region_14.15 | reduce | flops 2031616 | bytes 4325378 | tf_op jit(solution)/shard_map/reduce_sum | solution.py:274
  219.1 2.9 %collective-permute-start.4 = (bf16[16,4096]{1,0:T(8,128)(2,1)}, bf16[16,4096]{1,0:T(8,128)(2,1)}, u32[]{:S(2)}, u32[]{:S(2)}) collective-permute-start(bf16[16,4096]{1,0:T(8,128)(2,1)} %reduce_sum.188), channel_id=1, source_target_pairs={{0,1},{1,0},{2,3},{3,2},{4,5},{5,4},{6,7},{7,6},{8,9},{9,8},{10,11... | collective-permute-start | bytes 393224 | tf_op jit(solution)/shard_map/ppermute | solution.py:208
  222.0 1.4 copy-done.2
  223.5 1.0 copy-done.4
  225.4 5.9 %shard_map.130 = (bf16[128,1024]{1,0:T(8,128)(2,1)}, bf16[128,1024]{1,0:T(8,128)(2,1)}, bf16[128,1024]{1,0:T(8,128)(2,1)}, f32[296,128]{1,0:T(8,128)S(1)}) custom-call(f32[1024,128]{1,0:T(8,128)S(1)} %get-tuple-element.21.gf, f32[1024,128]{1,0:T(8,128)S(1)} %copy-done.4, f32[3072,128]{1,0:T(8,128)S(1)} %get-tuple-element.18.ys, f32[3264,128]{1,0:T(8,128)S(1)} %copy-done.2, ...), custom_call_target="tpu_custom_call" | custom-call | flops 10000000 | bytes 4000000 | tf_op jit(solution)/shard_map/pallas_call | solution.py:27
  231.3 2.1 all-gather.8
  233.4 13.6 %all-gather.9 = f32[1184,128]{1,0:T(8,128)S(1)} all-gather(f32[296,128]{1,0:T(8,128)S(1)} %reduce_sum.189), channel_id=11, replica_groups=mesh['yl'=2,'x'=4,'z'=4,'core'=2,'yh'=2] {'z'}, dimensions={0}, use_global_device_ids=true | all-gather | bytes 757760 | tf_op jit(solution)/shard_map/all_gather | solution.py:294
  247.1 13.2 %all-gather.10 = f32[1184,128]{1,0:T(8,128)S(1)} all-gather(f32[296,128]{1,0:T(8,128)S(1)} %reduce_sum.190), channel_id=12, replica_groups=mesh['yl'=2,'x'=4,'z'=4,'core'=2,'yh'=2] {'x'}, dimensions={0}, use_global_device_ids=true | all-gather | bytes 757760 | tf_op jit(solution)/shard_map/all_gather | solution.py:294
  260.3 16.0 %all-gather.11 = f32[1184,128]{1,0:T(8,128)S(1)} all-gather(f32[296,128]{1,0:T(8,128)S(1)} %reduce_sum.191), channel_id=13, replica_groups=mesh['yl'=2,'x'=4,'z'=4,'core'=2,'yh'=2] {'yl','yh'}, dimensions={0}, use_global_device_ids=true | all-gather | bytes 757760 | tf_op jit(solution)/shard_map/all_gather | solution.py:294
  277.7 1.6 convert_add_fusion
  (104 shorter events, 14.2 us)
Async XLA Ops:
  0.6 109.4 %copy-start = (bf16[1,128,4096]{2,1,0:T(8,128)(2,1)S(1)}, bf16[1,128,4096]{2,1,0:T(8,128)(2,1)}, u32[]{:S(2)}) copy-start(bf16[1,128,4096]{2,1,0:T(8,128)(2,1)} %param.11) | copy-start | bytes 3145732
  4.1 9.6 %slice-start = ((bf16[1,128,1024]{2,1,0:T(8,128)(2,1)}), bf16[1,8,1024]{2,1,0:T(8,128)(2,1)S(1)}, s32[]{:S(2)}) async-start(bf16[1,128,1024]{2,1,0:T(8,128)(2,1)} %param.8), calls=%async_computation.2 | async-start | bytes 32768 | tf_op jit(solution)/shard_map/slice | solution.py:249
  4.1 9.6 %slice-start.1 = ((bf16[1,128,1024]{2,1,0:T(8,128)(2,1)}), bf16[1,8,1024]{2,1,0:T(8,128)(2,1)S(1)}, s32[]{:S(2)}) async-start(bf16[1,128,1024]{2,1,0:T(8,128)(2,1)} %param.9), calls=%async_computation.3 | async-start | bytes 32768 | tf_op jit(solution)/shard_map/slice | solution.py:249
  4.1 9.6 %slice-start.2 = ((bf16[1,128,1024]{2,1,0:T(8,128)(2,1)}), bf16[1,8,1024]{2,1,0:T(8,128)(2,1)S(1)}, s32[]{:S(2)}) async-start(bf16[1,128,1024]{2,1,0:T(8,128)(2,1)} %param.10), calls=%async_computation.4 | async-start | bytes 32768 | tf_op jit(solution)/shard_map/slice | solution.py:249
  4.1 11.2 %copy-start.20 = (f32[1024,16]{0,1:T(8,128)S(1)}, f32[1024,16]{0,1:T(8,128)}, u32[]{:S(2)}) copy-start(f32[1024,16]{0,1:T(8,128)} %param.15) | copy-start | bytes 196612
  4.1 11.9 %copy-start.18 = (f32[3,1024,7]{1,2,0:T(8,128)S(1)}, f32[3,1024,7]{1,2,0:T(8,128)}, u32[]{:S(2)}) copy-start(f32[3,1024,7]{1,2,0:T(8,128)} %param.13) | copy-start | bytes 258052
  4.1 11.9 %copy-start.19 = (f32[1024,16]{0,1:T(8,128)S(1)}, f32[1024,16]{0,1:T(8,128)}, u32[]{:S(2)}) copy-start(f32[1024,16]{0,1:T(8,128)} %param.14) | copy-start | bytes 196612
  4.2 13.4 %copy-start.7 = (bf16[1,128,1024]{2,1,0:T(8,128)(2,1)S(1)}, bf16[1,128,1024]{2,1,0:T(8,128)(2,1)}, u32[]{:S(2)}) copy-start(bf16[1,128,1024]{2,1,0:T(8,128)(2,1)} %param.8) | copy-start | bytes 786436
  4.2 109.1 %all-to-all-start = ((bf16[32,16,4096]{2,1,0:T(8,128)(2,1)}), bf16[32,16,4096]{2,1,0:T(8,128)(2,1)}, u32[]{:S(2)}, u32[]{:S(2)}) async-start(bf16[32,16,4096]{2,1,0:T(8,128)(2,1)} %broadcast_in_dim.108), calls=%async_computation | async-start | bytes 8388608 | tf_op jit(solution)/shard_map/all_to_all | solution.py:243
  13.7 3.8 %collective-permute-start.1 = (bf16[3,8,1024]{2,1,0:T(8,128)(2,1)S(1)}, bf16[3,8,1024]{2,1,0:T(8,128)(2,1)S(1)}, u32[]{:S(2)}, u32[]{:S(2)}) collective-permute-start(bf16[3,8,1024]{2,1,0:T(8,128)(2,1)S(1)} %pad_maximum_fusion.1), channel_id=1, source_target_pairs={{0,2},{2,4},{4,6},{6,8},{8,10},{10,12},{12,14},{14,16},{16,18},{18... | collective-permute-start | bytes 147464 | tf_op jit(solution)/shard_map/ppermute | solution.py:204
  16.2 135.8 %copy-start.11 = (f32[128,128]{1,0:T(8,128)}, f32[128,128]{1,0:T(8,128)S(1)}, u32[]{:S(2)}) copy-start(f32[128,128]{1,0:T(8,128)S(1)} %neg.85) | copy-start | bytes 196612
  16.2 97.1 %copy-start.12 = (f32[128,128]{1,0:T(8,128)}, f32[128,128]{1,0:T(8,128)S(1)}, u32[]{:S(2)}) copy-start(f32[128,128]{1,0:T(8,128)S(1)} %neg.88) | copy-start | bytes 196612
  17.6 1.0 copy-start.8
  18.5 0.9 copy-start.9
  21.3 1.2 copy-start.1
  109.3 0.8 copy-start.5
  113.3 7.5 %collective-permute-start.3 = (bf16[512,4096]{1,0:T(8,128)(2,1)}, bf16[512,4096]{1,0:T(8,128)(2,1)}, u32[]{:S(2)}, u32[]{:S(2)}) collective-permute-start(bf16[512,4096]{1,0:T(8,128)(2,1)} %convolution_convert_fusion), channel_id=1, source_target_pairs={{0,2},{2,0},{1,3},{3,1},{4,6},{6,4},{5,7},{7,5},{8,10},{10,8},{9,1... | collective-permute-start | bytes 12582920 | tf_op jit(solution)/shard_map/ppermute | solution.py:208
  113.3 21.0 %collective-permute-start = (bf16[32,16,4096]{2,1,0:T(8,128)(2,1)}, bf16[32,16,4096]{2,1,0:T(8,128)(2,1)}, u32[]{:S(2)}, u32[]{:S(2)}) collective-permute-start(bf16[32,16,4096]{2,1,0:T(8,128)(2,1)} %all-to-all-done), channel_id=1, source_target_pairs={{0,2},{2,0},{1,3},{3,1},{4,6},{6,4},{5,7},{7,5},{8,10},{10,8},{9,1... | collective-permute-start | bytes 12582920 | tf_op jit(solution)/shard_map/ppermute | solution.py:208
  126.2 7.4 %copy-start.17 = (f32[16,1024]{1,0:T(8,128)S(1)}, f32[16,1024]{1,0:T(8,128)}, u32[]{:S(2)}) copy-start(f32[16,1024]{1,0:T(8,128)} %get-tuple-element.44) | copy-start | bytes 196612
  126.2 89.4 %all-to-all-start.1 = ((bf16[32,16,4096]{2,1,0:T(8,128)(2,1)}), bf16[32,16,4096]{2,1,0:T(8,128)(2,1)}, u32[]{:S(2)}, u32[]{:S(2)}) async-start(bf16[32,16,4096]{2,1,0:T(8,128)(2,1)} %bitcast.61), calls=%async_computation.1 | async-start | bytes 8388608 | tf_op jit(solution)/shard_map/all_to_all | solution.py:273
  142.8 2.9 %copy-start.6 = (f32[1024,128]{1,0:T(8,128)S(1)}, f32[1024,128]{1,0:T(8,128)}, u32[]{:S(2)}) copy-start(f32[1024,128]{1,0:T(8,128)} %copy-done.5) | copy-start | bytes 1572868
  142.8 48.4 %copy-start.13 = (f32[128,128]{1,0:T(8,128)S(1)}, f32[128,128]{1,0:T(8,128)}, u32[]{:S(2)}) copy-start(f32[128,128]{1,0:T(8,128)} %copy-done.12) | copy-start | bytes 196612
  145.7 63.7 %copy-start.14 = (f32[128,128]{1,0:T(8,128)S(1)}, f32[128,128]{1,0:T(8,128)}, u32[]{:S(2)}) copy-start(f32[128,128]{1,0:T(8,128)} %neg.91) | copy-start | bytes 196612
  145.8 68.9 %copy-start.15 = (f32[128,128]{1,0:T(8,128)S(1)}, f32[128,128]{1,0:T(8,128)}, u32[]{:S(2)}) copy-start(f32[128,128]{1,0:T(8,128)} %neg.94) | copy-start | bytes 196612
  146.5 0.8 copy-start.3
  148.0 74.1 %collective-permute-start.2 = (f32[256,128]{1,0:T(8,128)}, f32[256,128]{1,0:T(8,128)}, u32[]{:S(2)}, u32[]{:S(2)}) collective-permute-start(f32[256,128]{1,0:T(8,128)} %pad_maximum_fusion), channel_id=1, source_target_pairs={{2,0},{4,2},{6,4},{8,6},{10,8},{12,10},{14,12},{16,14},{18,16},{20... | collective-permute-start | bytes 393224 | tf_op jit(solution)/shard_map/ppermute | solution.py:204
  219.1 58.6 %collective-permute-start.4 = (bf16[16,4096]{1,0:T(8,128)(2,1)}, bf16[16,4096]{1,0:T(8,128)(2,1)}, u32[]{:S(2)}, u32[]{:S(2)}) collective-permute-start(bf16[16,4096]{1,0:T(8,128)(2,1)} %reduce_sum.188), channel_id=1, source_target_pairs={{0,1},{1,0},{2,3},{3,2},{4,5},{5,4},{6,7},{7,6},{8,9},{9,8},{10,11... | collective-permute-start | bytes 393224 | tf_op jit(solution)/shard_map/ppermute | solution.py:208
  222.0 1.4 copy-start.2
  223.5 1.0 copy-start.4
  224.5 0.8 copy-start.10
  231.3 46.4 %copy-start.16 = (bf16[16,4096]{1,0:T(8,128)(2,1)S(1)}, bf16[16,4096]{1,0:T(8,128)(2,1)}, u32[]{:S(2)}) copy-start(bf16[16,4096]{1,0:T(8,128)(2,1)} %reduce_sum.188) | copy-start | bytes 393220

commit v2 on v1

v2 whole, which is shorter than its diff:
```python
import jax
import jax.numpy as jnp
from jax import lax
from jax.experimental import pallas as pl
from jax.experimental.pallas import tpu as pltpu
from jax.sharding import Mesh, PartitionSpec as P

BF = jnp.bfloat16
F32 = jnp.float32
T = 128
C = 1024
D = 4096
M = 16
PAD = 64
ROWS = 8 * T
XR = PAD + ROWS
CTX = ("yl", "x", "z", "core")
GRP = ("yl", "x", "z")
XZ = ("x", "z")
WA = 2688
HALF = 152
GA = 1792

VMEM = pl.BlockSpec(memory_space=pltpu.VMEM)


def call(body, outs, ins, scratch=(), flops=10_000_000):
    return pl.pallas_call(
        body,
        out_shape=outs,
        in_specs=[VMEM] * len(ins),
        out_specs=[VMEM] * len(outs),
        scratch_shapes=list(scratch),
        compiler_params=pltpu.CompilerParams(vmem_limit_bytes=16 * 1024 * 1024),
        cost_estimate=pl.CostEstimate(flops=flops, bytes_accessed=4_000_000, transcendentals=0),
    )(*ins)


def row(ref, at):
    return ref[pl.ds(pl.multiple_of(at, 8), 8), :]


def put(ref, at, value):
    ref[pl.ds(pl.multiple_of(at, 8), 8), :] = value


def shape_kernel(q, k, v, halo, taps, factor, xs, ys, ends):
    for i, src in enumerate((q, k, v)):
        base = i * XR
        xs[base : base + PAD, :] = halo[i * PAD : (i + 1) * PAD, :]
        for g in range(T // 16):
            for s in range(8):
                val = src[16 * g : 16 * g + 16, 128 * s : 128 * s + 128].astype(F32)
                xs[pl.ds(base + PAD + 128 * g + s, 16, stride=8), :] = val
    for i in range(3):
        tap = [taps[(i * 7 + j) * 8 : (i * 7 + j) * 8 + 8, :] for j in range(7)]

        def body(b, _):
            at = i * XR + PAD + b * 64
            win = [row(xs, at + 8 * d) for d in range(-6, 8)]
            for t in range(8):
                acc = tap[0] * win[t + 6]
                for j in range(1, 7):
                    acc = acc + tap[j] * win[t + 6 - j]
                put(ys, i * ROWS + b * 64 + 8 * t, acc)
            return 0

        lax.fori_loop(0, T // 8, body, 0)
    fac = [factor[8 * m : 8 * m + 8, :] for m in range(M)]

    def step(b, state):
        for u in range(8):
            at = b * 64 + u * 8
            mixed = row(ys, ROWS + at) * row(ys, 2 * ROWS + at)
            state = tuple(f * x + mixed for f, x in zip(fac, state))
        return state

    state = lax.fori_loop(0, T // 8, step, (jnp.zeros((8, 128), F32),) * M)
    for m in range(M):
        ends[8 * m : 8 * m + 8, :] = state[m]


def tree(terms):
    while len(terms) > 1:
        terms = [a + b for a, b in zip(terms[::2], terms[1::2])]
    return terms[0]


def back_kernel(core, up_mine, up_theirs, ys, ends, factor, up, gf, packed, scr):
    zero = core[0] == 0
    for s in range(8):
        half = jnp.where(core[1] == s // 4, 0, 256)
        blocks = []
        for n in range(4):
            at = pl.ds(pl.multiple_of(half + 64 * (s % 4) + 16 * n, 16), 16)
            one, two = up_mine[at, :], up_theirs[at, :]
            blocks += [jnp.where(zero, one, two), jnp.where(zero, two, one)]
        up[pl.ds(s, T, stride=8), :] = jnp.concatenate(blocks, axis=0).T
    fac = [factor[8 * m : 8 * m + 8, :] for m in range(M)]

    def step(b, state):
        for u in range(8):
            at = ROWS - 8 - b * 64 - u * 8
            grad = row(up, at) * row(ys, at)
            put(gf, at, grad)
            state = tuple(f * x + grad for f, x in zip(fac, state))
        return state

    state = lax.fori_loop(0, T // 8, step, (jnp.zeros((8, 128), F32),) * M)
    for m in range(M):
        scr[8 * m : 8 * m + 8, :] = state[m]
    for n in range(2):
        packed[pl.ds(n, 64, stride=4), :] = ends[pl.ds(n, 64, stride=2), :]
        packed[pl.ds(2 + n, 64, stride=4), :] = scr[pl.ds(n, 64, stride=2), :]


def scan_kernel(parts, span, out):
    decay = span[0:2, :]
    state = jnp.zeros((2, 128), F32)
    for b in range(64):
        out[4 * b : 4 * b + 2, :] = state
        state = decay * state + parts[4 * b : 4 * b + 2, :]
    state = jnp.zeros((2, 128), F32)
    for b in range(63, -1, -1):
        out[4 * b + 2 : 4 * b + 4, :] = state
        state = decay * state + parts[4 * b + 2 : 4 * b + 4, :]


def fore_kernel(ys, factor, coef, carries, filt, gated_t, final, scr):
    for n in range(2):
        final[pl.ds(n, 64, stride=2), :] = carries[pl.ds(n, 64, stride=4), :]
    state = tuple(final[8 * m : 8 * m + 8, :] for m in range(M))

    def step(b, state):
        for u in range(4):
            at = b * 32 + u * 8
            mixed = row(ys, ROWS + at) * row(ys, 2 * ROWS + at)
            state = tuple(factor[8 * m : 8 * m + 8, :] * state[m] + mixed for m in range(M))
            value = tree([coef[8 * m : 8 * m + 8, :] * state[m] for m in range(M)])
            put(filt, at, value)
            put(scr, at, value * row(ys, at))
        return state

    state = lax.fori_loop(0, T // 4, step, state)
    for m in range(M):
        final[8 * m : 8 * m + 8, :] = state[m]
    for s in range(8):
        turned = scr[pl.ds(s, T, stride=8), :].T.astype(BF)
        for n in range(8):
            at = 64 * s + 16 * (n // 2)
            gated_t[n % 2, at : at + 16, :] = turned[16 * n : 16 * n + 16, :]


def last_kernel(
    up, gf, filt, ys, xs, halo, final, carries, factor, coef, inverse, norm, taps, oq, ok, ov, sums, gs, res, outgoing
):
    for n in range(2):
        outgoing[pl.ds(n, 64, stride=2), :] = carries[pl.ds(2 + n, 64, stride=4), :]
    sums[37 * 8 :, :] = jnp.zeros((8, 128), F32)
    adj = [outgoing[8 * m : 8 * m + 8, :] for m in range(M)]
    state = [final[8 * m : 8 * m + 8, :] for m in range(M)]
    for n in range(6):
        nup, nq, nk, nv = (halo[i * PAD + 8 * n : i * PAD + 8 * n + 8, :] for i in range(4))
        mixed = nk * nv
        state = [factor[8 * m : 8 * m + 8, :] * state[m] + mixed for m in range(M)]
        value = tree([coef[8 * m : 8 * m + 8, :] * state[m] for m in range(M)])
        mix = tree([coef[8 * m : 8 * m + 8, :] * adj[m] for m in range(M)])
        put(gs, ROWS + 8 * n, nup * value)
        put(gs, XR + ROWS + 8 * n, mix * nv)
        put(gs, 2 * XR + ROWS + 8 * n, mix * nk)
        if n < 5:
            first = nup * nq
            adj = [(adj[m] - first) * inverse[8 * m : 8 * m + 8, :] for m in range(M)]
    for n in range(6, 8):
        for i in range(3):
            put(gs, i * XR + ROWS + 8 * n, jnp.zeros((8, 128), F32))
    half = M // 2
    for part in range(2):
        ms = range(part * half, (part + 1) * half)
        adj = tuple(outgoing[8 * m : 8 * m + 8, :] for m in ms)
        total = (jnp.zeros((8, 128), F32),) * half

        def step(b, carry):
            adj, total = carry
            for u in range(4):
                at = ROWS - 8 - b * 32 - u * 8
                grad = row(gf, at)
                ks, vs = row(ys, ROWS + at), row(ys, 2 * ROWS + at)
                mixed = ks * vs
                adj = tuple(factor[8 * m : 8 * m + 8, :] * a + grad for m, a in zip(ms, adj))
                total = tuple(t + mixed * a for t, a in zip(total, adj))
                mix = tree([coef[8 * m : 8 * m + 8, :] * a for m, a in zip(ms, adj)])
                if part == 0:
                    put(res, at, mix)
                else:
                    mix = mix + row(res, at)
                    put(gs, at, row(up, at) * row(filt, at))
                    put(gs, XR + at, mix * vs)
                    put(gs, 2 * XR + at, mix * ks)
            return adj, total

        adj, total = lax.fori_loop(0, T // 4, step, (adj, total))
        for m, t in zip(ms, total):
            sums[21 * 8 + 8 * m : 21 * 8 + 8 * m + 8, :] = t * norm[8 * m : 8 * m + 8, :]
    for i, out in enumerate((oq, ok, ov)):
        tap = [taps[(i * 7 + j) * 8 : (i * 7 + j) * 8 + 8, :] for j in range(7)]

        def body(b, acc):
            at = i * XR + b * 64
            win = [row(gs, at + 8 * d) for d in range(14)]
            field = [row(xs, at + PAD + 8 * d) for d in range(-6, 8)]
            acc = list(acc)
            for t in range(8):
                value = tap[0] * win[t]
                for j in range(1, 7):
                    value = value + tap[j] * win[t + j]
                put(res, b * 64 + 8 * t, value)
                for j in range(7):
                    acc[j] = acc[j] + win[t] * field[t + 6 - j]
            return tuple(acc)

        acc = lax.fori_loop(0, T // 8, body, (jnp.zeros((8, 128), F32),) * 7)
        for j in range(7):
            sums[(i * 7 + j) * 8 : (i * 7 + j) * 8 + 8, :] = acc[j]
        for g in range(T // 16):
            for s in range(8):
                val = res[pl.ds(128 * g + s, 16, stride=8), :]
                out[16 * g : 16 * g + 16, 128 * s : 128 * s + 128] = val.astype(BF)


def join_kernel(own, one, two, three, part, other_part, out):
    width = own.shape[1]
    for d in range(16):
        at = slice(16 * d, 16 * d + 16)
        value = own[at, :] + one[at, :].astype(F32) + two[at, :].astype(F32) + three[at, :].astype(F32)
        out[at, 0:width] = value.astype(BF)
        here = slice(16 * d, min(16 * d + 16, HALF))
        rows = max(0, here.stop - here.start)
        sums = jnp.zeros((16, 128), F32)
        if rows > 0:
            sums = part[here, :] + other_part[here, :]
        if 0 < rows < 16:
            sums = jnp.concatenate([sums, jnp.zeros((16 - rows, 128), F32)], axis=0)
        high = sums.astype(BF)
        out[at, width : width + 128] = high
        out[at, width + 128 : width + 256] = (sums - high.astype(F32)).astype(BF)


def sds(*shape, dtype=F32):
    return jax.ShapeDtypeStruct(shape, dtype)


def shifted(value, steps):
    n = 64
    first, last = max(0, -steps), min(n, n - steps)
    return lax.ppermute(value, CTX, [(i, i + steps) for i in range(first, last)])


def swapped(value, axis):
    return lax.ppermute(value, axis, [(0, 1), (1, 0)])


def along_y(value, steps):
    pairs = []
    for y in range(4):
        to = (y + steps) % 4
        pairs.append((y % 2 * 2 + y // 2, to % 2 * 2 + to // 2))
    return lax.ppermute(value, ("yl", "yh"), pairs)


def turned_dot(rows, tokens):
    return lax.dot_general(rows, tokens, (((1,), (1,)), ((), ())), preferred_element_type=F32)


def rounded_dot(rows, columns):
    return jnp.dot(rows, columns, preferred_element_type=F32).astype(BF)


def shards(query_proj, key_proj, value_proj, grad_out, out_weight, short_taps, residues, decay_rate):
    q, k, v, go = query_proj[0], key_proj[0], value_proj[0], grad_out[0]
    core, yl, yh = lax.axis_index("core"), lax.axis_index("yl"), lax.axis_index("yh")
    tail = jnp.stack([q[T - 8 :], k[T - 8 :], v[T - 8 :]])
    behind = shifted(tail, 1).astype(F32).reshape(3 * PAD, 128)

    rate = decay_rate.T.reshape(M * 8, 128)
    factor = jnp.exp(-rate)
    norm = jnp.sqrt(-jnp.expm1(-2.0 * rate))
    coef = residues.T.reshape(M * 8, 128) * norm
    taps = jnp.transpose(short_taps, (0, 2, 1)).reshape(21 * 8, 128)
    place = lax.axis_index(CTX)
    span = jnp.exp(-T * lax.dynamic_slice(rate, (2 * place, 0), (2, 128)))

    xs, ys, ends = call(
        shape_kernel, [sds(3 * XR, 128), sds(3 * ROWS, 128), sds(M * 8, 128)], (q, k, v, behind, taps, factor)
    )
    near = lax.all_to_all(jnp.broadcast_to(out_weight[:, :WA], (16, 16, WA)), XZ, 0, 0)
    late = out_weight[:, WA:]
    late = jnp.stack([late, swapped(late, "yl")])
    near, ends = lax.optimization_barrier((near, ends))
    far_low, far_high = along_y(near[:8], 1), along_y(near[8:], -1)
    late = lax.all_to_all(jnp.broadcast_to(late, (16, 2, 16, D - WA)), XZ, 0, 0).reshape(512, D - WA)
    go_theirs = swapped(go, "core")
    go_both = jnp.concatenate([go, go_theirs], axis=0)

    early, rest = go_both[:, :WA], go_both[:, WA:]
    product = [turned_dot(part.reshape(-1, WA), early) for part in (near, far_low, far_high)]
    last = turned_dot(late, rest).reshape(16, 2, 16, 2 * T)
    up_both = jnp.concatenate(product, axis=0) + jnp.swapaxes(last, 0, 1).reshape(512, 2 * T)
    up_mine, up_theirs = up_both[:, :T], swapped(up_both[:, T:], "core")
    up, gf, packed = pl.pallas_call(
        back_kernel,
        out_shape=[sds(ROWS, 128), sds(ROWS, 128), sds(256, 128)],
        in_specs=[pl.BlockSpec(memory_space=pltpu.SMEM)] + [VMEM] * 5,
        out_specs=[VMEM] * 3,
        scratch_shapes=[pltpu.VMEM((M * 8, 128), F32)],
        compiler_params=pltpu.CompilerParams(vmem_limit_bytes=16 * 1024 * 1024),
        cost_estimate=pl.CostEstimate(flops=10_000_000, bytes_accessed=4_000_000, transcendentals=0),
    )(jnp.stack([core, yl]), up_mine, up_theirs, ys, ends, factor)
    head = jnp.concatenate([up[:PAD], ys[:PAD], ys[ROWS : ROWS + PAD], ys[2 * ROWS : 2 * ROWS + PAD]], axis=0)
    ahead = shifted(head, -1)
    blocks = lax.all_to_all(packed.reshape(64, 4, 128), CTX, 0, 0).reshape(256, 128)
    blocks, ahead = lax.optimization_barrier((blocks, ahead))
    (scanned,) = call(scan_kernel, [sds(256, 128)], (blocks, span))
    carries = lax.all_to_all(scanned.reshape(64, 4, 128), CTX, 0, 0).reshape(256, 128)
    filt, gated_t, final = call(
        fore_kernel,
        [sds(ROWS, 128), sds(2, 512, T, dtype=BF), sds(M * 8, 128)],
        (ys, factor, coef, carries),
        [pltpu.VMEM((ROWS, 128), F32)],
    )
    gated_theirs = swapped(lax.dynamic_index_in_dim(gated_t, 1 - core, 0, keepdims=False), "core")
    gated_mine = lax.dynamic_index_in_dim(gated_t, core, 0, keepdims=False)
    gated = jnp.concatenate([gated_mine, gated_theirs], axis=1).reshape(2, 256, 2 * T)
    ours = lax.dynamic_index_in_dim(gated, yl, 0, keepdims=False)
    others = lax.dynamic_index_in_dim(gated, 1 - yl, 0, keepdims=False)
    part_a = GA // 2
    here = lax.dynamic_slice(go_both, (0, part_a * yh), (2 * T, part_a))
    there = lax.dynamic_slice(go_both, (0, part_a * (1 - yh)), (2 * T, part_a))
    parts = [rounded_dot(ours, there), rounded_dot(others, here), rounded_dot(others, there)]
    *parts, gated = lax.optimization_barrier((*parts, gated))
    got = [
        lax.ppermute(parts[0], ("yl", "yh"), [(0, 1), (1, 0), (2, 3), (3, 2)]),
        lax.ppermute(parts[1], ("yl", "yh"), [(0, 2), (2, 0), (1, 3), (3, 1)]),
        lax.ppermute(parts[2], ("yl", "yh"), [(0, 3), (3, 0), (1, 2), (2, 1)]),
    ]
    spread = rounded_dot(jnp.swapaxes(gated.reshape(2, 16, 16, 2 * T), 0, 1).reshape(512, 2 * T), go_both[:, GA:])
    spread = lax.all_to_all(spread.reshape(16, 2, 16, D - GA), XZ, 0, 0)
    first = jnp.dot(ours, here, preferred_element_type=F32)
    up, *got = lax.optimization_barrier((up, *got))
    oq, ok, ov, sums = call(
        last_kernel,
        [sds(T, C, dtype=BF)] * 3 + [sds(304, 128)],
        (up, gf, filt, ys, xs, ahead, final, carries, factor, coef, jnp.exp(rate), norm, taps),
        [pltpu.VMEM((3 * XR, 128), F32), pltpu.VMEM((ROWS, 128), F32), pltpu.VMEM((M * 8, 128), F32)],
    )
    halves = sums.reshape(2, HALF, 128)
    part = lax.dynamic_index_in_dim(halves, core, 0, keepdims=False)
    other_part = swapped(lax.dynamic_index_in_dim(halves, 1 - core, 0, keepdims=False), "core")
    (joined,) = call(join_kernel, [sds(256, part_a + 256, dtype=BF)], (first, *got, part, other_part))
    joined, spread = lax.optimization_barrier((joined, spread))
    joined = lax.all_to_all(joined.reshape(16, 16, part_a + 256), XZ, 0, 0)
    spread = jnp.sum(spread.astype(F32), axis=0).astype(BF)
    near = lax.dynamic_index_in_dim(spread, yl, 0, keepdims=False)
    far = lax.dynamic_index_in_dim(spread, 1 - yl, 0, keepdims=False)
    levels = [
        swapped(near, "yh"),
        lax.ppermute(far, ("yl", "yh"), [(0, 2), (2, 0), (1, 3), (3, 1)]),
        lax.ppermute(far, ("yl", "yh"), [(0, 3), (3, 0), (1, 2), (2, 1)]),
    ]
    joined, *levels = lax.optimization_barrier((joined, *levels))
    joined = jnp.sum(joined.astype(F32), axis=0)
    first = joined[:, :part_a]
    first_other = swapped(first, "yh")
    part = joined[:, part_a : part_a + 128] + joined[:, part_a + 128 :]
    part = lax.all_to_all(jnp.broadcast_to(part, (64, 16, 128)), ("yl", "yh", "x", "z"), 0, 0)
    part = jnp.sum(part.reshape(4, 256, 128)[:, :HALF], axis=0)
    rest = swapped(part, "core")
    level = (near.astype(F32) + levels[0].astype(F32)) + (levels[1].astype(F32) + levels[2].astype(F32))
    weight_grad = jnp.concatenate(
        [jnp.where(yh == 0, first, first_other), jnp.where(yh == 0, first_other, first), level], axis=1
    )
    sums = jnp.where(core == 0, jnp.concatenate([part, rest], axis=0), jnp.concatenate([rest, part], axis=0))
    taps_grad = jnp.transpose(sums[: 21 * 8].reshape(3, 7, C), (0, 2, 1))
    residue_grad = sums[21 * 8 : 37 * 8].reshape(M, C).T
    return (oq[None], ok[None], ov[None], weight_grad, taps_grad, residue_grad)


def solution(mesh):
    grid = Mesh(mesh.devices.reshape(2, 4, 4, 2, 2), ("yl", "x", "z", "core", "yh"))
    stream = P("yh", CTX, None)
    return jax.shard_map(
        shards,
        mesh=grid,
        in_specs=(stream, stream, stream, stream, P(CTX, None), P(), P(), P()),
        out_specs=(stream, stream, stream, P(CTX, None), P(), P()),
        check_vma=False,
    )
```

time: 280 us -> 206 us (0.74)
  blocking collectives: 192 us -> 0 us
  waiting for transfers between devices: 7 us -> 74.3 us
  starting transfers between devices: 23 us -> 67.1 us
  other arithmetic: 19.8 us -> 8.62 us
  local copies, waits for them, and re-layouts: 15 us -> 24.7 us
  matrix products: 11.5 us -> 15.3 us
    all_gather x12 -> x0, blocking collectives: 192 us -> none  [the longest x8 147 us: carried(): parts = lax.all_gather(ends, axis)]
    all_to_all x2 -> x7, waiting for transfers between devices: 0.01 us -> 46.3 us  [the longest x1 11.9 us: shards(): lax.all_to_all(jnp.broadcast_to(part, (64, 16, 128)), ('yl', 'yh', 'x', '...]
    all_to_all x2 -> x7, starting transfers between devices: 16.9 us -> 44.8 us  [the longest x1 8.15 us: shards(): lax.all_to_all(jnp.broadcast_to(out_weight[:, :WA], (16, 16, WA)), XZ, 0, 0)]
    ppermute x0 -> x7, waiting for transfers between devices: none -> 21.2 us  [the longest x1 11 us: shards(): lax.ppermute(parts[0], ('yl', 'yh'), [(0, 1), (1, 0), (2, 3), (3, 2)])]
    ppermute x0 -> x7, starting transfers between devices: none -> 11.5 us  [the longest x2 4.81 us: along_y(): return lax.ppermute(value, ('yl', 'yh'), pairs)]
    select_n x1 -> x2, other arithmetic: 8.47 us -> 0.03 us  [the longest x1 0.02 us: shards(): jnp.where(yh == 0, first, first_other)]
    unnamed x42 -> x64, local copies, waits for them, and re-layouts: 8.06 us -> 14.8 us
    ppermute x3 -> x8, starting transfers between devices: 3.42 us -> 8.1 us  [swapped(): return lax.ppermute(value, axis, [(0, 1), (1, 0)])]
  transfers between devices with their start and end apart: 7 -> 24, of which waited for: 1 -> 15; matrix products, arithmetic and copies ran while one was open for 12% -> 10% of each run, Pallas kernels for 4% -> 4%
where the time goes in v2:
time: 206 us; the launch traced here: 203 us
  waiting for transfers between devices  74.3 us (36%)
  starting transfers between devices  67.1 us (33%)
  local copies, waits for them, and re-layouts  24.7 us (12%)
  matrix products  15.3 us (7%)
  Pallas kernels  12.2 us (6%)
  other arithmetic  8.62 us (4%)
    unnamed x64, local copies, waits for them, and re-layouts  14.8 us
    all_to_all x1, waiting for transfers between devices, shards(): lax.all_to_all(jnp.broadcast_to(part, (64, 16, 128)), ('yl', 'yh', 'x', '...  11.9 us
    ppermute x1, waiting for transfers between devices, shards(): lax.ppermute(parts[0], ('yl', 'yh'), [(0, 1), (1, 0), (2, 3), (3, 2)])  11 us
    pallas_call x5, Pallas kernels, call(): pl.pallas_call(body, out_shape=outs, in_specs=[VMEM] * len(ins), out_spec...  10.8 us
    all_to_all x1, waiting for transfers between devices, shards(): lax.all_to_all(jnp.broadcast_to(late, (16, 2, 16, D - WA)), XZ, 0, 0)  8.56 us
    all_to_all x1, waiting for transfers between devices, shards(): lax.all_to_all(scanned.reshape(64, 4, 128), CTX, 0, 0).reshape(256, 128)  8.43 us
    dot_general x4, matrix products, turned_dot(): lax.dot_general(rows, tokens, (((1,), (1,)), ((), ())), preferred_element...  8.22 us
    all_to_all x1, starting transfers between devices, shards(): lax.all_to_all(jnp.broadcast_to(out_weight[:, :WA], (16, 16, WA)), XZ, 0, 0)  8.15 us
  transfers between devices with their start and end apart: 24, of which 15 were waited for; matrix products, arithmetic and copies ran while one was open for 10% of the time, Pallas kernels for 4%

profile of v2, /device:TPU:0, one launch (start us, length us, event | category | flops | bytes accessed | tf_op | source)
XLA Modules:
  0.0 203.4 jit_solution(14230158168646237671)
XLA Ops:
  2.8 8.1 %all-to-all-start = ((bf16[16,16,2688]{2,1,0:T(8,128)(2,1)}), bf16[16,16,2688]{2,1,0:T(8,128)(2,1)}, u32[]{:S(2)}, u32[]{:S(2)}) async-start(bf16[16,16,2688]{2,1,0:T(8,128)(2,1)} %broadcast_in_dim.18), calls=%async_computation | async-start | bytes 2752512 | tf_op jit(solution)/shard_map/all_to_all | solution.py:296
  12.4 2.5 %collective-permute-start.1 = (bf16[128,4096]{1,0:T(8,128)(2,1)}, bf16[128,4096]{1,0:T(8,128)(2,1)}, u32[]{:S(2)}, u32[]{:S(2)}) collective-permute-start(bf16[128,4096]{1,0:T(8,128)(2,1)} %bitcast.8), channel_id=1, source_target_pairs={{0,2},{2,0},{1,3},{3,1},{4,6},{6,4},{5,7},{7,5},{8,10},{10,8},{9,1... | collective-permute-start | bytes 3145736 | tf_op jit(solution)/shard_map/ppermute | solution.py:260
  23.3 1.8 shard_map.127
  25.8 6.7 %all-to-all-done = bf16[16,16,2688]{2,1,0:T(8,128)(2,1)} async-done(((bf16[16,16,2688]{2,1,0:T(8,128)(2,1)}), bf16[16,16,2688]{2,1,0:T(8,128)(2,1)}, u32[]{:S(2)}, u32[]{:S(2)}) %all-to-all-start) | async-done | bytes 1376288 | tf_op jit(solution)/shard_map/all_to_all | solution.py:296
  32.5 2.1 %broadcast_in_dim.19 = bf16[16,2,16,1408]{3,2,1,0:T(8,128)(2,1)} broadcast(bf16[2,16,1408]{2,1,0:T(8,128)(2,1)} %pad_maximum_fusion.5), dimensions={1,2,3} | broadcast | bytes 1531904 | tf_op jit(solution)/shard_map/broadcast_in_dim | solution.py:301
  34.6 6.3 %all-to-all-start.1 = ((bf16[16,2,16,1408]{3,2,1,0:T(8,128)(2,1)}), bf16[16,2,16,1408]{3,2,1,0:T(8,128)(2,1)}, u32[]{:S(2)}, u32[]{:S(2)}) async-start(bf16[16,2,16,1408]{3,2,1,0:T(8,128)(2,1)} %broadcast_in_dim.19), calls=%async_computation.1 | async-start | bytes 2883584 | tf_op jit(solution)/shard_map/all_to_all | solution.py:301
  41.0 2.5 %fusion.22 = (bf16[8,16,2688]{2,1,0:T(8,128)(2,1)}, bf16[8,16,2688]{2,1,0:T(8,128)(2,1)}) fusion(bf16[16,16,2688]{2,1,0:T(8,128)(2,1)} %all-to-all-done), kind=kLoop, calls=%fused_computation.59 | loop fusion | bytes 2752512 | tf_op jit(solution)/shard_map/slice | solution.py:300
  43.5 4.7 %collective-permute-start.3 = (bf16[8,16,2688]{2,1,0:T(8,128)(2,1)}, bf16[8,16,2688]{2,1,0:T(8,128)(2,1)}, u32[]{:S(2)}, u32[]{:S(2)}) collective-permute-start(bf16[8,16,2688]{2,1,0:T(8,128)(2,1)} %get-tuple-element.74), channel_id=1, source_target_pairs={{0,65},{64,0},{1,64},{65,1},{2,67},{66,2},{3,66},{67,3},{4,69},{68... | collective-permute-start | bytes 2064392 | tf_op jit(solution)/shard_map/ppermute | solution.py:268
  50.7 2.6 %fusion.24 = f32[256,256]{1,0:T(8,128)} fusion(bf16[256,2688]{1,0:T(8,128)(2,1)} %bitcast.7, bf16[256,2688]{1,0:T(8,128)(2,1)S(1)} %fusion), kind=kOutput, calls=%fused_computation.61 | convolution fusion | flops 352321536 | bytes 3014656 | tf_op jit(solution)/shard_map/dot_general | solution.py:272
  53.3 8.6 %all-to-all-done.1 = bf16[16,2,16,1408]{3,2,1,0:T(8,128)(2,1)} async-done(((bf16[16,2,16,1408]{3,2,1,0:T(8,128)(2,1)}), bf16[16,2,16,1408]{3,2,1,0:T(8,128)(2,1)}, u32[]{:S(2)}, u32[]{:S(2)}) %all-to-all-start.1) | async-done | bytes 1441824 | tf_op jit(solution)/shard_map/all_to_all | solution.py:301
  61.9 2.2 %convolution_bitcast_fusion = f32[2,16,16,256]{3,2,0,1:T(8,128)S(1)} fusion(bf16[16,2,16,1408]{3,2,1,0:T(8,128)(2,1)} %all-to-all-done.1, bf16[128,4096]{1,0:T(8,128)(2,1)} %bitcast.8, bf16[128,4096]{1,0:T(8,128)(2,1)} %collective-permute-done.1), kind=kOutput, calls=%fused_computation.13 | convolution fusion | flops 370540544 | bytes 4063232 | tf_op jit(solution)/shard_map/dot_general | solution.py:272
  65.9 1.7 fusion.25
  75.0 8.1 %all-to-all-start.2 = ((f32[64,4,128]{2,1,0:T(4,128)}), f32[64,4,128]{2,1,0:T(4,128)S(1)}, u32[]{:S(2)}, u32[]{:S(2)}) async-start(f32[64,4,128]{2,1,0:T(4,128)} %bitcast.81), calls=%async_computation.2 | async-start | bytes 262144 | tf_op jit(solution)/shard_map/all_to_all | solution.py:321
  83.8 7.7 %all-to-all-done.2 = f32[64,4,128]{2,1,0:T(4,128)S(1)} async-done(((f32[64,4,128]{2,1,0:T(4,128)}), f32[64,4,128]{2,1,0:T(4,128)S(1)}, u32[]{:S(2)}, u32[]{:S(2)}) %all-to-all-start.2) | async-done | bytes 131104 | tf_op jit(solution)/shard_map/all_to_all | solution.py:321
  92.3 4.6 %all-to-all-start.3 = ((f32[64,4,128]{2,1,0:T(4,128)}), f32[64,4,128]{2,1,0:T(4,128)S(1)}, u32[]{:S(2)}, u32[]{:S(2)}) async-start(f32[64,4,128]{2,1,0:T(4,128)} %bitcast.75), calls=%async_computation.3 | async-start | bytes 262144 | tf_op jit(solution)/shard_map/all_to_all | solution.py:324
  97.0 8.4 %all-to-all-done.3 = f32[64,4,128]{2,1,0:T(4,128)S(1)} async-done(((f32[64,4,128]{2,1,0:T(4,128)}), f32[64,4,128]{2,1,0:T(4,128)S(1)}, u32[]{:S(2)}, u32[]{:S(2)}) %all-to-all-start.3) | async-done | bytes 131104 | tf_op jit(solution)/shard_map/all_to_all | solution.py:324
  112.9 3.5 %convolution_convert_fusion = bf16[512,2304]{1,0:T(8,128)(2,1)} fusion(bf16[512,256]{1,0:T(8,128)(2,1)S(1)} %bitcast.93, bf16[128,4096]{1,0:T(8,128)(2,1)} %collective-permute-done.1, bf16[128,4096]{1,0:T(8,128)(2,1)} %bitcast.8), kind=kOutput, calls=%fused_computation | convolution fusion | flops 607518720 | bytes 4718592 | tf_op jit(solution)/shard_map/dot_general | solution.py:276
  116.4 4.4 %all-to-all-start.4 = ((bf16[16,2,16,2304]{3,2,1,0:T(8,128)(2,1)}), bf16[16,2,16,2304]{3,2,1,0:T(8,128)(2,1)}, u32[]{:S(2)}, u32[]{:S(2)}) async-start(bf16[16,2,16,2304]{3,2,1,0:T(8,128)(2,1)} %bitcast.82), calls=%async_computation.4 | async-start | bytes 4718592 | tf_op jit(solution)/shard_map/all_to_all | solution.py:347
  122.6 2.4 %collective-permute-start.10 = (bf16[256,896]{1,0:T(8,128)(2,1)}, bf16[256,896]{1,0:T(8,128)(2,1)S(1)}, u32[]{:S(2)}, u32[]{:S(2)}) collective-permute-start(bf16[256,896]{1,0:T(8,128)(2,1)} %convolution_convert_fusion.1), channel_id=1, source_target_pairs={{0,65},{65,0},{1,64},{64,1},{2,67},{67,2},{3,66},{66,3},{4,69},{69... | collective-permute-start | bytes 1376264 | tf_op jit(solution)/shard_map/ppermute | solution.py:344
  125.0 11.0 %collective-permute-done.8.one = bf16[256,896]{1,0:T(8,128)(2,1)S(1)} collective-permute-done((bf16[256,896]{1,0:T(8,128)(2,1)}, bf16[256,896]{1,0:T(8,128)(2,1)S(1)}, u32[]{:S(2)}, u32[]{:S(2)}) %collective-permute-start.8) | collective-permute-done | bytes 458784 | tf_op jit(solution)/shard_map/ppermute | solution.py:342
  136.0 7.5 %collective-permute-done.9.two = bf16[256,896]{1,0:T(8,128)(2,1)S(1)} collective-permute-done((bf16[256,896]{1,0:T(8,128)(2,1)}, bf16[256,896]{1,0:T(8,128)(2,1)S(1)}, u32[]{:S(2)}, u32[]{:S(2)}) %collective-permute-start.9) | collective-permute-done | bytes 458784 | tf_op jit(solution)/shard_map/ppermute | solution.py:343
  143.5 1.7 collective-permute-done.10.three
  151.7 6.1 %shard_map.131 = (bf16[128,1024]{1,0:T(8,128)(2,1)}, bf16[128,1024]{1,0:T(8,128)(2,1)}, bf16[128,1024]{1,0:T(8,128)(2,1)}, f32[304,128]{1,0:T(8,128)S(1)}) custom-call(f32[1024,128]{1,0:T(8,128)S(1)} %copy-done.1, f32[1024,128]{1,0:T(8,128)S(1)} %copy-done.5, f32[1024,128]{1,0:T(8,128)S(1)} %copy-done.7, f32[3072,128]{1,0:T(8,128)S(1)} %get-tuple-element.39.ys, ...), custom_call_target="tpu_custom_call" | custom-call | flops 10000000 | bytes 4000000 | tf_op jit(solution)/shard_map/pallas_call | solution.py:28
  160.4 6.7 %all-to-all-start.5 = ((bf16[16,16,1152]{2,1,0:T(8,128)(2,1)}), bf16[16,16,1152]{2,1,0:T(8,128)(2,1)S(1)}, u32[]{:S(2)}, u32[]{:S(2)}) async-start(bf16[16,16,1152]{2,1,0:T(8,128)(2,1)} %bitcast.37), calls=%async_computation.5 | async-start | bytes 1179648 | tf_op jit(solution)/shard_map/all_to_all | solution.py:361
  167.1 2.0 reduce_sum.30
  169.2 1.7 collective-permute-start.12
  171.0 2.3 %collective-permute-start.14 = (bf16[16,2304]{1,0:T(8,128)(2,1)S(1)}, bf16[16,2304]{1,0:T(8,128)(2,1)S(1)}, u32[]{:S(2)}, u32[]{:S(2)}) collective-permute-start(bf16[16,2304]{1,0:T(8,128)(2,1)S(1)} %get-tuple-element.81), channel_id=1, source_target_pairs={{0,65},{65,0},{1,64},{64,1},{2,67},{67,2},{3,66},{66,3},{4,69},{69... | collective-permute-start | bytes 221192 | tf_op jit(solution)/shard_map/ppermute | solution.py:368
  173.3 2.3 %collective-permute-done.12 = bf16[16,2304]{1,0:T(8,128)(2,1)S(1)} collective-permute-done((bf16[16,2304]{1,0:T(8,128)(2,1)S(1)}, bf16[16,2304]{1,0:T(8,128)(2,1)S(1)}, u32[]{:S(2)}, u32[]{:S(2)}) %collective-permute-start.12) | collective-permute-done | bytes 73760 | tf_op jit(solution)/shard_map/ppermute | solution.py:260
  176.7 3.0 %all-to-all-done.5 = bf16[16,16,1152]{2,1,0:T(8,128)(2,1)S(1)} async-done(((bf16[16,16,1152]{2,1,0:T(8,128)(2,1)}), bf16[16,16,1152]{2,1,0:T(8,128)(2,1)S(1)}, u32[]{:S(2)}, u32[]{:S(2)}) %all-to-all-start.5) | async-done | bytes 589856 | tf_op jit(solution)/shard_map/all_to_all | solution.py:361
  179.7 1.7 collective-permute-start.15
  182.3 6.4 %all-to-all-start.6 = ((f32[64,16,128]{2,1,0:T(8,128)}), f32[64,16,128]{2,1,0:T(8,128)S(1)}, u32[]{:S(2)}, u32[]{:S(2)}) async-start(f32[64,16,128]{2,1,0:T(8,128)} %broadcast_in_dim.23), calls=%async_computation.6 | async-start | bytes 1048576 | tf_op jit(solution)/shard_map/all_to_all | solution.py:375
  188.9 11.9 %all-to-all-done.6 = f32[64,16,128]{2,1,0:T(8,128)S(1)} async-done(((f32[64,16,128]{2,1,0:T(8,128)}), f32[64,16,128]{2,1,0:T(8,128)S(1)}, u32[]{:S(2)}, u32[]{:S(2)}) %all-to-all-start.6) | async-done | bytes 524320 | tf_op jit(solution)/shard_map/all_to_all | solution.py:375
  (142 shorter events, 48.5 us)
Async XLA Ops:
  2.7 8.2 %slice-start = ((bf16[1,128,1024]{2,1,0:T(8,128)(2,1)}), bf16[1,8,1024]{2,1,0:T(8,128)(2,1)S(1)}, s32[]{:S(2)}) async-start(bf16[1,128,1024]{2,1,0:T(8,128)(2,1)} %param.8), calls=%async_computation.7 | async-start | bytes 32768 | tf_op jit(solution)/shard_map/slice | solution.py:282
  2.7 8.2 %slice-start.1 = ((bf16[1,128,1024]{2,1,0:T(8,128)(2,1)}), bf16[1,8,1024]{2,1,0:T(8,128)(2,1)S(1)}, s32[]{:S(2)}) async-start(bf16[1,128,1024]{2,1,0:T(8,128)(2,1)} %param.9), calls=%async_computation.8 | async-start | bytes 32768 | tf_op jit(solution)/shard_map/slice | solution.py:282
  2.7 8.2 %slice-start.2 = ((bf16[1,128,1024]{2,1,0:T(8,128)(2,1)}), bf16[1,8,1024]{2,1,0:T(8,128)(2,1)S(1)}, s32[]{:S(2)}) async-start(bf16[1,128,1024]{2,1,0:T(8,128)(2,1)} %param.10), calls=%async_computation.9 | async-start | bytes 32768 | tf_op jit(solution)/shard_map/slice | solution.py:282
  2.7 14.6 %copy-start.30 = (f32[1024,16]{0,1:T(8,128)S(1)}, f32[1024,16]{0,1:T(8,128)}, u32[]{:S(2)}) copy-start(f32[1024,16]{0,1:T(8,128)} %param.15) | copy-start | bytes 196612
  2.7 14.6 %copy-start.31 = (f32[1024,16]{0,1:T(8,128)S(1)}, f32[1024,16]{0,1:T(8,128)}, u32[]{:S(2)}) copy-start(f32[1024,16]{0,1:T(8,128)} %param.14) | copy-start | bytes 196612
  2.7 15.4 %copy-start.29 = (f32[3,1024,7]{1,2,0:T(8,128)S(1)}, f32[3,1024,7]{1,2,0:T(8,128)}, u32[]{:S(2)}) copy-start(f32[3,1024,7]{1,2,0:T(8,128)} %param.13) | copy-start | bytes 258052
  2.8 29.8 %all-to-all-start = ((bf16[16,16,2688]{2,1,0:T(8,128)(2,1)}), bf16[16,16,2688]{2,1,0:T(8,128)(2,1)}, u32[]{:S(2)}, u32[]{:S(2)}) async-start(bf16[16,16,2688]{2,1,0:T(8,128)(2,1)} %broadcast_in_dim.18), calls=%async_computation | async-start | bytes 2752512 | tf_op jit(solution)/shard_map/all_to_all | solution.py:296
  11.0 9.5 %collective-permute-start = (bf16[3,8,1024]{2,1,0:T(8,128)(2,1)S(1)}, bf16[3,8,1024]{2,1,0:T(8,128)(2,1)S(1)}, u32[]{:S(2)}, u32[]{:S(2)}) collective-permute-start(bf16[3,8,1024]{2,1,0:T(8,128)(2,1)S(1)} %pad_maximum_fusion.6), channel_id=1, source_target_pairs={{0,2},{2,4},{4,6},{6,8},{8,10},{10,12},{12,14},{14,16},{16,18},{18... | collective-permute-start | bytes 147464 | tf_op jit(solution)/shard_map/ppermute | solution.py:256
  12.4 35.8 %collective-permute-start.1 = (bf16[128,4096]{1,0:T(8,128)(2,1)}, bf16[128,4096]{1,0:T(8,128)(2,1)}, u32[]{:S(2)}, u32[]{:S(2)}) collective-permute-start(bf16[128,4096]{1,0:T(8,128)(2,1)} %bitcast.8), channel_id=1, source_target_pairs={{0,2},{2,0},{1,3},{3,1},{4,6},{6,4},{5,7},{7,5},{8,10},{10,8},{9,1... | collective-permute-start | bytes 3145736 | tf_op jit(solution)/shard_map/ppermute | solution.py:260
  15.7 4.0 %collective-permute-start.4 = (bf16[16,1408]{1,0:T(8,128)(2,1)S(1)}, bf16[16,1408]{1,0:T(8,128)(2,1)S(1)}, u32[]{:S(2)}, u32[]{:S(2)}) collective-permute-start(bf16[16,1408]{1,0:T(8,128)(2,1)S(1)} %get-tuple-element.86), channel_id=1, source_target_pairs={{0,64},{64,0},{1,65},{65,1},{2,66},{66,2},{3,67},{67,3},{4,68},{68... | collective-permute-start | bytes 135176 | tf_op jit(solution)/shard_map/ppermute | solution.py:260
  34.6 27.2 %all-to-all-start.1 = ((bf16[16,2,16,1408]{3,2,1,0:T(8,128)(2,1)}), bf16[16,2,16,1408]{3,2,1,0:T(8,128)(2,1)}, u32[]{:S(2)}, u32[]{:S(2)}) async-start(bf16[16,2,16,1408]{3,2,1,0:T(8,128)(2,1)} %broadcast_in_dim.19), calls=%async_computation.1 | async-start | bytes 2883584 | tf_op jit(solution)/shard_map/all_to_all | solution.py:301
  43.5 20.7 %collective-permute-start.3 = (bf16[8,16,2688]{2,1,0:T(8,128)(2,1)}, bf16[8,16,2688]{2,1,0:T(8,128)(2,1)}, u32[]{:S(2)}, u32[]{:S(2)}) collective-permute-start(bf16[8,16,2688]{2,1,0:T(8,128)(2,1)} %get-tuple-element.74), channel_id=1, source_target_pairs={{0,65},{64,0},{1,64},{65,1},{2,67},{66,2},{3,66},{67,3},{4,69},{68... | collective-permute-start | bytes 2064392 | tf_op jit(solution)/shard_map/ppermute | solution.py:268
  49.7 16.2 %collective-permute-start.2 = (bf16[8,16,2688]{2,1,0:T(8,128)(2,1)}, bf16[8,16,2688]{2,1,0:T(8,128)(2,1)}, u32[]{:S(2)}, u32[]{:S(2)}) collective-permute-start(bf16[8,16,2688]{2,1,0:T(8,128)(2,1)} %get-tuple-element.73), channel_id=1, source_target_pairs={{0,64},{64,1},{1,65},{65,0},{2,66},{66,3},{3,67},{67,2},{4,68},{68... | collective-permute-start | bytes 2064392 | tf_op jit(solution)/shard_map/ppermute | solution.py:268
  67.8 1.6 collective-permute-start.5
  73.7 17.8 %collective-permute-start.6 = (f32[256,128]{1,0:T(8,128)}, f32[256,128]{1,0:T(8,128)}, u32[]{:S(2)}, u32[]{:S(2)}) collective-permute-start(f32[256,128]{1,0:T(8,128)} %pad_maximum_fusion.4), channel_id=1, source_target_pairs={{2,0},{4,2},{6,4},{8,6},{10,8},{12,10},{14,12},{16,14},{18,16},{20... | collective-permute-start | bytes 393224 | tf_op jit(solution)/shard_map/ppermute | solution.py:256
  75.0 16.5 %all-to-all-start.2 = ((f32[64,4,128]{2,1,0:T(4,128)}), f32[64,4,128]{2,1,0:T(4,128)S(1)}, u32[]{:S(2)}, u32[]{:S(2)}) async-start(f32[64,4,128]{2,1,0:T(4,128)} %bitcast.81), calls=%async_computation.2 | async-start | bytes 262144 | tf_op jit(solution)/shard_map/all_to_all | solution.py:321
  92.3 13.1 %all-to-all-start.3 = ((f32[64,4,128]{2,1,0:T(4,128)}), f32[64,4,128]{2,1,0:T(4,128)S(1)}, u32[]{:S(2)}, u32[]{:S(2)}) async-start(f32[64,4,128]{2,1,0:T(4,128)} %bitcast.75), calls=%async_computation.3 | async-start | bytes 262144 | tf_op jit(solution)/shard_map/all_to_all | solution.py:324
  107.9 1.6 collective-permute-start.7
  116.4 44.0 %all-to-all-start.4 = ((bf16[16,2,16,2304]{3,2,1,0:T(8,128)(2,1)}), bf16[16,2,16,2304]{3,2,1,0:T(8,128)(2,1)}, u32[]{:S(2)}, u32[]{:S(2)}) async-start(bf16[16,2,16,2304]{3,2,1,0:T(8,128)(2,1)} %bitcast.82), calls=%async_computation.4 | async-start | bytes 4718592 | tf_op jit(solution)/shard_map/all_to_all | solution.py:347
  120.8 15.2 %collective-permute-start.8 = (bf16[256,896]{1,0:T(8,128)(2,1)}, bf16[256,896]{1,0:T(8,128)(2,1)S(1)}, u32[]{:S(2)}, u32[]{:S(2)}) collective-permute-start(bf16[256,896]{1,0:T(8,128)(2,1)} %convolution_convert_fusion.3), channel_id=1, source_target_pairs={{0,1},{1,0},{64,65},{65,64},{2,3},{3,2},{66,67},{67,66},{4,5},{5,4... | collective-permute-start | bytes 1376264 | tf_op jit(solution)/shard_map/ppermute | solution.py:342
  122.3 21.3 %collective-permute-start.9 = (bf16[256,896]{1,0:T(8,128)(2,1)}, bf16[256,896]{1,0:T(8,128)(2,1)S(1)}, u32[]{:S(2)}, u32[]{:S(2)}) collective-permute-start(bf16[256,896]{1,0:T(8,128)(2,1)} %convolution_convert_fusion.2), channel_id=1, source_target_pairs={{0,64},{64,0},{1,65},{65,1},{2,66},{66,2},{3,67},{67,3},{4,68},{68... | collective-permute-start | bytes 1376264 | tf_op jit(solution)/shard_map/ppermute | solution.py:343
  122.6 22.6 %collective-permute-start.10 = (bf16[256,896]{1,0:T(8,128)(2,1)}, bf16[256,896]{1,0:T(8,128)(2,1)S(1)}, u32[]{:S(2)}, u32[]{:S(2)}) collective-permute-start(bf16[256,896]{1,0:T(8,128)(2,1)} %convolution_convert_fusion.1), channel_id=1, source_target_pairs={{0,65},{65,0},{1,64},{64,1},{2,67},{67,2},{3,66},{66,3},{4,69},{69... | collective-permute-start | bytes 1376264 | tf_op jit(solution)/shard_map/ppermute | solution.py:344
  151.7 6.4 %copy-start.24 = (bf16[256,896]{1,0:T(8,128)(2,1)S(1)}, bf16[256,896]{1,0:T(8,128)(2,1)}, u32[]{:S(2)}) copy-start(bf16[256,896]{1,0:T(8,128)(2,1)} %copy-done.23) | copy-start | bytes 1376260
  151.7 6.4 %copy-start.26 = (bf16[512,128]{1,0:T(8,128)(2,1)S(1)}, bf16[512,128]{1,0:T(8,128)(2,1)}, u32[]{:S(2)}) copy-start(bf16[512,128]{1,0:T(8,128)(2,1)} %copy-done.25) | copy-start | bytes 393220
  157.9 1.3 collective-permute-start.11
  160.4 19.3 %all-to-all-start.5 = ((bf16[16,16,1152]{2,1,0:T(8,128)(2,1)}), bf16[16,16,1152]{2,1,0:T(8,128)(2,1)S(1)}, u32[]{:S(2)}, u32[]{:S(2)}) async-start(bf16[16,16,1152]{2,1,0:T(8,128)(2,1)} %bitcast.37), calls=%async_computation.5 | async-start | bytes 1179648 | tf_op jit(solution)/shard_map/all_to_all | solution.py:361
  169.2 6.5 %collective-permute-start.12 = (bf16[16,2304]{1,0:T(8,128)(2,1)S(1)}, bf16[16,2304]{1,0:T(8,128)(2,1)S(1)}, u32[]{:S(2)}, u32[]{:S(2)}) collective-permute-start(bf16[16,2304]{1,0:T(8,128)(2,1)S(1)} %get-tuple-element.82), channel_id=1, source_target_pairs={{0,1},{1,0},{2,3},{3,2},{4,5},{5,4},{6,7},{7,6},{8,9},{9,8},{10,11... | collective-permute-start | bytes 221192 | tf_op jit(solution)/shard_map/ppermute | solution.py:260
  170.9 4.8 %collective-permute-start.13 = (bf16[16,2304]{1,0:T(8,128)(2,1)S(1)}, bf16[16,2304]{1,0:T(8,128)(2,1)S(1)}, u32[]{:S(2)}, u32[]{:S(2)}) collective-permute-start(bf16[16,2304]{1,0:T(8,128)(2,1)S(1)} %get-tuple-element.81), channel_id=1, source_target_pairs={{0,64},{64,0},{1,65},{65,1},{2,66},{66,2},{3,67},{67,3},{4,68},{68... | collective-permute-start | bytes 221192 | tf_op jit(solution)/shard_map/ppermute | solution.py:367
  171.0 5.6 %collective-permute-start.14 = (bf16[16,2304]{1,0:T(8,128)(2,1)S(1)}, bf16[16,2304]{1,0:T(8,128)(2,1)S(1)}, u32[]{:S(2)}, u32[]{:S(2)}) collective-permute-start(bf16[16,2304]{1,0:T(8,128)(2,1)S(1)} %get-tuple-element.81), channel_id=1, source_target_pairs={{0,65},{65,0},{1,64},{64,1},{2,67},{67,2},{3,66},{66,3},{4,69},{69... | collective-permute-start | bytes 221192 | tf_op jit(solution)/shard_map/ppermute | solution.py:368
  179.7 9.1 %collective-permute-start.15 = (f32[16,896]{1,0:T(8,128)S(1)}, f32[16,896]{1,0:T(8,128)S(1)}, u32[]{:S(2)}, u32[]{:S(2)}) collective-permute-start(f32[16,896]{1,0:T(8,128)S(1)} %slice.97), channel_id=1, source_target_pairs={{0,1},{1,0},{2,3},{3,2},{4,5},{5,4},{6,7},{7,6},{8,9},{9,8},{10,11... | collective-permute-start | bytes 172040 | tf_op jit(solution)/shard_map/ppermute | solution.py:260
  182.3 18.4 %all-to-all-start.6 = ((f32[64,16,128]{2,1,0:T(8,128)}), f32[64,16,128]{2,1,0:T(8,128)S(1)}, u32[]{:S(2)}, u32[]{:S(2)}) async-start(f32[64,16,128]{2,1,0:T(8,128)} %broadcast_in_dim.23), calls=%async_computation.6 | async-start | bytes 1048576 | tf_op jit(solution)/shard_map/all_to_all | solution.py:375
  200.7 1.4 collective-permute-start.16
  (27 other events, 39.3 us)

commit v3 on v2

--- a/solution.py
+++ b/solution.py
@@ -18,6 +18,7 @@
 GRP = ("yl", "x", "z")
 XZ = ("x", "z")
 WA = 2688
+LAST = 7_000_000_000
 HALF = 152
 GA = 1792
 
@@ -86,7 +87,7 @@
     return terms[0]
 
 
-def back_kernel(core, up_mine, up_theirs, ys, ends, factor, up, gf, packed, scr):
+def back_kernel(core, up_mine, up_theirs, ys, ends, factor, up, packed, scr):
     zero = core[0] == 0
     for s in range(8):
         half = jnp.where(core[1] == s // 4, 0, 256)
@@ -102,7 +103,6 @@
         for u in range(8):
             at = ROWS - 8 - b * 64 - u * 8
             grad = row(up, at) * row(ys, at)
-            put(gf, at, grad)
             state = tuple(f * x + grad for f, x in zip(fac, state))
         return state
 
@@ -152,7 +152,7 @@
 
 
 def last_kernel(
-    up, gf, filt, ys, xs, halo, final, carries, factor, coef, inverse, norm, taps, oq, ok, ov, sums, gs, res, outgoing
+    up, filt, ys, xs, halo, final, carries, factor, coef, inverse, norm, taps, oq, ok, ov, sums, gs, res, outgoing
 ):
     for n in range(2):
         outgoing[pl.ds(n, 64, stride=2), :] = carries[pl.ds(2 + n, 64, stride=4), :]
@@ -184,7 +184,7 @@
             adj, total = carry
             for u in range(4):
                 at = ROWS - 8 - b * 32 - u * 8
-                grad = row(gf, at)
+                grad = row(up, at) * row(ys, at)
                 ks, vs = row(ys, ROWS + at), row(ys, 2 * ROWS + at)
                 mixed = ks * vs
                 adj = tuple(factor[8 * m : 8 * m + 8, :] * a + grad for m, a in zip(ms, adj))
@@ -307,11 +307,11 @@
     last = turned_dot(late, rest).reshape(16, 2, 16, 2 * T)
     up_both = jnp.concatenate(product, axis=0) + jnp.swapaxes(last, 0, 1).reshape(512, 2 * T)
     up_mine, up_theirs = up_both[:, :T], swapped(up_both[:, T:], "core")
-    up, gf, packed = pl.pallas_call(
+    up, packed = pl.pallas_call(
         back_kernel,
-        out_shape=[sds(ROWS, 128), sds(ROWS, 128), sds(256, 128)],
+        out_shape=[sds(ROWS, 128), sds(256, 128)],
         in_specs=[pl.BlockSpec(memory_space=pltpu.SMEM)] + [VMEM] * 5,
-        out_specs=[VMEM] * 3,
+        out_specs=[VMEM] * 2,
         scratch_shapes=[pltpu.VMEM((M * 8, 128), F32)],
         compiler_params=pltpu.CompilerParams(vmem_limit_bytes=16 * 1024 * 1024),
         cost_estimate=pl.CostEstimate(flops=10_000_000, bytes_accessed=4_000_000, transcendentals=0),
@@ -337,7 +337,6 @@
     here = lax.dynamic_slice(go_both, (0, part_a * yh), (2 * T, part_a))
     there = lax.dynamic_slice(go_both, (0, part_a * (1 - yh)), (2 * T, part_a))
     parts = [rounded_dot(ours, there), rounded_dot(others, here), rounded_dot(others, there)]
-    *parts, gated = lax.optimization_barrier((*parts, gated))
     got = [
         lax.ppermute(parts[0], ("yl", "yh"), [(0, 1), (1, 0), (2, 3), (3, 2)]),
         lax.ppermute(parts[1], ("yl", "yh"), [(0, 2), (2, 0), (1, 3), (3, 1)]),
@@ -346,12 +345,12 @@
     spread = rounded_dot(jnp.swapaxes(gated.reshape(2, 16, 16, 2 * T), 0, 1).reshape(512, 2 * T), go_both[:, GA:])
     spread = lax.all_to_all(spread.reshape(16, 2, 16, D - GA), XZ, 0, 0)
     first = jnp.dot(ours, here, preferred_element_type=F32)
-    up, *got = lax.optimization_barrier((up, *got))
     oq, ok, ov, sums = call(
         last_kernel,
         [sds(T, C, dtype=BF)] * 3 + [sds(304, 128)],
-        (up, gf, filt, ys, xs, ahead, final, carries, factor, coef, jnp.exp(rate), norm, taps),
+        (up, filt, ys, xs, ahead, final, carries, factor, coef, jnp.exp(rate), norm, taps),
         [pltpu.VMEM((3 * XR, 128), F32), pltpu.VMEM((ROWS, 128), F32), pltpu.VMEM((M * 8, 128), F32)],
+        flops=LAST,
     )
     halves = sums.reshape(2, HALF, 128)
     part = lax.dynamic_index_in_dim(halves, core, 0, keepdims=False)

time: 206 us -> 189 us (0.917)
  local copies, waits for them, and re-layouts: 24.7 us -> 12 us
  waiting for transfers between devices: 74.3 us -> 78.4 us
  matrix products: 15.3 us -> 12.1 us
  other arithmetic: 8.62 us -> 5.99 us
    unnamed x64 -> x24, local copies, waits for them, and re-layouts: 14.8 us -> 2.91 us
    ppermute x1, waiting for transfers between devices: 11 us -> 3.56 us  [shards(): lax.ppermute(parts[0], ('yl', 'yh'), [(0, 1), (1, 0), (2, 3), (3, 2)])]
    all_to_all x1, waiting for transfers between devices: 0.01 us -> 6.83 us  [shards(): spread = lax.all_to_all(spread.reshape(16, 2, 16, D - GA), XZ, 0, 0)]
    all_to_all x1, waiting for transfers between devices: 6.71 us -> 9.4 us  [shards(): lax.all_to_all(jnp.broadcast_to(out_weight[:, :WA], (16, 16, WA)), XZ, 0, 0)]
    dot_general x4, matrix products: 6.77 us -> 4.36 us  [rounded_dot(): return jnp.dot(rows, columns, preferred_element_type=F32).astype(BF)]
  transfers between devices with their start and end apart: 24 -> 24, of which waited for: 15 -> 17; matrix products, arithmetic and copies ran while one was open for 10% -> 10% of each run, Pallas kernels for 4% -> 4%
where the time goes in v3:
time: 189 us; the launch traced here: 187 us
  waiting for transfers between devices  78.4 us (41%)
  starting transfers between devices  65.1 us (34%)
  Pallas kernels  12.5 us (7%)
  matrix products  12.1 us (6%)
  local copies, waits for them, and re-layouts  12 us (6%)
  other arithmetic  5.99 us (3%)
    all_to_all x1, waiting for transfers between devices, shards(): lax.all_to_all(jnp.broadcast_to(part, (64, 16, 128)), ('yl', 'yh', 'x', '...  11.8 us
    pallas_call x5, Pallas kernels, call(): pl.pallas_call(body, out_shape=outs, in_specs=[VMEM] * len(ins), out_spec...  10.4 us
    all_to_all x1, waiting for transfers between devices, shards(): lax.all_to_all(jnp.broadcast_to(out_weight[:, :WA], (16, 16, WA)), XZ, 0, 0)  9.4 us
    all_to_all x1, waiting for transfers between devices, shards(): lax.all_to_all(jnp.broadcast_to(late, (16, 2, 16, D - WA)), XZ, 0, 0)  9.08 us
    all_to_all x1, waiting for transfers between devices, shards(): lax.all_to_all(scanned.reshape(64, 4, 128), CTX, 0, 0).reshape(256, 128)  8.44 us
    all_to_all x1, waiting for transfers between devices, shards(): lax.all_to_all(packed.reshape(64, 4, 128), CTX, 0, 0).reshape(256, 128)  8.41 us
    ppermute x8, waiting for transfers between devices, swapped(): return lax.ppermute(value, axis, [(0, 1), (1, 0)])  8.3 us
    all_to_all x1, starting transfers between devices, shards(): lax.all_to_all(packed.reshape(64, 4, 128), CTX, 0, 0).reshape(256, 128)  8.29 us
  transfers between devices with their start and end apart: 24, of which 17 were waited for; matrix products, arithmetic and copies ran while one was open for 10% of the time, Pallas kernels for 4%

profile of v3, /device:TPU:0, one launch (start us, length us, event | category | flops | bytes accessed | tf_op | source)
XLA Modules:
  0.0 187.3 jit_solution(12028748620747183262)
XLA Ops:
  2.8 8.1 %all-to-all-start = ((bf16[16,16,2688]{2,1,0:T(8,128)(2,1)}), bf16[16,16,2688]{2,1,0:T(8,128)(2,1)}, u32[]{:S(2)}, u32[]{:S(2)}) async-start(bf16[16,16,2688]{2,1,0:T(8,128)(2,1)} %broadcast_in_dim.18), calls=%async_computation | async-start | bytes 2752512 | tf_op jit(solution)/shard_map/all_to_all | solution.py:296
  12.6 2.5 %collective-permute-start.1 = (bf16[128,4096]{1,0:T(8,128)(2,1)}, bf16[128,4096]{1,0:T(8,128)(2,1)}, u32[]{:S(2)}, u32[]{:S(2)}) collective-permute-start(bf16[128,4096]{1,0:T(8,128)(2,1)} %bitcast.8), channel_id=1, source_target_pairs={{0,2},{2,0},{1,3},{3,1},{4,6},{6,4},{5,7},{7,5},{8,10},{10,8},{9,1... | collective-permute-start | bytes 3145736 | tf_op jit(solution)/shard_map/ppermute | solution.py:260
  17.7 2.3 %collective-permute-done.4 = bf16[16,1408]{1,0:T(8,128)(2,1)S(1)} collective-permute-done((bf16[16,1408]{1,0:T(8,128)(2,1)S(1)}, bf16[16,1408]{1,0:T(8,128)(2,1)S(1)}, u32[]{:S(2)}, u32[]{:S(2)}) %collective-permute-start.4) | collective-permute-done | bytes 45088 | tf_op jit(solution)/shard_map/ppermute | solution.py:260
  20.1 1.8 shard_map.127
  23.1 9.4 %all-to-all-done = bf16[16,16,2688]{2,1,0:T(8,128)(2,1)} async-done(((bf16[16,16,2688]{2,1,0:T(8,128)(2,1)}), bf16[16,16,2688]{2,1,0:T(8,128)(2,1)}, u32[]{:S(2)}, u32[]{:S(2)}) %all-to-all-start) | async-done | bytes 1376288 | tf_op jit(solution)/shard_map/all_to_all | solution.py:296
  33.8 4.4 %all-to-all-start.1 = ((bf16[16,2,16,1408]{3,2,1,0:T(8,128)(2,1)}), bf16[16,2,16,1408]{3,2,1,0:T(8,128)(2,1)}, u32[]{:S(2)}, u32[]{:S(2)}) async-start(bf16[16,2,16,1408]{3,2,1,0:T(8,128)(2,1)} %broadcast_in_dim.19), calls=%async_computation.1 | async-start | bytes 2883584 | tf_op jit(solution)/shard_map/all_to_all | solution.py:301
  38.2 2.6 %fusion.22 = (bf16[8,16,2688]{2,1,0:T(8,128)(2,1)}, bf16[8,16,2688]{2,1,0:T(8,128)(2,1)}) fusion(bf16[16,16,2688]{2,1,0:T(8,128)(2,1)} %all-to-all-done), kind=kLoop, calls=%fused_computation.59 | loop fusion | bytes 2752512 | tf_op jit(solution)/shard_map/slice | solution.py:300
  40.7 4.4 %collective-permute-start.3 = (bf16[8,16,2688]{2,1,0:T(8,128)(2,1)}, bf16[8,16,2688]{2,1,0:T(8,128)(2,1)}, u32[]{:S(2)}, u32[]{:S(2)}) collective-permute-start(bf16[8,16,2688]{2,1,0:T(8,128)(2,1)} %get-tuple-element.56), channel_id=1, source_target_pairs={{0,65},{64,0},{1,64},{65,1},{2,67},{66,2},{3,66},{67,3},{4,69},{68... | collective-permute-start | bytes 2064392 | tf_op jit(solution)/shard_map/ppermute | solution.py:268
  47.7 1.9 %fusion.24 = f32[256,256]{1,0:T(8,128)S(1)} fusion(bf16[256,2688]{1,0:T(8,128)(2,1)} %bitcast.7, bf16[256,2688]{1,0:T(8,128)(2,1)S(1)} %fusion), kind=kOutput, calls=%fused_computation.61 | convolution fusion | flops 352321536 | bytes 3014656 | tf_op jit(solution)/shard_map/dot_general | solution.py:272
  49.6 9.1 %all-to-all-done.1 = bf16[16,2,16,1408]{3,2,1,0:T(8,128)(2,1)} async-done(((bf16[16,2,16,1408]{3,2,1,0:T(8,128)(2,1)}), bf16[16,2,16,1408]{3,2,1,0:T(8,128)(2,1)}, u32[]{:S(2)}, u32[]{:S(2)}) %all-to-all-start.1) | async-done | bytes 1441824 | tf_op jit(solution)/shard_map/all_to_all | solution.py:301
  58.7 2.2 %convolution_bitcast_fusion = f32[2,16,16,256]{3,2,0,1:T(8,128)S(1)} fusion(bf16[16,2,16,1408]{3,2,1,0:T(8,128)(2,1)} %all-to-all-done.1, bf16[128,4096]{1,0:T(8,128)(2,1)} %bitcast.8, bf16[128,4096]{1,0:T(8,128)(2,1)} %collective-permute-done.1), kind=kOutput, calls=%fused_computation.13 | convolution fusion | flops 370540544 | bytes 4063232 | tf_op jit(solution)/shard_map/dot_general | solution.py:272
  61.0 1.7 fusion.26
  66.1 2.1 %shard_map.128 = (f32[1024,128]{1,0:T(8,128)S(1)}, f32[256,128]{1,0:T(8,128)}) custom-call(s32[2]{0:T(128)S(1)} %pad_add_fusion.core, f32[512,128]{1,0:T(8,128)S(1)} %get-tuple-element.58.up_mine, f32[512,128]{1,0:T(8,128)S(1)} %collective-permute-done.5.up_theirs, f32[3072,128]{1,0:T(8,128)S(1)} %get-tuple-element.30.ys, ...), custom_call_target="tpu_custom_call" | custom-call | flops 10000000 | bytes 4000000 | tf_op jit(solution)/shard_map/pallas_call | solution.py:310
  69.5 8.3 %all-to-all-start.2 = ((f32[64,4,128]{2,1,0:T(4,128)}), f32[64,4,128]{2,1,0:T(4,128)S(1)}, u32[]{:S(2)}, u32[]{:S(2)}) async-start(f32[64,4,128]{2,1,0:T(4,128)} %bitcast.18), calls=%async_computation.2 | async-start | bytes 262144 | tf_op jit(solution)/shard_map/all_to_all | solution.py:321
  77.8 8.4 %all-to-all-done.2 = f32[64,4,128]{2,1,0:T(4,128)S(1)} async-done(((f32[64,4,128]{2,1,0:T(4,128)}), f32[64,4,128]{2,1,0:T(4,128)S(1)}, u32[]{:S(2)}, u32[]{:S(2)}) %all-to-all-start.2) | async-done | bytes 131104 | tf_op jit(solution)/shard_map/all_to_all | solution.py:321
  87.0 4.6 %all-to-all-start.3 = ((f32[64,4,128]{2,1,0:T(4,128)}), f32[64,4,128]{2,1,0:T(4,128)S(1)}, u32[]{:S(2)}, u32[]{:S(2)}) async-start(f32[64,4,128]{2,1,0:T(4,128)} %bitcast.20), calls=%async_computation.3 | async-start | bytes 262144 | tf_op jit(solution)/shard_map/all_to_all | solution.py:324
  91.6 8.4 %all-to-all-done.3 = f32[64,4,128]{2,1,0:T(4,128)S(1)} async-done(((f32[64,4,128]{2,1,0:T(4,128)}), f32[64,4,128]{2,1,0:T(4,128)S(1)}, u32[]{:S(2)}, u32[]{:S(2)}) %all-to-all-start.3) | async-done | bytes 131104 | tf_op jit(solution)/shard_map/all_to_all | solution.py:324
  103.8 3.5 %convolution_convert_fusion = bf16[512,2304]{1,0:T(8,128)(2,1)} fusion(bf16[512,256]{1,0:T(8,128)(2,1)S(1)} %bitcast.92, bf16[128,4096]{1,0:T(8,128)(2,1)} %collective-permute-done.1, bf16[128,4096]{1,0:T(8,128)(2,1)} %bitcast.8), kind=kOutput, calls=%fused_computation | convolution fusion | flops 607518720 | bytes 4718592 | tf_op jit(solution)/shard_map/dot_general | solution.py:276
  107.3 4.4 %all-to-all-start.4 = ((bf16[16,2,16,2304]{3,2,1,0:T(8,128)(2,1)}), bf16[16,2,16,2304]{3,2,1,0:T(8,128)(2,1)}, u32[]{:S(2)}, u32[]{:S(2)}) async-start(bf16[16,2,16,2304]{3,2,1,0:T(8,128)(2,1)} %bitcast.81), calls=%async_computation.4 | async-start | bytes 4718592 | tf_op jit(solution)/shard_map/all_to_all | solution.py:346
  115.9 2.5 %collective-permute-start.10 = (bf16[256,896]{1,0:T(8,128)(2,1)S(1)}, bf16[256,896]{1,0:T(8,128)(2,1)S(1)}, u32[]{:S(2)}, u32[]{:S(2)}) collective-permute-start(bf16[256,896]{1,0:T(8,128)(2,1)S(1)} %convolution_convert_fusion.1), channel_id=1, source_target_pairs={{0,65},{65,0},{1,64},{64,1},{2,67},{67,2},{3,66},{66,3},{4,69},{69... | collective-permute-start | bytes 1376264 | tf_op jit(solution)/shard_map/ppermute | solution.py:343
  118.4 5.1 %shard_map.131 = (bf16[128,1024]{1,0:T(8,128)(2,1)}, bf16[128,1024]{1,0:T(8,128)(2,1)}, bf16[128,1024]{1,0:T(8,128)(2,1)}, f32[304,128]{1,0:T(8,128)S(1)}) custom-call(f32[1024,128]{1,0:T(8,128)S(1)} %get-tuple-element.32.up, f32[1024,128]{1,0:T(8,128)S(1)} %get-tuple-element.35.filt, f32[3072,128]{1,0:T(8,128)S(1)} %get-tuple-element.30.ys, ...), custom_call_target="tpu_custom_call" | custom-call | flops 7000000000 | bytes 4000000 | tf_op jit(solution)/shard_map/pallas_call | solution.py:29
  124.9 3.6 %collective-permute-done.8.one = bf16[256,896]{1,0:T(8,128)(2,1)S(1)} collective-permute-done((bf16[256,896]{1,0:T(8,128)(2,1)S(1)}, bf16[256,896]{1,0:T(8,128)(2,1)S(1)}, u32[]{:S(2)}, u32[]{:S(2)}) %collective-permute-start.8) | collective-permute-done | bytes 458784 | tf_op jit(solution)/shard_map/ppermute | solution.py:341
  128.5 7.1 %collective-permute-done.9.two = bf16[256,896]{1,0:T(8,128)(2,1)S(1)} collective-permute-done((bf16[256,896]{1,0:T(8,128)(2,1)S(1)}, bf16[256,896]{1,0:T(8,128)(2,1)S(1)}, u32[]{:S(2)}, u32[]{:S(2)}) %collective-permute-start.9) | collective-permute-done | bytes 458784 | tf_op jit(solution)/shard_map/ppermute | solution.py:342
  135.6 1.9 collective-permute-done.10.three
  138.5 6.8 %all-to-all-done.4 = bf16[16,2,16,2304]{3,2,1,0:T(8,128)(2,1)} async-done(((bf16[16,2,16,2304]{3,2,1,0:T(8,128)(2,1)}), bf16[16,2,16,2304]{3,2,1,0:T(8,128)(2,1)}, u32[]{:S(2)}, u32[]{:S(2)}) %all-to-all-start.4) | async-done | bytes 2359328 | tf_op jit(solution)/shard_map/all_to_all | solution.py:346
  145.4 5.9 %all-to-all-start.5 = ((bf16[16,16,1152]{2,1,0:T(8,128)(2,1)}), bf16[16,16,1152]{2,1,0:T(8,128)(2,1)S(1)}, u32[]{:S(2)}, u32[]{:S(2)}) async-start(bf16[16,16,1152]{2,1,0:T(8,128)(2,1)} %bitcast.38), calls=%async_computation.5 | async-start | bytes 1179648 | tf_op jit(solution)/shard_map/all_to_all | solution.py:360
  151.3 2.0 %reduce_sum.30 = bf16[2,16,2304]{2,1,0:T(8,128)(2,1)S(1)} reduce(bf16[16,2,16,2304]{3,2,1,0:T(8,128)(2,1)} %all-to-all-done.4, bf16[]{:T(256)} %constant.68.clone.1), dimensions={0}, to_apply=%region_0.1 | reduce | flops 1105920 | bytes 2506754 | tf_op jit(solution)/shard_map/reduce_sum | solution.py:361
  155.1 2.5 %collective-permute-start.14 = (bf16[16,2304]{1,0:T(8,128)(2,1)S(1)}, bf16[16,2304]{1,0:T(8,128)(2,1)S(1)}, u32[]{:S(2)}, u32[]{:S(2)}) collective-permute-start(bf16[16,2304]{1,0:T(8,128)(2,1)S(1)} %get-tuple-element.63), channel_id=1, source_target_pairs={{0,65},{65,0},{1,64},{64,1},{2,67},{67,2},{3,66},{66,3},{4,69},{69... | collective-permute-start | bytes 221192 | tf_op jit(solution)/shard_map/ppermute | solution.py:367
  157.5 1.8 collective-permute-done.12
  160.6 2.3 %all-to-all-done.5 = bf16[16,16,1152]{2,1,0:T(8,128)(2,1)S(1)} async-done(((bf16[16,16,1152]{2,1,0:T(8,128)(2,1)}), bf16[16,16,1152]{2,1,0:T(8,128)(2,1)S(1)}, u32[]{:S(2)}, u32[]{:S(2)}) %all-to-all-start.5) | async-done | bytes 589856 | tf_op jit(solution)/shard_map/all_to_all | solution.py:360
  165.2 7.5 %all-to-all-start.6 = ((f32[64,16,128]{2,1,0:T(8,128)}), f32[64,16,128]{2,1,0:T(8,128)S(1)}, u32[]{:S(2)}, u32[]{:S(2)}) async-start(f32[64,16,128]{2,1,0:T(8,128)} %broadcast_in_dim.23), calls=%async_computation.6 | async-start | bytes 1048576 | tf_op jit(solution)/shard_map/all_to_all | solution.py:374
  172.8 11.8 %all-to-all-done.6 = f32[64,16,128]{2,1,0:T(8,128)S(1)} async-done(((f32[64,16,128]{2,1,0:T(8,128)}), f32[64,16,128]{2,1,0:T(8,128)S(1)}, u32[]{:S(2)}, u32[]{:S(2)}) %all-to-all-start.6) | async-done | bytes 524320 | tf_op jit(solution)/shard_map/all_to_all | solution.py:374
  (102 shorter events, 35.0 us)
Async XLA Ops:
  2.7 8.2 %slice-start.1 = ((bf16[1,128,1024]{2,1,0:T(8,128)(2,1)}), bf16[1,8,1024]{2,1,0:T(8,128)(2,1)S(1)}, s32[]{:S(2)}) async-start(bf16[1,128,1024]{2,1,0:T(8,128)(2,1)} %param.9), calls=%async_computation.8 | async-start | bytes 32768 | tf_op jit(solution)/shard_map/slice | solution.py:282
  2.7 8.2 %slice-start.2 = ((bf16[1,128,1024]{2,1,0:T(8,128)(2,1)}), bf16[1,8,1024]{2,1,0:T(8,128)(2,1)S(1)}, s32[]{:S(2)}) async-start(bf16[1,128,1024]{2,1,0:T(8,128)(2,1)} %param.10), calls=%async_computation.9 | async-start | bytes 32768 | tf_op jit(solution)/shard_map/slice | solution.py:282
  2.7 14.8 %copy-start.10 = (f32[1024,16]{0,1:T(8,128)S(1)}, f32[1024,16]{0,1:T(8,128)}, u32[]{:S(2)}) copy-start(f32[1024,16]{0,1:T(8,128)} %param.15) | copy-start | bytes 196612
  2.7 14.8 %copy-start.11 = (f32[1024,16]{0,1:T(8,128)S(1)}, f32[1024,16]{0,1:T(8,128)}, u32[]{:S(2)}) copy-start(f32[1024,16]{0,1:T(8,128)} %param.14) | copy-start | bytes 196612
  2.8 14.9 %copy-start.9 = (f32[3,1024,7]{1,2,0:T(8,128)S(1)}, f32[3,1024,7]{1,2,0:T(8,128)}, u32[]{:S(2)}) copy-start(f32[3,1024,7]{1,2,0:T(8,128)} %param.13) | copy-start | bytes 258052
  2.8 29.8 %all-to-all-start = ((bf16[16,16,2688]{2,1,0:T(8,128)(2,1)}), bf16[16,16,2688]{2,1,0:T(8,128)(2,1)}, u32[]{:S(2)}, u32[]{:S(2)}) async-start(bf16[16,16,2688]{2,1,0:T(8,128)(2,1)} %broadcast_in_dim.18), calls=%async_computation | async-start | bytes 2752512 | tf_op jit(solution)/shard_map/all_to_all | solution.py:296
  10.9 9.1 %copy-start = (bf16[1,128,1024]{2,1,0:T(8,128)(2,1)S(1)}, bf16[1,128,1024]{2,1,0:T(8,128)(2,1)}, u32[]{:S(2)}) copy-start(bf16[1,128,1024]{2,1,0:T(8,128)(2,1)} %param.8) | copy-start | bytes 786436
  10.9 9.1 %copy-start.1 = (bf16[1,128,1024]{2,1,0:T(8,128)(2,1)S(1)}, bf16[1,128,1024]{2,1,0:T(8,128)(2,1)}, u32[]{:S(2)}) copy-start(bf16[1,128,1024]{2,1,0:T(8,128)(2,1)} %param.9) | copy-start | bytes 786436
  10.9 9.1 %copy-start.2 = (bf16[1,128,1024]{2,1,0:T(8,128)(2,1)S(1)}, bf16[1,128,1024]{2,1,0:T(8,128)(2,1)}, u32[]{:S(2)}) copy-start(bf16[1,128,1024]{2,1,0:T(8,128)(2,1)} %param.10) | copy-start | bytes 786436
  11.0 9.0 %collective-permute-start = (bf16[3,8,1024]{2,1,0:T(8,128)(2,1)S(1)}, bf16[3,8,1024]{2,1,0:T(8,128)(2,1)S(1)}, u32[]{:S(2)}, u32[]{:S(2)}) collective-permute-start(bf16[3,8,1024]{2,1,0:T(8,128)(2,1)S(1)} %pad_maximum_fusion.5), channel_id=1, source_target_pairs={{0,2},{2,4},{4,6},{6,8},{8,10},{10,12},{12,14},{14,16},{16,18},{18... | collective-permute-start | bytes 147464 | tf_op jit(solution)/shard_map/ppermute | solution.py:256
  12.6 32.6 %collective-permute-start.1 = (bf16[128,4096]{1,0:T(8,128)(2,1)}, bf16[128,4096]{1,0:T(8,128)(2,1)}, u32[]{:S(2)}, u32[]{:S(2)}) collective-permute-start(bf16[128,4096]{1,0:T(8,128)(2,1)} %bitcast.8), channel_id=1, source_target_pairs={{0,2},{2,0},{1,3},{3,1},{4,6},{6,4},{5,7},{7,5},{8,10},{10,8},{9,1... | collective-permute-start | bytes 3145736 | tf_op jit(solution)/shard_map/ppermute | solution.py:260
  15.9 4.0 %collective-permute-start.4 = (bf16[16,1408]{1,0:T(8,128)(2,1)S(1)}, bf16[16,1408]{1,0:T(8,128)(2,1)S(1)}, u32[]{:S(2)}, u32[]{:S(2)}) collective-permute-start(bf16[16,1408]{1,0:T(8,128)(2,1)S(1)} %get-tuple-element.68), channel_id=1, source_target_pairs={{0,64},{64,0},{1,65},{65,1},{2,66},{66,2},{3,67},{67,3},{4,68},{68... | collective-permute-start | bytes 135176 | tf_op jit(solution)/shard_map/ppermute | solution.py:260
  33.8 24.9 %all-to-all-start.1 = ((bf16[16,2,16,1408]{3,2,1,0:T(8,128)(2,1)}), bf16[16,2,16,1408]{3,2,1,0:T(8,128)(2,1)}, u32[]{:S(2)}, u32[]{:S(2)}) async-start(bf16[16,2,16,1408]{3,2,1,0:T(8,128)(2,1)} %broadcast_in_dim.19), calls=%async_computation.1 | async-start | bytes 2883584 | tf_op jit(solution)/shard_map/all_to_all | solution.py:301
  40.7 20.2 %collective-permute-start.3 = (bf16[8,16,2688]{2,1,0:T(8,128)(2,1)}, bf16[8,16,2688]{2,1,0:T(8,128)(2,1)}, u32[]{:S(2)}, u32[]{:S(2)}) collective-permute-start(bf16[8,16,2688]{2,1,0:T(8,128)(2,1)} %get-tuple-element.56), channel_id=1, source_target_pairs={{0,65},{64,0},{1,64},{65,1},{2,67},{66,2},{3,66},{67,3},{4,69},{68... | collective-permute-start | bytes 2064392 | tf_op jit(solution)/shard_map/ppermute | solution.py:268
  46.6 16.1 %collective-permute-start.2 = (bf16[8,16,2688]{2,1,0:T(8,128)(2,1)}, bf16[8,16,2688]{2,1,0:T(8,128)(2,1)}, u32[]{:S(2)}, u32[]{:S(2)}) collective-permute-start(bf16[8,16,2688]{2,1,0:T(8,128)(2,1)} %get-tuple-element.55), channel_id=1, source_target_pairs={{0,64},{64,1},{1,65},{65,0},{2,66},{66,3},{3,67},{67,2},{4,68},{68... | collective-permute-start | bytes 2064392 | tf_op jit(solution)/shard_map/ppermute | solution.py:268
  64.5 1.6 collective-permute-start.5
  68.2 18.0 %collective-permute-start.6 = (f32[256,128]{1,0:T(8,128)S(1)}, f32[256,128]{1,0:T(8,128)S(1)}, u32[]{:S(2)}, u32[]{:S(2)}) collective-permute-start(f32[256,128]{1,0:T(8,128)S(1)} %pad_maximum_fusion.3), channel_id=1, source_target_pairs={{2,0},{4,2},{6,4},{8,6},{10,8},{12,10},{14,12},{16,14},{18,16},{20... | collective-permute-start | bytes 393224 | tf_op jit(solution)/shard_map/ppermute | solution.py:256
  69.5 16.7 %all-to-all-start.2 = ((f32[64,4,128]{2,1,0:T(4,128)}), f32[64,4,128]{2,1,0:T(4,128)S(1)}, u32[]{:S(2)}, u32[]{:S(2)}) async-start(f32[64,4,128]{2,1,0:T(4,128)} %bitcast.18), calls=%async_computation.2 | async-start | bytes 262144 | tf_op jit(solution)/shard_map/all_to_all | solution.py:321
  87.0 13.1 %all-to-all-start.3 = ((f32[64,4,128]{2,1,0:T(4,128)}), f32[64,4,128]{2,1,0:T(4,128)S(1)}, u32[]{:S(2)}, u32[]{:S(2)}) async-start(f32[64,4,128]{2,1,0:T(4,128)} %bitcast.20), calls=%async_computation.3 | async-start | bytes 262144 | tf_op jit(solution)/shard_map/all_to_all | solution.py:324
  101.7 1.4 collective-permute-start.7
  107.3 38.1 %all-to-all-start.4 = ((bf16[16,2,16,2304]{3,2,1,0:T(8,128)(2,1)}), bf16[16,2,16,2304]{3,2,1,0:T(8,128)(2,1)}, u32[]{:S(2)}, u32[]{:S(2)}) async-start(bf16[16,2,16,2304]{3,2,1,0:T(8,128)(2,1)} %bitcast.81), calls=%async_computation.4 | async-start | bytes 4718592 | tf_op jit(solution)/shard_map/all_to_all | solution.py:346
  113.5 15.0 %collective-permute-start.8 = (bf16[256,896]{1,0:T(8,128)(2,1)S(1)}, bf16[256,896]{1,0:T(8,128)(2,1)S(1)}, u32[]{:S(2)}, u32[]{:S(2)}) collective-permute-start(bf16[256,896]{1,0:T(8,128)(2,1)S(1)} %convolution_convert_fusion.3), channel_id=1, source_target_pairs={{0,1},{1,0},{64,65},{65,64},{2,3},{3,2},{66,67},{67,66},{4,5},{5,4... | collective-permute-start | bytes 1376264 | tf_op jit(solution)/shard_map/ppermute | solution.py:341
  115.1 20.5 %collective-permute-start.9 = (bf16[256,896]{1,0:T(8,128)(2,1)S(1)}, bf16[256,896]{1,0:T(8,128)(2,1)S(1)}, u32[]{:S(2)}, u32[]{:S(2)}) collective-permute-start(bf16[256,896]{1,0:T(8,128)(2,1)S(1)} %convolution_convert_fusion.2), channel_id=1, source_target_pairs={{0,64},{64,0},{1,65},{65,1},{2,66},{66,2},{3,67},{67,3},{4,68},{68... | collective-permute-start | bytes 1376264 | tf_op jit(solution)/shard_map/ppermute | solution.py:342
  115.9 21.6 %collective-permute-start.10 = (bf16[256,896]{1,0:T(8,128)(2,1)S(1)}, bf16[256,896]{1,0:T(8,128)(2,1)S(1)}, u32[]{:S(2)}, u32[]{:S(2)}) collective-permute-start(bf16[256,896]{1,0:T(8,128)(2,1)S(1)} %convolution_convert_fusion.1), channel_id=1, source_target_pairs={{0,65},{65,0},{1,64},{64,1},{2,67},{67,2},{3,66},{66,3},{4,69},{69... | collective-permute-start | bytes 1376264 | tf_op jit(solution)/shard_map/ppermute | solution.py:343
  123.6 1.3 collective-permute-start.11
  145.4 17.5 %all-to-all-start.5 = ((bf16[16,16,1152]{2,1,0:T(8,128)(2,1)}), bf16[16,16,1152]{2,1,0:T(8,128)(2,1)S(1)}, u32[]{:S(2)}, u32[]{:S(2)}) async-start(bf16[16,16,1152]{2,1,0:T(8,128)(2,1)} %bitcast.38), calls=%async_computation.5 | async-start | bytes 1179648 | tf_op jit(solution)/shard_map/all_to_all | solution.py:360
  153.4 6.0 %collective-permute-start.12 = (bf16[16,2304]{1,0:T(8,128)(2,1)S(1)}, bf16[16,2304]{1,0:T(8,128)(2,1)S(1)}, u32[]{:S(2)}, u32[]{:S(2)}) collective-permute-start(bf16[16,2304]{1,0:T(8,128)(2,1)S(1)} %get-tuple-element.64), channel_id=1, source_target_pairs={{0,1},{1,0},{2,3},{3,2},{4,5},{5,4},{6,7},{7,6},{8,9},{9,8},{10,11... | collective-permute-start | bytes 221192 | tf_op jit(solution)/shard_map/ppermute | solution.py:260
  154.7 4.7 %collective-permute-start.13 = (bf16[16,2304]{1,0:T(8,128)(2,1)S(1)}, bf16[16,2304]{1,0:T(8,128)(2,1)S(1)}, u32[]{:S(2)}, u32[]{:S(2)}) collective-permute-start(bf16[16,2304]{1,0:T(8,128)(2,1)S(1)} %get-tuple-element.63), channel_id=1, source_target_pairs={{0,64},{64,0},{1,65},{65,1},{2,66},{66,2},{3,67},{67,3},{4,68},{68... | collective-permute-start | bytes 221192 | tf_op jit(solution)/shard_map/ppermute | solution.py:366
  155.1 5.6 %collective-permute-start.14 = (bf16[16,2304]{1,0:T(8,128)(2,1)S(1)}, bf16[16,2304]{1,0:T(8,128)(2,1)S(1)}, u32[]{:S(2)}, u32[]{:S(2)}) collective-permute-start(bf16[16,2304]{1,0:T(8,128)(2,1)S(1)} %get-tuple-element.63), channel_id=1, source_target_pairs={{0,65},{65,0},{1,64},{64,1},{2,67},{67,2},{3,66},{66,3},{4,69},{69... | collective-permute-start | bytes 221192 | tf_op jit(solution)/shard_map/ppermute | solution.py:367
  163.0 9.8 %collective-permute-start.15 = (f32[16,896]{1,0:T(8,128)S(1)}, f32[16,896]{1,0:T(8,128)S(1)}, u32[]{:S(2)}, u32[]{:S(2)}) collective-permute-start(f32[16,896]{1,0:T(8,128)S(1)} %slice.97), channel_id=1, source_target_pairs={{0,1},{1,0},{2,3},{3,2},{4,5},{5,4},{6,7},{7,6},{8,9},{9,8},{10,11... | collective-permute-start | bytes 172040 | tf_op jit(solution)/shard_map/ppermute | solution.py:260
  165.2 19.4 %all-to-all-start.6 = ((f32[64,16,128]{2,1,0:T(8,128)}), f32[64,16,128]{2,1,0:T(8,128)S(1)}, u32[]{:S(2)}, u32[]{:S(2)}) async-start(f32[64,16,128]{2,1,0:T(8,128)} %broadcast_in_dim.23), calls=%async_computation.6 | async-start | bytes 1048576 | tf_op jit(solution)/shard_map/all_to_all | solution.py:374
  184.6 1.4 collective-permute-start.16
  (7 other events, 19.8 us)

commit v4 on v3

--- a/solution.py
+++ b/solution.py
@@ -20,7 +20,8 @@
 WA = 2688
 LAST = 7_000_000_000
 HALF = 152
-GA = 1792
+SHARE = 10
+GA = 2048
 
 VMEM = pl.BlockSpec(memory_space=pltpu.VMEM)
 
@@ -234,12 +235,12 @@
         at = slice(16 * d, 16 * d + 16)
         value = own[at, :] + one[at, :].astype(F32) + two[at, :].astype(F32) + three[at, :].astype(F32)
         out[at, 0:width] = value.astype(BF)
-        here = slice(16 * d, min(16 * d + 16, HALF))
+        here = slice(SHARE * d, min(SHARE * d + SHARE, HALF))
         rows = max(0, here.stop - here.start)
         sums = jnp.zeros((16, 128), F32)
         if rows > 0:
             sums = part[here, :] + other_part[here, :]
-        if 0 < rows < 16:
+        if rows > 0:
             sums = jnp.concatenate([sums, jnp.zeros((16 - rows, 128), F32)], axis=0)
         high = sums.astype(BF)
         out[at, width : width + 128] = high
@@ -304,6 +305,7 @@
 
     early, rest = go_both[:, :WA], go_both[:, WA:]
     product = [turned_dot(part.reshape(-1, WA), early) for part in (near, far_low, far_high)]
+    late, *product = lax.optimization_barrier((late, *product))
     last = turned_dot(late, rest).reshape(16, 2, 16, 2 * T)
     up_both = jnp.concatenate(product, axis=0) + jnp.swapaxes(last, 0, 1).reshape(512, 2 * T)
     up_mine, up_theirs = up_both[:, :T], swapped(up_both[:, T:], "core")
@@ -371,8 +373,9 @@
     first = joined[:, :part_a]
     first_other = swapped(first, "yh")
     part = joined[:, part_a : part_a + 128] + joined[:, part_a + 128 :]
-    part = lax.all_to_all(jnp.broadcast_to(part, (64, 16, 128)), ("yl", "yh", "x", "z"), 0, 0)
-    part = jnp.sum(part.reshape(4, 256, 128)[:, :HALF], axis=0)
+    part = part[:SHARE].reshape(SHARE // 2, 2, 128)
+    part = lax.all_to_all(jnp.broadcast_to(part, (64, SHARE // 2, 2, 128)), ("yl", "yh", "x", "z"), 0, 0)
+    part = jnp.sum(part.reshape(4, 16 * SHARE, 128)[:, :HALF], axis=0)
     rest = swapped(part, "core")
     level = (near.astype(F32) + levels[0].astype(F32)) + (levels[1].astype(F32) + levels[2].astype(F32))
     weight_grad = jnp.concatenate(

time: 189 us -> 184 us (0.974)
  waiting for transfers between devices: 78.4 us -> 73.3 us
  matrix products: 12.1 us -> 15 us
    ppermute x2, waiting for transfers between devices: 0.01 us -> 9.25 us  [along_y(): return lax.ppermute(value, ('yl', 'yh'), pairs)]
    all_to_all x1, waiting for transfers between devices: 9.08 us -> 0.01 us  [shards(): lax.all_to_all(jnp.broadcast_to(late, (16, 2, 16, D - WA)), XZ, 0, 0)]
    all_to_all x1, waiting for transfers between devices: 6.83 us -> 1.28 us  [shards(): spread = lax.all_to_all(spread.reshape(16, 2, 16, D - GA), XZ, 0, 0)]
    dot_general x4, matrix products: 4.36 us -> 7.36 us  [rounded_dot(): return jnp.dot(rows, columns, preferred_element_type=F32).astype(BF)]
    ppermute x8, waiting for transfers between devices: 8.3 us -> 5.43 us  [swapped(): return lax.ppermute(value, axis, [(0, 1), (1, 0)])]
    ppermute x1, waiting for transfers between devices: 7.14 us -> 9.6 us  [shards(): lax.ppermute(parts[1], ('yl', 'yh'), [(0, 2), (2, 0), (1, 3), (3, 1)])]
    all_to_all x1, waiting for transfers between devices: 9.4 us -> 11.8 us  [shards(): lax.all_to_all(jnp.broadcast_to(out_weight[:, :WA], (16, 16, WA)), XZ, 0, 0)]
    ppermute x8, starting transfers between devices: 7.24 us -> 9.63 us  [swapped(): return lax.ppermute(value, axis, [(0, 1), (1, 0)])]
  transfers between devices with their start and end apart: 24 -> 24, of which waited for: 17 -> 16; matrix products, arithmetic and copies ran while one was open for 10% -> 11% of each run, Pallas kernels for 4% -> 4%
where the time goes in v4:
time: 184 us; the launch traced here: 182 us
  waiting for transfers between devices  73.3 us (40%)
  starting transfers between devices  64.7 us (35%)
  matrix products  15 us (8%)
  Pallas kernels  12.6 us (7%)
  local copies, waits for them, and re-layouts  11 us (6%)
  other arithmetic  4.57 us (2%)
    all_to_all x1, waiting for transfers between devices, shards(): lax.all_to_all(jnp.broadcast_to(out_weight[:, :WA], (16, 16, WA)), XZ, 0, 0)  11.8 us
    all_to_all x1, waiting for transfers between devices, shards(): lax.all_to_all(jnp.broadcast_to(part, (64, SHARE // 2, 2, 128)), ('yl', '...  10.8 us
    pallas_call x5, Pallas kernels, call(): pl.pallas_call(body, out_shape=outs, in_specs=[VMEM] * len(ins), out_spec...  10.5 us
    ppermute x8, starting transfers between devices, swapped(): return lax.ppermute(value, axis, [(0, 1), (1, 0)])  9.63 us
    ppermute x1, waiting for transfers between devices, shards(): lax.ppermute(parts[1], ('yl', 'yh'), [(0, 2), (2, 0), (1, 3), (3, 1)])  9.6 us
    ppermute x2, waiting for transfers between devices, along_y(): return lax.ppermute(value, ('yl', 'yh'), pairs)  9.25 us
    all_to_all x1, starting transfers between devices, shards(): lax.all_to_all(packed.reshape(64, 4, 128), CTX, 0, 0).reshape(256, 128)  9.04 us
    all_to_all x1, waiting for transfers between devices, shards(): lax.all_to_all(scanned.reshape(64, 4, 128), CTX, 0, 0).reshape(256, 128)  8.44 us
  transfers between devices with their start and end apart: 24, of which 16 were waited for; matrix products, arithmetic and copies ran while one was open for 11% of the time, Pallas kernels for 4%

profile of v4, /device:TPU:0, one launch (start us, length us, event | category | flops | bytes accessed | tf_op | source)
XLA Modules:
  0.0 182.3 jit_solution(1815365826661663420)
XLA Ops:
  2.8 8.1 %all-to-all-start.1 = ((bf16[16,16,2688]{2,1,0:T(8,128)(2,1)}), bf16[16,16,2688]{2,1,0:T(8,128)(2,1)}, u32[]{:S(2)}, u32[]{:S(2)}) async-start(bf16[16,16,2688]{2,1,0:T(8,128)(2,1)} %broadcast_in_dim.19), calls=%async_computation.1 | async-start | bytes 2752512 | tf_op jit(solution)/shard_map/all_to_all | solution.py:297
  14.7 2.7 %collective-permute-start.2 = (bf16[128,4096]{1,0:T(8,128)(2,1)}, bf16[128,4096]{1,0:T(8,128)(2,1)}, u32[]{:S(2)}, u32[]{:S(2)}) collective-permute-start(bf16[128,4096]{1,0:T(8,128)(2,1)} %bitcast.11), channel_id=1, source_target_pairs={{0,2},{2,0},{1,3},{3,1},{4,6},{6,4},{5,7},{7,5},{8,10},{10,8},{9,1... | collective-permute-start | bytes 3145736 | tf_op jit(solution)/shard_map/ppermute | solution.py:261
  17.7 1.8 %shard_map.127 = (f32[3264,128]{1,0:T(8,128)S(1)}, f32[3072,128]{1,0:T(8,128)S(1)}, f32[128,128]{1,0:T(8,128)S(1)}) custom-call(bf16[128,1024]{1,0:T(8,128)(2,1)S(1)} %bitcast.70, bf16[128,1024]{1,0:T(8,128)(2,1)S(1)} %bitcast.71, bf16[128,1024]{1,0:T(8,128)(2,1)S(1)} %bitcast.72, f32[192,128]{1,0:T(8,128)S(1)} %reshape.117.halo, ...), custom_call_target="tpu_custom_call" | custom-call | flops 10000000 | bytes 4000000 | tf_op jit(solution)/shard_map/pallas_call | solution.py:30
  20.7 11.8 %all-to-all-done.1 = bf16[16,16,2688]{2,1,0:T(8,128)(2,1)} async-done(((bf16[16,16,2688]{2,1,0:T(8,128)(2,1)}), bf16[16,16,2688]{2,1,0:T(8,128)(2,1)}, u32[]{:S(2)}, u32[]{:S(2)}) %all-to-all-start.1) | async-done | bytes 1376288 | tf_op jit(solution)/shard_map/all_to_all | solution.py:297
  33.7 4.4 %all-to-all-start = ((bf16[16,2,16,1408]{3,2,1,0:T(8,128)(2,1)}), bf16[16,2,16,1408]{3,2,1,0:T(8,128)(2,1)}, u32[]{:S(2)}, u32[]{:S(2)}) async-start(bf16[16,2,16,1408]{3,2,1,0:T(8,128)(2,1)} %broadcast_in_dim.18), calls=%async_computation | async-start | bytes 2883584 | tf_op jit(solution)/shard_map/all_to_all | solution.py:302
  38.1 2.6 %fusion.26 = (bf16[8,16,2688]{2,1,0:T(8,128)(2,1)}, bf16[8,16,2688]{2,1,0:T(8,128)(2,1)}) fusion(bf16[16,16,2688]{2,1,0:T(8,128)(2,1)} %all-to-all-done.1), kind=kLoop, calls=%fused_computation.58 | loop fusion | bytes 2752512 | tf_op jit(solution)/shard_map/slice | solution.py:301
  40.7 2.7 %collective-permute-start.3 = (bf16[8,16,2688]{2,1,0:T(8,128)(2,1)}, bf16[8,16,2688]{2,1,0:T(8,128)(2,1)}, u32[]{:S(2)}, u32[]{:S(2)}) collective-permute-start(bf16[8,16,2688]{2,1,0:T(8,128)(2,1)} %get-tuple-element.62), channel_id=1, source_target_pairs={{0,64},{64,1},{1,65},{65,0},{2,66},{66,3},{3,67},{67,2},{4,68},{68... | collective-permute-start | bytes 2064392 | tf_op jit(solution)/shard_map/ppermute | solution.py:269
  43.4 1.7 collective-permute-start.4
  46.5 1.9 %fusion.29 = f32[256,256]{1,0:T(8,128)S(1)} fusion(bf16[256,2688]{1,0:T(8,128)(2,1)} %bitcast.10, bf16[256,2688]{1,0:T(8,128)(2,1)S(1)} %fusion), kind=kOutput, calls=%fused_computation.61 | convolution fusion | flops 352321536 | bytes 3014656 | tf_op jit(solution)/shard_map/dot_general | solution.py:273
  48.5 9.2 %collective-permute-done.3 = bf16[8,16,2688]{2,1,0:T(8,128)(2,1)} collective-permute-done((bf16[8,16,2688]{2,1,0:T(8,128)(2,1)}, bf16[8,16,2688]{2,1,0:T(8,128)(2,1)}, u32[]{:S(2)}, u32[]{:S(2)}) %collective-permute-start.3) | collective-permute-done | bytes 688160 | tf_op jit(solution)/shard_map/ppermute | solution.py:269
  57.7 1.7 fusion.30
  60.0 2.1 %fusion.3 = f32[512,256]{1,0:T(8,128)S(1)} fusion(bf16[512,1408]{1,0:T(8,128)(2,1)} %bitcast.4, bf16[128,4096]{1,0:T(8,128)(2,1)} %bitcast.11, bf16[128,4096]{1,0:T(8,128)(2,1)} %collective-permute-done.2), kind=kOutput, calls=%fused_computation.17 | convolution fusion | flops 370540544 | bytes 4063232 | tf_op jit(solution)/shard_map/dot_general | solution.py:273
  63.9 2.1 %shard_map.128 = (f32[1024,128]{1,0:T(8,128)S(1)}, f32[256,128]{1,0:T(8,128)}) custom-call(s32[2]{0:T(128)S(1)} %pad_add_fusion.core, f32[512,128]{1,0:T(8,128)S(1)} %get-tuple-element.64.up_mine, f32[512,128]{1,0:T(8,128)S(1)} %collective-permute-done.5.up_theirs, f32[3072,128]{1,0:T(8,128)S(1)} %get-tuple-element.38.ys, ...), custom_call_target="tpu_custom_call" | custom-call | flops 10000000 | bytes 4000000 | tf_op jit(solution)/shard_map/pallas_call | solution.py:312
  67.3 9.0 %all-to-all-start.2 = ((f32[64,4,128]{2,1,0:T(4,128)}), f32[64,4,128]{2,1,0:T(4,128)S(1)}, u32[]{:S(2)}, u32[]{:S(2)}) async-start(f32[64,4,128]{2,1,0:T(4,128)} %bitcast.18), calls=%async_computation.2 | async-start | bytes 262144 | tf_op jit(solution)/shard_map/all_to_all | solution.py:323
  76.4 8.4 %all-to-all-done.2 = f32[64,4,128]{2,1,0:T(4,128)S(1)} async-done(((f32[64,4,128]{2,1,0:T(4,128)}), f32[64,4,128]{2,1,0:T(4,128)S(1)}, u32[]{:S(2)}, u32[]{:S(2)}) %all-to-all-start.2) | async-done | bytes 131104 | tf_op jit(solution)/shard_map/all_to_all | solution.py:323
  85.6 4.6 %all-to-all-start.3 = ((f32[64,4,128]{2,1,0:T(4,128)}), f32[64,4,128]{2,1,0:T(4,128)S(1)}, u32[]{:S(2)}, u32[]{:S(2)}) async-start(f32[64,4,128]{2,1,0:T(4,128)} %bitcast.20), calls=%async_computation.3 | async-start | bytes 262144 | tf_op jit(solution)/shard_map/all_to_all | solution.py:326
  90.2 8.4 %all-to-all-done.3 = f32[64,4,128]{2,1,0:T(4,128)S(1)} async-done(((f32[64,4,128]{2,1,0:T(4,128)}), f32[64,4,128]{2,1,0:T(4,128)S(1)}, u32[]{:S(2)}, u32[]{:S(2)}) %all-to-all-start.3) | async-done | bytes 131104 | tf_op jit(solution)/shard_map/all_to_all | solution.py:326
  98.6 1.6 shard_map.130
  102.4 3.2 %convolution_convert_fusion = bf16[512,2048]{1,0:T(8,128)(2,1)} fusion(bf16[512,256]{1,0:T(8,128)(2,1)S(1)} %bitcast.86, bf16[128,4096]{1,0:T(8,128)(2,1)} %collective-permute-done.2, bf16[128,4096]{1,0:T(8,128)(2,1)} %bitcast.11), kind=kOutput, calls=%fused_computation | convolution fusion | flops 540016640 | bytes 4456448 | tf_op jit(solution)/shard_map/dot_general | solution.py:277
  105.6 4.4 %all-to-all-start.4 = ((bf16[16,2,16,2048]{3,2,1,0:T(8,128)(2,1)}), bf16[16,2,16,2048]{3,2,1,0:T(8,128)(2,1)}, u32[]{:S(2)}, u32[]{:S(2)}) async-start(bf16[16,2,16,2048]{3,2,1,0:T(8,128)(2,1)} %bitcast.74), calls=%async_computation.4 | async-start | bytes 4194304 | tf_op jit(solution)/shard_map/all_to_all | solution.py:348
  111.5 2.4 %collective-permute-start.8 = (bf16[256,1024]{1,0:T(8,128)(2,1)S(1)}, bf16[256,1024]{1,0:T(8,128)(2,1)S(1)}, u32[]{:S(2)}, u32[]{:S(2)}) collective-permute-start(bf16[256,1024]{1,0:T(8,128)(2,1)S(1)} %convolution_convert_fusion.3), channel_id=1, source_target_pairs={{0,1},{1,0},{64,65},{65,64},{2,3},{3,2},{66,67},{67,66},{4,5},{5,4... | collective-permute-start | bytes 1572872 | tf_op jit(solution)/shard_map/ppermute | solution.py:343
  118.5 5.1 %shard_map.131 = (bf16[128,1024]{1,0:T(8,128)(2,1)}, bf16[128,1024]{1,0:T(8,128)(2,1)}, bf16[128,1024]{1,0:T(8,128)(2,1)}, f32[304,128]{1,0:T(8,128)S(1)}) custom-call(f32[1024,128]{1,0:T(8,128)S(1)} %get-tuple-element.40.up, f32[1024,128]{1,0:T(8,128)S(1)} %get-tuple-element.43.filt, f32[3072,128]{1,0:T(8,128)S(1)} %get-tuple-element.38.ys, ...), custom_call_target="tpu_custom_call" | custom-call | flops 7000000000 | bytes 4000000 | tf_op jit(solution)/shard_map/pallas_call | solution.py:30
  125.1 2.8 %collective-permute-done.8.one = bf16[256,1024]{1,0:T(8,128)(2,1)S(1)} collective-permute-done((bf16[256,1024]{1,0:T(8,128)(2,1)S(1)}, bf16[256,1024]{1,0:T(8,128)(2,1)S(1)}, u32[]{:S(2)}, u32[]{:S(2)}) %collective-permute-start.8) | collective-permute-done | bytes 524320 | tf_op jit(solution)/shard_map/ppermute | solution.py:343
  127.9 9.6 %collective-permute-done.9.two = bf16[256,1024]{1,0:T(8,128)(2,1)S(1)} collective-permute-done((bf16[256,1024]{1,0:T(8,128)(2,1)S(1)}, bf16[256,1024]{1,0:T(8,128)(2,1)S(1)}, u32[]{:S(2)}, u32[]{:S(2)}) %collective-permute-start.9) | collective-permute-done | bytes 524320 | tf_op jit(solution)/shard_map/ppermute | solution.py:344
  140.8 5.5 %all-to-all-start.5 = ((bf16[16,16,1280]{2,1,0:T(8,128)(2,1)}), bf16[16,16,1280]{2,1,0:T(8,128)(2,1)S(1)}, u32[]{:S(2)}, u32[]{:S(2)}) async-start(bf16[16,16,1280]{2,1,0:T(8,128)(2,1)} %bitcast.38), calls=%async_computation.5 | async-start | bytes 1310720 | tf_op jit(solution)/shard_map/all_to_all | solution.py:362
  146.3 2.0 %reduce_sum.30 = bf16[2,16,2048]{2,1,0:T(8,128)(2,1)S(1)} reduce(bf16[16,2,16,2048]{3,2,1,0:T(8,128)(2,1)} %all-to-all-done.4, bf16[]{:T(256)} %constant.68.clone.1), dimensions={0}, to_apply=%region_0.1 | reduce | flops 983040 | bytes 2228226 | tf_op jit(solution)/shard_map/reduce_sum | solution.py:363
  148.3 2.4 %collective-permute-start.12 = (bf16[16,2048]{1,0:T(8,128)(2,1)S(1)}, bf16[16,2048]{1,0:T(8,128)(2,1)S(1)}, u32[]{:S(2)}, u32[]{:S(2)}) collective-permute-start(bf16[16,2048]{1,0:T(8,128)(2,1)S(1)} %get-tuple-element.72), channel_id=1, source_target_pairs={{0,1},{1,0},{2,3},{3,2},{4,5},{5,4},{6,7},{7,6},{8,9},{9,8},{10,11... | collective-permute-start | bytes 196616 | tf_op jit(solution)/shard_map/ppermute | solution.py:261
  152.5 2.2 %collective-permute-done.12 = bf16[16,2048]{1,0:T(8,128)(2,1)S(1)} collective-permute-done((bf16[16,2048]{1,0:T(8,128)(2,1)S(1)}, bf16[16,2048]{1,0:T(8,128)(2,1)S(1)}, u32[]{:S(2)}, u32[]{:S(2)}) %collective-permute-start.12) | collective-permute-done | bytes 65568 | tf_op jit(solution)/shard_map/ppermute | solution.py:261
  156.5 2.8 %all-to-all-done.5 = bf16[16,16,1280]{2,1,0:T(8,128)(2,1)S(1)} async-done(((bf16[16,16,1280]{2,1,0:T(8,128)(2,1)}), bf16[16,16,1280]{2,1,0:T(8,128)(2,1)S(1)}, u32[]{:S(2)}, u32[]{:S(2)}) %all-to-all-start.5) | async-done | bytes 655392 | tf_op jit(solution)/shard_map/all_to_all | solution.py:362
  159.5 2.5 %collective-permute-start.15 = (f32[16,1024]{1,0:T(8,128)S(1)}, f32[16,1024]{1,0:T(8,128)S(1)}, u32[]{:S(2)}, u32[]{:S(2)}) collective-permute-start(f32[16,1024]{1,0:T(8,128)S(1)} %slice.101), channel_id=1, source_target_pairs={{0,1},{1,0},{2,3},{3,2},{4,5},{5,4},{6,7},{7,6},{8,9},{9,8},{10,11... | collective-permute-start | bytes 196616 | tf_op jit(solution)/shard_map/ppermute | solution.py:261
  162.8 5.8 %all-to-all-start.6 = ((f32[64,5,2,128]{3,2,1,0:T(2,128)}), f32[64,5,2,128]{3,2,1,0:T(2,128)S(1)}, u32[]{:S(2)}, u32[]{:S(2)}) async-start(f32[64,5,2,128]{3,2,1,0:T(2,128)} %broadcast_in_dim.23), calls=%async_computation.6 | async-start | bytes 655360 | tf_op jit(solution)/shard_map/all_to_all | solution.py:377
  168.7 10.8 %all-to-all-done.6 = f32[64,5,2,128]{3,2,1,0:T(2,128)S(1)} async-done(((f32[64,5,2,128]{3,2,1,0:T(2,128)}), f32[64,5,2,128]{3,2,1,0:T(2,128)S(1)}, u32[]{:S(2)}, u32[]{:S(2)}) %all-to-all-start.6) | async-done | bytes 327712 | tf_op jit(solution)/shard_map/all_to_all | solution.py:377
  (99 shorter events, 34.4 us)
Async XLA Ops:
  2.7 10.7 %slice-start = ((bf16[1,128,1024]{2,1,0:T(8,128)(2,1)}), bf16[1,8,1024]{2,1,0:T(8,128)(2,1)S(1)}, s32[]{:S(2)}) async-start(bf16[1,128,1024]{2,1,0:T(8,128)(2,1)} %param.8), calls=%async_computation.7 | async-start | bytes 32768 | tf_op jit(solution)/shard_map/slice | solution.py:283
  2.7 10.7 %slice-start.1 = ((bf16[1,128,1024]{2,1,0:T(8,128)(2,1)}), bf16[1,8,1024]{2,1,0:T(8,128)(2,1)S(1)}, s32[]{:S(2)}) async-start(bf16[1,128,1024]{2,1,0:T(8,128)(2,1)} %param.9), calls=%async_computation.8 | async-start | bytes 32768 | tf_op jit(solution)/shard_map/slice | solution.py:283
  2.7 10.7 %slice-start.2 = ((bf16[1,128,1024]{2,1,0:T(8,128)(2,1)}), bf16[1,8,1024]{2,1,0:T(8,128)(2,1)S(1)}, s32[]{:S(2)}) async-start(bf16[1,128,1024]{2,1,0:T(8,128)(2,1)} %param.10), calls=%async_computation.9 | async-start | bytes 32768 | tf_op jit(solution)/shard_map/slice | solution.py:283
  2.7 14.7 %copy-start.8 = (f32[1024,16]{0,1:T(8,128)S(1)}, f32[1024,16]{0,1:T(8,128)}, u32[]{:S(2)}) copy-start(f32[1024,16]{0,1:T(8,128)} %param.15) | copy-start | bytes 196612
  2.7 14.7 %copy-start.9 = (f32[1024,16]{0,1:T(8,128)S(1)}, f32[1024,16]{0,1:T(8,128)}, u32[]{:S(2)}) copy-start(f32[1024,16]{0,1:T(8,128)} %param.14) | copy-start | bytes 196612
  2.7 14.8 %copy-start.7 = (f32[3,1024,7]{1,2,0:T(8,128)S(1)}, f32[3,1024,7]{1,2,0:T(8,128)}, u32[]{:S(2)}) copy-start(f32[3,1024,7]{1,2,0:T(8,128)} %param.13) | copy-start | bytes 258052
  2.8 29.8 %all-to-all-start.1 = ((bf16[16,16,2688]{2,1,0:T(8,128)(2,1)}), bf16[16,16,2688]{2,1,0:T(8,128)(2,1)}, u32[]{:S(2)}, u32[]{:S(2)}) async-start(bf16[16,16,2688]{2,1,0:T(8,128)(2,1)} %broadcast_in_dim.19), calls=%async_computation.1 | async-start | bytes 2752512 | tf_op jit(solution)/shard_map/all_to_all | solution.py:297
  10.9 6.7 %copy-start = (bf16[1,128,1024]{2,1,0:T(8,128)(2,1)S(1)}, bf16[1,128,1024]{2,1,0:T(8,128)(2,1)}, u32[]{:S(2)}) copy-start(bf16[1,128,1024]{2,1,0:T(8,128)(2,1)} %param.8) | copy-start | bytes 786436
  10.9 6.7 %copy-start.1 = (bf16[1,128,1024]{2,1,0:T(8,128)(2,1)S(1)}, bf16[1,128,1024]{2,1,0:T(8,128)(2,1)}, u32[]{:S(2)}) copy-start(bf16[1,128,1024]{2,1,0:T(8,128)(2,1)} %param.9) | copy-start | bytes 786436
  11.8 5.8 %collective-permute-start = (bf16[16,1408]{1,0:T(8,128)(2,1)S(1)}, bf16[16,1408]{1,0:T(8,128)(2,1)S(1)}, u32[]{:S(2)}, u32[]{:S(2)}) collective-permute-start(bf16[16,1408]{1,0:T(8,128)(2,1)S(1)} %get-tuple-element.74), channel_id=1, source_target_pairs={{0,64},{64,0},{1,65},{65,1},{2,66},{66,2},{3,67},{67,3},{4,68},{68... | collective-permute-start | bytes 135176 | tf_op jit(solution)/shard_map/ppermute | solution.py:261
  13.4 4.2 %collective-permute-start.1 = (bf16[3,8,1024]{2,1,0:T(8,128)(2,1)S(1)}, bf16[3,8,1024]{2,1,0:T(8,128)(2,1)S(1)}, u32[]{:S(2)}, u32[]{:S(2)}) collective-permute-start(bf16[3,8,1024]{2,1,0:T(8,128)(2,1)S(1)} %pad_maximum_fusion.5), channel_id=1, source_target_pairs={{0,2},{2,4},{4,6},{6,8},{8,10},{10,12},{12,14},{14,16},{16,18},{18... | collective-permute-start | bytes 147464 | tf_op jit(solution)/shard_map/ppermute | solution.py:257
  14.7 30.4 %collective-permute-start.2 = (bf16[128,4096]{1,0:T(8,128)(2,1)}, bf16[128,4096]{1,0:T(8,128)(2,1)}, u32[]{:S(2)}, u32[]{:S(2)}) collective-permute-start(bf16[128,4096]{1,0:T(8,128)(2,1)} %bitcast.11), channel_id=1, source_target_pairs={{0,2},{2,0},{1,3},{3,1},{4,6},{6,4},{5,7},{7,5},{8,10},{10,8},{9,1... | collective-permute-start | bytes 3145736 | tf_op jit(solution)/shard_map/ppermute | solution.py:261
  33.7 26.2 %all-to-all-start = ((bf16[16,2,16,1408]{3,2,1,0:T(8,128)(2,1)}), bf16[16,2,16,1408]{3,2,1,0:T(8,128)(2,1)}, u32[]{:S(2)}, u32[]{:S(2)}) async-start(bf16[16,2,16,1408]{3,2,1,0:T(8,128)(2,1)} %broadcast_in_dim.18), calls=%async_computation | async-start | bytes 2883584 | tf_op jit(solution)/shard_map/all_to_all | solution.py:302
  40.7 17.0 %collective-permute-start.3 = (bf16[8,16,2688]{2,1,0:T(8,128)(2,1)}, bf16[8,16,2688]{2,1,0:T(8,128)(2,1)}, u32[]{:S(2)}, u32[]{:S(2)}) collective-permute-start(bf16[8,16,2688]{2,1,0:T(8,128)(2,1)} %get-tuple-element.62), channel_id=1, source_target_pairs={{0,64},{64,1},{1,65},{65,0},{2,66},{66,3},{3,67},{67,2},{4,68},{68... | collective-permute-start | bytes 2064392 | tf_op jit(solution)/shard_map/ppermute | solution.py:269
  43.4 16.0 %collective-permute-start.4 = (bf16[8,16,2688]{2,1,0:T(8,128)(2,1)}, bf16[8,16,2688]{2,1,0:T(8,128)(2,1)S(1)}, u32[]{:S(2)}, u32[]{:S(2)}) collective-permute-start(bf16[8,16,2688]{2,1,0:T(8,128)(2,1)} %get-tuple-element.61), channel_id=1, source_target_pairs={{0,65},{64,0},{1,64},{65,1},{2,67},{66,2},{3,66},{67,3},{4,69},{68... | collective-permute-start | bytes 2064392 | tf_op jit(solution)/shard_map/ppermute | solution.py:269
  62.3 1.6 collective-permute-start.5
  66.0 18.8 %collective-permute-start.6 = (f32[256,128]{1,0:T(8,128)S(1)}, f32[256,128]{1,0:T(8,128)S(1)}, u32[]{:S(2)}, u32[]{:S(2)}) collective-permute-start(f32[256,128]{1,0:T(8,128)S(1)} %pad_maximum_fusion.3), channel_id=1, source_target_pairs={{2,0},{4,2},{6,4},{8,6},{10,8},{12,10},{14,12},{16,14},{18,16},{20... | collective-permute-start | bytes 393224 | tf_op jit(solution)/shard_map/ppermute | solution.py:257
  67.3 17.5 %all-to-all-start.2 = ((f32[64,4,128]{2,1,0:T(4,128)}), f32[64,4,128]{2,1,0:T(4,128)S(1)}, u32[]{:S(2)}, u32[]{:S(2)}) async-start(f32[64,4,128]{2,1,0:T(4,128)} %bitcast.18), calls=%async_computation.2 | async-start | bytes 262144 | tf_op jit(solution)/shard_map/all_to_all | solution.py:323
  85.6 13.1 %all-to-all-start.3 = ((f32[64,4,128]{2,1,0:T(4,128)}), f32[64,4,128]{2,1,0:T(4,128)S(1)}, u32[]{:S(2)}, u32[]{:S(2)}) async-start(f32[64,4,128]{2,1,0:T(4,128)} %bitcast.20), calls=%async_computation.3 | async-start | bytes 262144 | tf_op jit(solution)/shard_map/all_to_all | solution.py:326
  100.3 1.4 collective-permute-start.7
  105.6 35.1 %all-to-all-start.4 = ((bf16[16,2,16,2048]{3,2,1,0:T(8,128)(2,1)}), bf16[16,2,16,2048]{3,2,1,0:T(8,128)(2,1)}, u32[]{:S(2)}, u32[]{:S(2)}) async-start(bf16[16,2,16,2048]{3,2,1,0:T(8,128)(2,1)} %bitcast.74), calls=%async_computation.4 | async-start | bytes 4194304 | tf_op jit(solution)/shard_map/all_to_all | solution.py:348
  111.5 16.4 %collective-permute-start.8 = (bf16[256,1024]{1,0:T(8,128)(2,1)S(1)}, bf16[256,1024]{1,0:T(8,128)(2,1)S(1)}, u32[]{:S(2)}, u32[]{:S(2)}) collective-permute-start(bf16[256,1024]{1,0:T(8,128)(2,1)S(1)} %convolution_convert_fusion.3), channel_id=1, source_target_pairs={{0,1},{1,0},{64,65},{65,64},{2,3},{3,2},{66,67},{67,66},{4,5},{5,4... | collective-permute-start | bytes 1572872 | tf_op jit(solution)/shard_map/ppermute | solution.py:343
  115.3 22.2 %collective-permute-start.9 = (bf16[256,1024]{1,0:T(8,128)(2,1)S(1)}, bf16[256,1024]{1,0:T(8,128)(2,1)S(1)}, u32[]{:S(2)}, u32[]{:S(2)}) collective-permute-start(bf16[256,1024]{1,0:T(8,128)(2,1)S(1)} %convolution_convert_fusion.2), channel_id=1, source_target_pairs={{0,64},{64,0},{1,65},{65,1},{2,66},{66,2},{3,67},{67,3},{4,68},{68... | collective-permute-start | bytes 1572872 | tf_op jit(solution)/shard_map/ppermute | solution.py:344
  117.1 21.2 %collective-permute-start.10 = (bf16[256,1024]{1,0:T(8,128)(2,1)S(1)}, bf16[256,1024]{1,0:T(8,128)(2,1)S(1)}, u32[]{:S(2)}, u32[]{:S(2)}) collective-permute-start(bf16[256,1024]{1,0:T(8,128)(2,1)S(1)} %convolution_convert_fusion.1), channel_id=1, source_target_pairs={{0,65},{65,0},{1,64},{64,1},{2,67},{67,2},{3,66},{66,3},{4,69},{69... | collective-permute-start | bytes 1572872 | tf_op jit(solution)/shard_map/ppermute | solution.py:345
  123.7 1.4 collective-permute-start.11
  140.8 18.6 %all-to-all-start.5 = ((bf16[16,16,1280]{2,1,0:T(8,128)(2,1)}), bf16[16,16,1280]{2,1,0:T(8,128)(2,1)S(1)}, u32[]{:S(2)}, u32[]{:S(2)}) async-start(bf16[16,16,1280]{2,1,0:T(8,128)(2,1)} %bitcast.38), calls=%async_computation.5 | async-start | bytes 1310720 | tf_op jit(solution)/shard_map/all_to_all | solution.py:362
  148.3 6.4 %collective-permute-start.12 = (bf16[16,2048]{1,0:T(8,128)(2,1)S(1)}, bf16[16,2048]{1,0:T(8,128)(2,1)S(1)}, u32[]{:S(2)}, u32[]{:S(2)}) collective-permute-start(bf16[16,2048]{1,0:T(8,128)(2,1)S(1)} %get-tuple-element.72), channel_id=1, source_target_pairs={{0,1},{1,0},{2,3},{3,2},{4,5},{5,4},{6,7},{7,6},{8,9},{9,8},{10,11... | collective-permute-start | bytes 196616 | tf_op jit(solution)/shard_map/ppermute | solution.py:261
  150.7 4.3 %collective-permute-start.13 = (bf16[16,2048]{1,0:T(8,128)(2,1)S(1)}, bf16[16,2048]{1,0:T(8,128)(2,1)S(1)}, u32[]{:S(2)}, u32[]{:S(2)}) collective-permute-start(bf16[16,2048]{1,0:T(8,128)(2,1)S(1)} %get-tuple-element.71), channel_id=1, source_target_pairs={{0,64},{64,0},{1,65},{65,1},{2,66},{66,2},{3,67},{67,3},{4,68},{68... | collective-permute-start | bytes 196616 | tf_op jit(solution)/shard_map/ppermute | solution.py:368
  151.1 5.5 %collective-permute-start.14 = (bf16[16,2048]{1,0:T(8,128)(2,1)S(1)}, bf16[16,2048]{1,0:T(8,128)(2,1)S(1)}, u32[]{:S(2)}, u32[]{:S(2)}) collective-permute-start(bf16[16,2048]{1,0:T(8,128)(2,1)S(1)} %get-tuple-element.71), channel_id=1, source_target_pairs={{0,65},{65,0},{1,64},{64,1},{2,67},{67,2},{3,66},{66,3},{4,69},{69... | collective-permute-start | bytes 196616 | tf_op jit(solution)/shard_map/ppermute | solution.py:369
  159.5 9.2 %collective-permute-start.15 = (f32[16,1024]{1,0:T(8,128)S(1)}, f32[16,1024]{1,0:T(8,128)S(1)}, u32[]{:S(2)}, u32[]{:S(2)}) collective-permute-start(f32[16,1024]{1,0:T(8,128)S(1)} %slice.101), channel_id=1, source_target_pairs={{0,1},{1,0},{2,3},{3,2},{4,5},{5,4},{6,7},{7,6},{8,9},{9,8},{10,11... | collective-permute-start | bytes 196616 | tf_op jit(solution)/shard_map/ppermute | solution.py:261
  162.8 16.7 %all-to-all-start.6 = ((f32[64,5,2,128]{3,2,1,0:T(2,128)}), f32[64,5,2,128]{3,2,1,0:T(2,128)S(1)}, u32[]{:S(2)}, u32[]{:S(2)}) async-start(f32[64,5,2,128]{3,2,1,0:T(2,128)} %broadcast_in_dim.23), calls=%async_computation.6 | async-start | bytes 655360 | tf_op jit(solution)/shard_map/all_to_all | solution.py:377
  179.6 1.4 collective-permute-start.16
  (5 other events, 15.7 us)

commit v5 on v4

--- a/solution.py
+++ b/solution.py
@@ -321,9 +321,9 @@
     head = jnp.concatenate([up[:PAD], ys[:PAD], ys[ROWS : ROWS + PAD], ys[2 * ROWS : 2 * ROWS + PAD]], axis=0)
     ahead = shifted(head, -1)
     blocks = lax.all_to_all(packed.reshape(64, 4, 128), CTX, 0, 0).reshape(256, 128)
-    blocks, ahead = lax.optimization_barrier((blocks, ahead))
     (scanned,) = call(scan_kernel, [sds(256, 128)], (blocks, span))
     carries = lax.all_to_all(scanned.reshape(64, 4, 128), CTX, 0, 0).reshape(256, 128)
+    carries, ahead = lax.optimization_barrier((carries, ahead))
     filt, gated_t, final = call(
         fore_kernel,
         [sds(ROWS, 128), sds(2, 512, T, dtype=BF), sds(M * 8, 128)],

time: 184 us -> 182 us (0.989)
  transfers between devices with their start and end apart: 24 -> 24, of which waited for: 16 -> 16; matrix products, arithmetic and copies ran while one was open for 11% -> 11% of each run, Pallas kernels for 4% -> 5%
where the time goes in v5:
time: 182 us; the launch traced here: 180 us
  waiting for transfers between devices  71.9 us (40%)
  starting transfers between devices  63.5 us (35%)
  matrix products  15.1 us (8%)
  Pallas kernels  12.6 us (7%)
  local copies, waits for them, and re-layouts  10.9 us (6%)
  other arithmetic  4.57 us (3%)
    all_to_all x1, waiting for transfers between devices, shards(): lax.all_to_all(jnp.broadcast_to(out_weight[:, :WA], (16, 16, WA)), XZ, 0, 0)  11.8 us
    all_to_all x1, waiting for transfers between devices, shards(): lax.all_to_all(jnp.broadcast_to(part, (64, SHARE // 2, 2, 128)), ('yl', '...  10.8 us
    pallas_call x5, Pallas kernels, call(): pl.pallas_call(body, out_shape=outs, in_specs=[VMEM] * len(ins), out_spec...  10.5 us
    ppermute x8, starting transfers between devices, swapped(): return lax.ppermute(value, axis, [(0, 1), (1, 0)])  10.2 us
    ppermute x1, waiting for transfers between devices, shards(): lax.ppermute(parts[1], ('yl', 'yh'), [(0, 2), (2, 0), (1, 3), (3, 1)])  9.92 us
    ppermute x2, waiting for transfers between devices, along_y(): return lax.ppermute(value, ('yl', 'yh'), pairs)  9.23 us
    all_to_all x1, waiting for transfers between devices, shards(): lax.all_to_all(scanned.reshape(64, 4, 128), CTX, 0, 0).reshape(256, 128)  8.43 us
    all_to_all x1, starting transfers between devices, shards(): lax.all_to_all(jnp.broadcast_to(out_weight[:, :WA], (16, 16, WA)), XZ, 0, 0)  8.15 us
  transfers between devices with their start and end apart: 24, of which 16 were waited for; matrix products, arithmetic and copies ran while one was open for 11% of the time, Pallas kernels for 5%

profile of v5, /device:TPU:0, one launch (start us, length us, event | category | flops | bytes accessed | tf_op | source)
XLA Modules:
  0.0 179.7 jit_solution(17006339703524960530)
XLA Ops:
  2.8 8.1 %all-to-all-start.1 = ((bf16[16,16,2688]{2,1,0:T(8,128)(2,1)}), bf16[16,16,2688]{2,1,0:T(8,128)(2,1)}, u32[]{:S(2)}, u32[]{:S(2)}) async-start(bf16[16,16,2688]{2,1,0:T(8,128)(2,1)} %broadcast_in_dim.19), calls=%async_computation.1 | async-start | bytes 2752512 | tf_op jit(solution)/shard_map/all_to_all | solution.py:297
  14.7 2.7 %collective-permute-start.2 = (bf16[128,4096]{1,0:T(8,128)(2,1)}, bf16[128,4096]{1,0:T(8,128)(2,1)}, u32[]{:S(2)}, u32[]{:S(2)}) collective-permute-start(bf16[128,4096]{1,0:T(8,128)(2,1)} %bitcast.11), channel_id=1, source_target_pairs={{0,2},{2,0},{1,3},{3,1},{4,6},{6,4},{5,7},{7,5},{8,10},{10,8},{9,1... | collective-permute-start | bytes 3145736 | tf_op jit(solution)/shard_map/ppermute | solution.py:261
  17.7 1.8 %shard_map.127 = (f32[3264,128]{1,0:T(8,128)S(1)}, f32[3072,128]{1,0:T(8,128)S(1)}, f32[128,128]{1,0:T(8,128)S(1)}) custom-call(bf16[128,1024]{1,0:T(8,128)(2,1)S(1)} %bitcast.70, bf16[128,1024]{1,0:T(8,128)(2,1)S(1)} %bitcast.71, bf16[128,1024]{1,0:T(8,128)(2,1)S(1)} %bitcast.72, f32[192,128]{1,0:T(8,128)S(1)} %reshape.117.halo, ...), custom_call_target="tpu_custom_call" | custom-call | flops 10000000 | bytes 4000000 | tf_op jit(solution)/shard_map/pallas_call | solution.py:30
  20.7 11.8 %all-to-all-done.1 = bf16[16,16,2688]{2,1,0:T(8,128)(2,1)} async-done(((bf16[16,16,2688]{2,1,0:T(8,128)(2,1)}), bf16[16,16,2688]{2,1,0:T(8,128)(2,1)}, u32[]{:S(2)}, u32[]{:S(2)}) %all-to-all-start.1) | async-done | bytes 1376288 | tf_op jit(solution)/shard_map/all_to_all | solution.py:297
  33.7 4.4 %all-to-all-start = ((bf16[16,2,16,1408]{3,2,1,0:T(8,128)(2,1)}), bf16[16,2,16,1408]{3,2,1,0:T(8,128)(2,1)}, u32[]{:S(2)}, u32[]{:S(2)}) async-start(bf16[16,2,16,1408]{3,2,1,0:T(8,128)(2,1)} %broadcast_in_dim.18), calls=%async_computation | async-start | bytes 2883584 | tf_op jit(solution)/shard_map/all_to_all | solution.py:302
  38.1 2.3 %fusion.26 = (bf16[8,16,2688]{2,1,0:T(8,128)(2,1)S(1)}, bf16[8,16,2688]{2,1,0:T(8,128)(2,1)}) fusion(bf16[16,16,2688]{2,1,0:T(8,128)(2,1)} %all-to-all-done.1), kind=kLoop, calls=%fused_computation.58 | loop fusion | bytes 2752512 | tf_op jit(solution)/shard_map/slice | solution.py:301
  40.5 2.7 %collective-permute-start.3 = (bf16[8,16,2688]{2,1,0:T(8,128)(2,1)}, bf16[8,16,2688]{2,1,0:T(8,128)(2,1)}, u32[]{:S(2)}, u32[]{:S(2)}) collective-permute-start(bf16[8,16,2688]{2,1,0:T(8,128)(2,1)} %get-tuple-element.62), channel_id=1, source_target_pairs={{0,64},{64,1},{1,65},{65,0},{2,66},{66,3},{3,67},{67,2},{4,68},{68... | collective-permute-start | bytes 2064392 | tf_op jit(solution)/shard_map/ppermute | solution.py:269
  43.1 1.7 collective-permute-start.4
  46.3 1.9 %fusion.29 = f32[256,256]{1,0:T(8,128)S(1)} fusion(bf16[256,2688]{1,0:T(8,128)(2,1)} %bitcast.10, bf16[256,2688]{1,0:T(8,128)(2,1)S(1)} %fusion), kind=kOutput, calls=%fused_computation.61 | convolution fusion | flops 352321536 | bytes 3014656 | tf_op jit(solution)/shard_map/dot_general | solution.py:273
  48.2 9.2 %collective-permute-done.3 = bf16[8,16,2688]{2,1,0:T(8,128)(2,1)} collective-permute-done((bf16[8,16,2688]{2,1,0:T(8,128)(2,1)}, bf16[8,16,2688]{2,1,0:T(8,128)(2,1)}, u32[]{:S(2)}, u32[]{:S(2)}) %collective-permute-start.3) | collective-permute-done | bytes 688160 | tf_op jit(solution)/shard_map/ppermute | solution.py:269
  57.4 1.7 fusion.30
  59.7 2.1 %fusion.3 = f32[512,256]{1,0:T(8,128)S(1)} fusion(bf16[512,1408]{1,0:T(8,128)(2,1)} %bitcast.4, bf16[128,4096]{1,0:T(8,128)(2,1)} %bitcast.11, bf16[128,4096]{1,0:T(8,128)(2,1)} %collective-permute-done.2), kind=kOutput, calls=%fused_computation.17 | convolution fusion | flops 370540544 | bytes 4063232 | tf_op jit(solution)/shard_map/dot_general | solution.py:273
  63.6 2.1 %shard_map.128 = (f32[1024,128]{1,0:T(8,128)S(1)}, f32[256,128]{1,0:T(8,128)}) custom-call(s32[2]{0:T(128)S(1)} %pad_add_fusion.core, f32[512,128]{1,0:T(8,128)S(1)} %get-tuple-element.64.up_mine, f32[512,128]{1,0:T(8,128)S(1)} %collective-permute-done.5.up_theirs, f32[3072,128]{1,0:T(8,128)S(1)} %get-tuple-element.38.ys, ...), custom_call_target="tpu_custom_call" | custom-call | flops 10000000 | bytes 4000000 | tf_op jit(solution)/shard_map/pallas_call | solution.py:312
  65.7 7.8 %all-to-all-start.2 = ((f32[64,4,128]{2,1,0:T(4,128)}), f32[64,4,128]{2,1,0:T(4,128)S(1)}, u32[]{:S(2)}, u32[]{:S(2)}) async-start(f32[64,4,128]{2,1,0:T(4,128)} %bitcast.18), calls=%async_computation.2 | async-start | bytes 262144 | tf_op jit(solution)/shard_map/all_to_all | solution.py:323
  74.8 7.1 %all-to-all-done.2 = f32[64,4,128]{2,1,0:T(4,128)S(1)} async-done(((f32[64,4,128]{2,1,0:T(4,128)}), f32[64,4,128]{2,1,0:T(4,128)S(1)}, u32[]{:S(2)}, u32[]{:S(2)}) %all-to-all-start.2) | async-done | bytes 131104 | tf_op jit(solution)/shard_map/all_to_all | solution.py:323
  82.7 4.6 %all-to-all-start.3 = ((f32[64,4,128]{2,1,0:T(4,128)}), f32[64,4,128]{2,1,0:T(4,128)S(1)}, u32[]{:S(2)}, u32[]{:S(2)}) async-start(f32[64,4,128]{2,1,0:T(4,128)} %bitcast.20), calls=%async_computation.3 | async-start | bytes 262144 | tf_op jit(solution)/shard_map/all_to_all | solution.py:325
  87.3 8.4 %all-to-all-done.3 = f32[64,4,128]{2,1,0:T(4,128)S(1)} async-done(((f32[64,4,128]{2,1,0:T(4,128)}), f32[64,4,128]{2,1,0:T(4,128)S(1)}, u32[]{:S(2)}, u32[]{:S(2)}) %all-to-all-start.3) | async-done | bytes 131104 | tf_op jit(solution)/shard_map/all_to_all | solution.py:325
  95.8 1.6 shard_map.130
  99.6 3.2 %convolution_convert_fusion = bf16[512,2048]{1,0:T(8,128)(2,1)} fusion(bf16[512,256]{1,0:T(8,128)(2,1)S(1)} %bitcast.86, bf16[128,4096]{1,0:T(8,128)(2,1)} %collective-permute-done.2, bf16[128,4096]{1,0:T(8,128)(2,1)} %bitcast.11), kind=kOutput, calls=%fused_computation | convolution fusion | flops 540016640 | bytes 4456448 | tf_op jit(solution)/shard_map/dot_general | solution.py:277
  102.8 4.4 %all-to-all-start.4 = ((bf16[16,2,16,2048]{3,2,1,0:T(8,128)(2,1)}), bf16[16,2,16,2048]{3,2,1,0:T(8,128)(2,1)}, u32[]{:S(2)}, u32[]{:S(2)}) async-start(bf16[16,2,16,2048]{3,2,1,0:T(8,128)(2,1)} %bitcast.74), calls=%async_computation.4 | async-start | bytes 4194304 | tf_op jit(solution)/shard_map/all_to_all | solution.py:348
  108.6 2.7 %collective-permute-start.8 = (bf16[256,1024]{1,0:T(8,128)(2,1)S(1)}, bf16[256,1024]{1,0:T(8,128)(2,1)S(1)}, u32[]{:S(2)}, u32[]{:S(2)}) collective-permute-start(bf16[256,1024]{1,0:T(8,128)(2,1)S(1)} %convolution_convert_fusion.3), channel_id=1, source_target_pairs={{0,1},{1,0},{64,65},{65,64},{2,3},{3,2},{66,67},{67,66},{4,5},{5,4... | collective-permute-start | bytes 1572872 | tf_op jit(solution)/shard_map/ppermute | solution.py:343
  115.8 5.1 %shard_map.131 = (bf16[128,1024]{1,0:T(8,128)(2,1)}, bf16[128,1024]{1,0:T(8,128)(2,1)}, bf16[128,1024]{1,0:T(8,128)(2,1)}, f32[304,128]{1,0:T(8,128)S(1)}) custom-call(f32[1024,128]{1,0:T(8,128)S(1)} %get-tuple-element.40.up, f32[1024,128]{1,0:T(8,128)S(1)} %copy-done.6, f32[3072,128]{1,0:T(8,128)S(1)} %get-tuple-element.38.ys, f32[3264,128]{1,0:T(8,128)S(1)} %copy-done.4, ...), custom_call_target="tpu_custom_call" | custom-call | flops 7000000000 | bytes 4000000 | tf_op jit(solution)/shard_map/pallas_call | solution.py:30
  122.3 2.7 %collective-permute-done.8.one = bf16[256,1024]{1,0:T(8,128)(2,1)S(1)} collective-permute-done((bf16[256,1024]{1,0:T(8,128)(2,1)S(1)}, bf16[256,1024]{1,0:T(8,128)(2,1)S(1)}, u32[]{:S(2)}, u32[]{:S(2)}) %collective-permute-start.8) | collective-permute-done | bytes 524320 | tf_op jit(solution)/shard_map/ppermute | solution.py:343
  125.0 9.9 %collective-permute-done.9.two = bf16[256,1024]{1,0:T(8,128)(2,1)S(1)} collective-permute-done((bf16[256,1024]{1,0:T(8,128)(2,1)S(1)}, bf16[256,1024]{1,0:T(8,128)(2,1)S(1)}, u32[]{:S(2)}, u32[]{:S(2)}) %collective-permute-start.9) | collective-permute-done | bytes 524320 | tf_op jit(solution)/shard_map/ppermute | solution.py:344
  137.9 5.4 %all-to-all-start.5 = ((bf16[16,16,1280]{2,1,0:T(8,128)(2,1)}), bf16[16,16,1280]{2,1,0:T(8,128)(2,1)S(1)}, u32[]{:S(2)}, u32[]{:S(2)}) async-start(bf16[16,16,1280]{2,1,0:T(8,128)(2,1)} %bitcast.38), calls=%async_computation.5 | async-start | bytes 1310720 | tf_op jit(solution)/shard_map/all_to_all | solution.py:362
  143.4 2.0 %reduce_sum.30 = bf16[2,16,2048]{2,1,0:T(8,128)(2,1)S(1)} reduce(bf16[16,2,16,2048]{3,2,1,0:T(8,128)(2,1)} %all-to-all-done.4, bf16[]{:T(256)} %constant.68.clone.1), dimensions={0}, to_apply=%region_0.1 | reduce | flops 983040 | bytes 2228226 | tf_op jit(solution)/shard_map/reduce_sum | solution.py:363
  145.4 2.7 %collective-permute-start.12 = (bf16[16,2048]{1,0:T(8,128)(2,1)S(1)}, bf16[16,2048]{1,0:T(8,128)(2,1)S(1)}, u32[]{:S(2)}, u32[]{:S(2)}) collective-permute-start(bf16[16,2048]{1,0:T(8,128)(2,1)S(1)} %get-tuple-element.72), channel_id=1, source_target_pairs={{0,1},{1,0},{2,3},{3,2},{4,5},{5,4},{6,7},{7,6},{8,9},{9,8},{10,11... | collective-permute-start | bytes 196616 | tf_op jit(solution)/shard_map/ppermute | solution.py:261
  149.6 2.2 %collective-permute-done.12 = bf16[16,2048]{1,0:T(8,128)(2,1)S(1)} collective-permute-done((bf16[16,2048]{1,0:T(8,128)(2,1)S(1)}, bf16[16,2048]{1,0:T(8,128)(2,1)S(1)}, u32[]{:S(2)}, u32[]{:S(2)}) %collective-permute-start.12) | collective-permute-done | bytes 65568 | tf_op jit(solution)/shard_map/ppermute | solution.py:261
  154.0 2.5 %all-to-all-done.5 = bf16[16,16,1280]{2,1,0:T(8,128)(2,1)S(1)} async-done(((bf16[16,16,1280]{2,1,0:T(8,128)(2,1)}), bf16[16,16,1280]{2,1,0:T(8,128)(2,1)S(1)}, u32[]{:S(2)}, u32[]{:S(2)}) %all-to-all-start.5) | async-done | bytes 655392 | tf_op jit(solution)/shard_map/all_to_all | solution.py:362
  156.6 2.8 %collective-permute-start.15 = (f32[16,1024]{1,0:T(8,128)S(1)}, f32[16,1024]{1,0:T(8,128)S(1)}, u32[]{:S(2)}, u32[]{:S(2)}) collective-permute-start(f32[16,1024]{1,0:T(8,128)S(1)} %slice.101), channel_id=1, source_target_pairs={{0,1},{1,0},{2,3},{3,2},{4,5},{5,4},{6,7},{7,6},{8,9},{9,8},{10,11... | collective-permute-start | bytes 196616 | tf_op jit(solution)/shard_map/ppermute | solution.py:261
  160.3 5.8 %all-to-all-start.6 = ((f32[64,5,2,128]{3,2,1,0:T(2,128)}), f32[64,5,2,128]{3,2,1,0:T(2,128)S(1)}, u32[]{:S(2)}, u32[]{:S(2)}) async-start(f32[64,5,2,128]{3,2,1,0:T(2,128)} %broadcast_in_dim.23), calls=%async_computation.6 | async-start | bytes 655360 | tf_op jit(solution)/shard_map/all_to_all | solution.py:377
  166.2 10.8 %all-to-all-done.6 = f32[64,5,2,128]{3,2,1,0:T(2,128)S(1)} async-done(((f32[64,5,2,128]{3,2,1,0:T(2,128)}), f32[64,5,2,128]{3,2,1,0:T(2,128)S(1)}, u32[]{:S(2)}, u32[]{:S(2)}) %all-to-all-start.6) | async-done | bytes 327712 | tf_op jit(solution)/shard_map/all_to_all | solution.py:377
  (99 shorter events, 33.9 us)
Async XLA Ops:
  2.7 10.7 %slice-start = ((bf16[1,128,1024]{2,1,0:T(8,128)(2,1)}), bf16[1,8,1024]{2,1,0:T(8,128)(2,1)S(1)}, s32[]{:S(2)}) async-start(bf16[1,128,1024]{2,1,0:T(8,128)(2,1)} %param.8), calls=%async_computation.7 | async-start | bytes 32768 | tf_op jit(solution)/shard_map/slice | solution.py:283
  2.7 10.7 %slice-start.1 = ((bf16[1,128,1024]{2,1,0:T(8,128)(2,1)}), bf16[1,8,1024]{2,1,0:T(8,128)(2,1)S(1)}, s32[]{:S(2)}) async-start(bf16[1,128,1024]{2,1,0:T(8,128)(2,1)} %param.9), calls=%async_computation.8 | async-start | bytes 32768 | tf_op jit(solution)/shard_map/slice | solution.py:283
  2.7 10.7 %slice-start.2 = ((bf16[1,128,1024]{2,1,0:T(8,128)(2,1)}), bf16[1,8,1024]{2,1,0:T(8,128)(2,1)S(1)}, s32[]{:S(2)}) async-start(bf16[1,128,1024]{2,1,0:T(8,128)(2,1)} %param.10), calls=%async_computation.9 | async-start | bytes 32768 | tf_op jit(solution)/shard_map/slice | solution.py:283
  2.7 14.7 %copy-start.8 = (f32[1024,16]{0,1:T(8,128)S(1)}, f32[1024,16]{0,1:T(8,128)}, u32[]{:S(2)}) copy-start(f32[1024,16]{0,1:T(8,128)} %param.15) | copy-start | bytes 196612
  2.7 14.7 %copy-start.9 = (f32[1024,16]{0,1:T(8,128)S(1)}, f32[1024,16]{0,1:T(8,128)}, u32[]{:S(2)}) copy-start(f32[1024,16]{0,1:T(8,128)} %param.14) | copy-start | bytes 196612
  2.7 14.8 %copy-start.7 = (f32[3,1024,7]{1,2,0:T(8,128)S(1)}, f32[3,1024,7]{1,2,0:T(8,128)}, u32[]{:S(2)}) copy-start(f32[3,1024,7]{1,2,0:T(8,128)} %param.13) | copy-start | bytes 258052
  2.8 29.8 %all-to-all-start.1 = ((bf16[16,16,2688]{2,1,0:T(8,128)(2,1)}), bf16[16,16,2688]{2,1,0:T(8,128)(2,1)}, u32[]{:S(2)}, u32[]{:S(2)}) async-start(bf16[16,16,2688]{2,1,0:T(8,128)(2,1)} %broadcast_in_dim.19), calls=%async_computation.1 | async-start | bytes 2752512 | tf_op jit(solution)/shard_map/all_to_all | solution.py:297
  10.9 6.7 %copy-start = (bf16[1,128,1024]{2,1,0:T(8,128)(2,1)S(1)}, bf16[1,128,1024]{2,1,0:T(8,128)(2,1)}, u32[]{:S(2)}) copy-start(bf16[1,128,1024]{2,1,0:T(8,128)(2,1)} %param.8) | copy-start | bytes 786436
  10.9 6.7 %copy-start.1 = (bf16[1,128,1024]{2,1,0:T(8,128)(2,1)S(1)}, bf16[1,128,1024]{2,1,0:T(8,128)(2,1)}, u32[]{:S(2)}) copy-start(bf16[1,128,1024]{2,1,0:T(8,128)(2,1)} %param.9) | copy-start | bytes 786436
  11.8 5.8 %collective-permute-start = (bf16[16,1408]{1,0:T(8,128)(2,1)S(1)}, bf16[16,1408]{1,0:T(8,128)(2,1)S(1)}, u32[]{:S(2)}, u32[]{:S(2)}) collective-permute-start(bf16[16,1408]{1,0:T(8,128)(2,1)S(1)} %get-tuple-element.74), channel_id=1, source_target_pairs={{0,64},{64,0},{1,65},{65,1},{2,66},{66,2},{3,67},{67,3},{4,68},{68... | collective-permute-start | bytes 135176 | tf_op jit(solution)/shard_map/ppermute | solution.py:261
  13.4 4.2 %collective-permute-start.1 = (bf16[3,8,1024]{2,1,0:T(8,128)(2,1)S(1)}, bf16[3,8,1024]{2,1,0:T(8,128)(2,1)S(1)}, u32[]{:S(2)}, u32[]{:S(2)}) collective-permute-start(bf16[3,8,1024]{2,1,0:T(8,128)(2,1)S(1)} %pad_maximum_fusion.5), channel_id=1, source_target_pairs={{0,2},{2,4},{4,6},{6,8},{8,10},{10,12},{12,14},{14,16},{16,18},{18... | collective-permute-start | bytes 147464 | tf_op jit(solution)/shard_map/ppermute | solution.py:257
  14.7 30.2 %collective-permute-start.2 = (bf16[128,4096]{1,0:T(8,128)(2,1)}, bf16[128,4096]{1,0:T(8,128)(2,1)}, u32[]{:S(2)}, u32[]{:S(2)}) collective-permute-start(bf16[128,4096]{1,0:T(8,128)(2,1)} %bitcast.11), channel_id=1, source_target_pairs={{0,2},{2,0},{1,3},{3,1},{4,6},{6,4},{5,7},{7,5},{8,10},{10,8},{9,1... | collective-permute-start | bytes 3145736 | tf_op jit(solution)/shard_map/ppermute | solution.py:261
  33.7 26.0 %all-to-all-start = ((bf16[16,2,16,1408]{3,2,1,0:T(8,128)(2,1)}), bf16[16,2,16,1408]{3,2,1,0:T(8,128)(2,1)}, u32[]{:S(2)}, u32[]{:S(2)}) async-start(bf16[16,2,16,1408]{3,2,1,0:T(8,128)(2,1)} %broadcast_in_dim.18), calls=%async_computation | async-start | bytes 2883584 | tf_op jit(solution)/shard_map/all_to_all | solution.py:302
  40.5 17.0 %collective-permute-start.3 = (bf16[8,16,2688]{2,1,0:T(8,128)(2,1)}, bf16[8,16,2688]{2,1,0:T(8,128)(2,1)}, u32[]{:S(2)}, u32[]{:S(2)}) collective-permute-start(bf16[8,16,2688]{2,1,0:T(8,128)(2,1)} %get-tuple-element.62), channel_id=1, source_target_pairs={{0,64},{64,1},{1,65},{65,0},{2,66},{66,3},{3,67},{67,2},{4,68},{68... | collective-permute-start | bytes 2064392 | tf_op jit(solution)/shard_map/ppermute | solution.py:269
  43.1 16.0 %collective-permute-start.4 = (bf16[8,16,2688]{2,1,0:T(8,128)(2,1)S(1)}, bf16[8,16,2688]{2,1,0:T(8,128)(2,1)S(1)}, u32[]{:S(2)}, u32[]{:S(2)}) collective-permute-start(bf16[8,16,2688]{2,1,0:T(8,128)(2,1)S(1)} %get-tuple-element.61), channel_id=1, source_target_pairs={{0,65},{64,0},{1,64},{65,1},{2,67},{66,2},{3,66},{67,3},{4,69},{68... | collective-permute-start | bytes 2064392 | tf_op jit(solution)/shard_map/ppermute | solution.py:269
  62.0 1.6 collective-permute-start.5
  65.7 16.2 %all-to-all-start.2 = ((f32[64,4,128]{2,1,0:T(4,128)}), f32[64,4,128]{2,1,0:T(4,128)S(1)}, u32[]{:S(2)}, u32[]{:S(2)}) async-start(f32[64,4,128]{2,1,0:T(4,128)} %bitcast.18), calls=%async_computation.2 | async-start | bytes 262144 | tf_op jit(solution)/shard_map/all_to_all | solution.py:323
  73.5 13.8 %collective-permute-start.6 = (f32[256,128]{1,0:T(8,128)S(1)}, f32[256,128]{1,0:T(8,128)S(1)}, u32[]{:S(2)}, u32[]{:S(2)}) collective-permute-start(f32[256,128]{1,0:T(8,128)S(1)} %pad_maximum_fusion.3), channel_id=1, source_target_pairs={{2,0},{4,2},{6,4},{8,6},{10,8},{12,10},{14,12},{16,14},{18,16},{20... | collective-permute-start | bytes 393224 | tf_op jit(solution)/shard_map/ppermute | solution.py:257
  82.7 13.1 %all-to-all-start.3 = ((f32[64,4,128]{2,1,0:T(4,128)}), f32[64,4,128]{2,1,0:T(4,128)S(1)}, u32[]{:S(2)}, u32[]{:S(2)}) async-start(f32[64,4,128]{2,1,0:T(4,128)} %bitcast.20), calls=%async_computation.3 | async-start | bytes 262144 | tf_op jit(solution)/shard_map/all_to_all | solution.py:325
  98.2 1.3 collective-permute-start.7
  102.8 35.1 %all-to-all-start.4 = ((bf16[16,2,16,2048]{3,2,1,0:T(8,128)(2,1)}), bf16[16,2,16,2048]{3,2,1,0:T(8,128)(2,1)}, u32[]{:S(2)}, u32[]{:S(2)}) async-start(bf16[16,2,16,2048]{3,2,1,0:T(8,128)(2,1)} %bitcast.74), calls=%async_computation.4 | async-start | bytes 4194304 | tf_op jit(solution)/shard_map/all_to_all | solution.py:348
  108.6 16.4 %collective-permute-start.8 = (bf16[256,1024]{1,0:T(8,128)(2,1)S(1)}, bf16[256,1024]{1,0:T(8,128)(2,1)S(1)}, u32[]{:S(2)}, u32[]{:S(2)}) collective-permute-start(bf16[256,1024]{1,0:T(8,128)(2,1)S(1)} %convolution_convert_fusion.3), channel_id=1, source_target_pairs={{0,1},{1,0},{64,65},{65,64},{2,3},{3,2},{66,67},{67,66},{4,5},{5,4... | collective-permute-start | bytes 1572872 | tf_op jit(solution)/shard_map/ppermute | solution.py:343
  112.7 22.2 %collective-permute-start.9 = (bf16[256,1024]{1,0:T(8,128)(2,1)S(1)}, bf16[256,1024]{1,0:T(8,128)(2,1)S(1)}, u32[]{:S(2)}, u32[]{:S(2)}) collective-permute-start(bf16[256,1024]{1,0:T(8,128)(2,1)S(1)} %convolution_convert_fusion.2), channel_id=1, source_target_pairs={{0,64},{64,0},{1,65},{65,1},{2,66},{66,2},{3,67},{67,3},{4,68},{68... | collective-permute-start | bytes 1572872 | tf_op jit(solution)/shard_map/ppermute | solution.py:344
  114.7 20.7 %collective-permute-start.10 = (bf16[256,1024]{1,0:T(8,128)(2,1)S(1)}, bf16[256,1024]{1,0:T(8,128)(2,1)S(1)}, u32[]{:S(2)}, u32[]{:S(2)}) collective-permute-start(bf16[256,1024]{1,0:T(8,128)(2,1)S(1)} %convolution_convert_fusion.1), channel_id=1, source_target_pairs={{0,65},{65,0},{1,64},{64,1},{2,67},{67,2},{3,66},{66,3},{4,69},{69... | collective-permute-start | bytes 1572872 | tf_op jit(solution)/shard_map/ppermute | solution.py:345
  120.9 1.4 collective-permute-start.11
  137.9 18.5 %all-to-all-start.5 = ((bf16[16,16,1280]{2,1,0:T(8,128)(2,1)}), bf16[16,16,1280]{2,1,0:T(8,128)(2,1)S(1)}, u32[]{:S(2)}, u32[]{:S(2)}) async-start(bf16[16,16,1280]{2,1,0:T(8,128)(2,1)} %bitcast.38), calls=%async_computation.5 | async-start | bytes 1310720 | tf_op jit(solution)/shard_map/all_to_all | solution.py:362
  145.4 6.4 %collective-permute-start.12 = (bf16[16,2048]{1,0:T(8,128)(2,1)S(1)}, bf16[16,2048]{1,0:T(8,128)(2,1)S(1)}, u32[]{:S(2)}, u32[]{:S(2)}) collective-permute-start(bf16[16,2048]{1,0:T(8,128)(2,1)S(1)} %get-tuple-element.72), channel_id=1, source_target_pairs={{0,1},{1,0},{2,3},{3,2},{4,5},{5,4},{6,7},{7,6},{8,9},{9,8},{10,11... | collective-permute-start | bytes 196616 | tf_op jit(solution)/shard_map/ppermute | solution.py:261
  148.1 4.3 %collective-permute-start.13 = (bf16[16,2048]{1,0:T(8,128)(2,1)S(1)}, bf16[16,2048]{1,0:T(8,128)(2,1)S(1)}, u32[]{:S(2)}, u32[]{:S(2)}) collective-permute-start(bf16[16,2048]{1,0:T(8,128)(2,1)S(1)} %get-tuple-element.71), channel_id=1, source_target_pairs={{0,64},{64,0},{1,65},{65,1},{2,66},{66,2},{3,67},{67,3},{4,68},{68... | collective-permute-start | bytes 196616 | tf_op jit(solution)/shard_map/ppermute | solution.py:368
  148.5 5.5 %collective-permute-start.14 = (bf16[16,2048]{1,0:T(8,128)(2,1)S(1)}, bf16[16,2048]{1,0:T(8,128)(2,1)S(1)}, u32[]{:S(2)}, u32[]{:S(2)}) collective-permute-start(bf16[16,2048]{1,0:T(8,128)(2,1)S(1)} %get-tuple-element.71), channel_id=1, source_target_pairs={{0,65},{65,0},{1,64},{64,1},{2,67},{67,2},{3,66},{66,3},{4,69},{69... | collective-permute-start | bytes 196616 | tf_op jit(solution)/shard_map/ppermute | solution.py:369
  156.6 9.5 %collective-permute-start.15 = (f32[16,1024]{1,0:T(8,128)S(1)}, f32[16,1024]{1,0:T(8,128)S(1)}, u32[]{:S(2)}, u32[]{:S(2)}) collective-permute-start(f32[16,1024]{1,0:T(8,128)S(1)} %slice.101), channel_id=1, source_target_pairs={{0,1},{1,0},{2,3},{3,2},{4,5},{5,4},{6,7},{7,6},{8,9},{9,8},{10,11... | collective-permute-start | bytes 196616 | tf_op jit(solution)/shard_map/ppermute | solution.py:261
  160.3 16.7 %all-to-all-start.6 = ((f32[64,5,2,128]{3,2,1,0:T(2,128)}), f32[64,5,2,128]{3,2,1,0:T(2,128)S(1)}, u32[]{:S(2)}, u32[]{:S(2)}) async-start(f32[64,5,2,128]{3,2,1,0:T(2,128)} %broadcast_in_dim.23), calls=%async_computation.6 | async-start | bytes 655360 | tf_op jit(solution)/shard_map/all_to_all | solution.py:377
  177.0 1.4 collective-permute-start.16
  (5 other events, 14.8 us)
